TPU v7x, 256 devices: a whole 4x4x8 slice. The times are simulated.
256 devices in a mesh: pts: 128 (over x, y, z), ch: 2 (over core).
Axes of the slice: x: 4, y: 4, z: 8, core: 2. Of those that a mesh axis runs over, the one named last changes fastest.
Arguments:
- stream: bfloat16 [262144, 256], P('pts', 'ch'), may hold values from -6 to 6
- send_rows: int32 [2, 16384, 32], P(None, 'pts'), may hold values from -1 to 2047, as said below
- recv_slots: int32 [2, 262144], P(None, 'pts'), may hold values from 0 to 4095, as said below
- qkv_weight: bfloat16 [2, 256, 3, 256], P(None, None, None, 'ch'), as said below
- out_weight: bfloat16 [2, 256, 256], P(None, 'ch'), may hold values from -0.375 to 0.375
- up_weight: bfloat16 [2, 256, 1024], P(None, None, 'ch'), may hold values from -0.375 to 0.375
- down_weight: bfloat16 [2, 1024, 256], P(None, 'ch'), may hold values from -0.1875 to 0.1875
- gain_attn: float32 [2, 256], replicated, may hold values from 0.1 to 1.9
- gain_mlp: float32 [2, 256], replicated, may hold values from 0.1 to 1.9
Outputs:
- refined: bfloat16 [262144, 256], P('pts', 'ch')
Inputs may be any that keep to these rules, and one draw needn't show every extreme that they name: For block b and devices s, d of pts, row s * N + d of send_rows lists the local rows of s that go to d, -1 marking an empty slot; at most 32 rows go from one device to one device, and some pair has exactly 32. The number of rows from s to s + o (cyclically) depends only on b and o. Each local row is sent once. recv_slots[b, d * 2048 + r] = s * 32 + j names a filled slot j of the rows that device d receives from device s; each filled slot is named once, so that the two tables make a permutation of all points. `qkv_weight`: projection weights, between -1.2 and 1.2; the query and key parts may be scaled so that scores reach a few hundred.
All inputs are finite; a program needn't handle non-finite values.
Results may differ from a plain program's by a relative error of at most 0.015.
Values may be sent and summed in bfloat16 or wider, within the bound.
No kernel may reach another device: no remote copies, remote signals or barrier semaphores. Data moves between devices by JAX's collectives and lax.ppermute only.
A program may use at most 64 MiB of HBM per device.

v0:
```python
import math

import jax
import jax.numpy as jnp
from jax import lax
from jax.sharding import PartitionSpec as P

D = 256
HEAD = 64
WIN = 1024
BLOCKS = 2


def layer_norm(values, gain):
    average = jnp.mean(values, axis=-1, keepdims=True)
    centred = values - average
    spread = jnp.mean(centred * centred, axis=-1, keepdims=True)
    return centred * lax.rsqrt(spread + 1e-05) * gain


def regroup(stream, send_table, recv_table):
    picked = jnp.take(stream, jnp.maximum(send_table, 0), axis=0)
    moved_rows = lax.all_to_all(picked, "pts", split_axis=0, concat_axis=0, tiled=True)
    return jnp.take(moved_rows.reshape(-1, stream.shape[1]), recv_table, axis=0)


def attend(projected, local_width):
    points = projected.shape[0]
    head_count = local_width // HEAD
    windows = projected.reshape(points // WIN, WIN, 3, head_count, HEAD)

    def one_window(window_rows):
        scores = jnp.einsum(
            "qhd,khd->hqk", window_rows[:, 0], window_rows[:, 1], preferred_element_type=jnp.float32
        ) / math.sqrt(HEAD)
        weights = jax.nn.softmax(scores, axis=-1).astype(jnp.bfloat16)
        attended = jnp.einsum(
            "hqk,khd->qhd", weights, window_rows[:, 2], preferred_element_type=jnp.float32
        )
        return attended.astype(jnp.bfloat16).reshape(WIN, local_width)

    return lax.map(one_window, windows).reshape(points, local_width)


def shards(
    stream,
    send_rows,
    recv_slots,
    qkv_weight,
    out_weight,
    up_weight,
    down_weight,
    gain_attn,
    gain_mlp,
):
    local_width = stream.shape[1]
    mlp_update = None
    for layer_index in range(BLOCKS):
        stream = regroup(stream, send_rows[layer_index], recv_slots[layer_index])
        whole_rows = lax.all_gather(stream, "ch", axis=1, tiled=True)
        normed = layer_norm(whole_rows.astype(jnp.float32), gain_attn[layer_index]).astype(
            jnp.bfloat16
        )
        projected = jnp.dot(
            normed,
            qkv_weight[layer_index].reshape(D, 3 * local_width),
            preferred_element_type=jnp.float32,
        ).astype(jnp.bfloat16)
        attended = attend(projected, local_width)
        partial_value = jnp.dot(
            attended, out_weight[layer_index], preferred_element_type=jnp.float32
        )
        own_part = lax.psum_scatter(partial_value, "ch", scatter_dimension=1, tiled=True)
        hstream = (stream.astype(jnp.float32) + own_part).astype(jnp.bfloat16)
        full_h = lax.all_gather(hstream, "ch", axis=1, tiled=True)
        normed_two = layer_norm(full_h.astype(jnp.float32), gain_mlp[layer_index]).astype(
            jnp.bfloat16
        )
        hidden_act = jax.nn.gelu(
            jnp.dot(normed_two, up_weight[layer_index], preferred_element_type=jnp.float32)
        ).astype(jnp.bfloat16)
        mlp_update = lax.psum_scatter(
            jnp.dot(hidden_act, down_weight[layer_index], preferred_element_type=jnp.float32),
            "ch",
            scatter_dimension=1,
            tiled=True,
        )
        stream = (hstream.astype(jnp.float32) + mlp_update).astype(jnp.bfloat16)
    return stream


def solution(mesh):
    in_specs = (
        P("pts", "ch"),
        P(None, "pts", None),
        P(None, "pts"),
        P(None, None, None, "ch"),
        P(None, "ch", None),
        P(None, None, "ch"),
        P(None, "ch", None),
        P(),
        P(),
    )
    out_specs = P("pts", "ch")
    return jax.shard_map(shards, mesh=mesh, in_specs=in_specs, out_specs=out_specs, check_vma=False)
```

profile of v0, /device:TPU:1, one launch (start us, length us, event | category | flops | bytes accessed | tf_op | source)
XLA Modules:
  0.0 364.2 jit_solution(3428423957356002292)
XLA Ops:
  6.5 0.8 compare_select_fusion
  7.3 0.8 compare_and_fusion
  8.4 12.1 %gather_fusion = bf16[4096,128]{1,0:T(8,128)(2,1)S(1)} fusion(bf16[2048,128]{1,0:T(8,128)(2,1)S(1)} %copy-done, s32[4096]{0:T(1024)S(1)} %broadcast_clamp_fusion.1), kind=kCustom, calls=%fused_computation.clone | custom fusion | bytes 2113536 | tf_op jit(solution)/shard_map/jit(_take)/gather | solution.py:22
  20.6 2.0 broadcast_select_fusion.1
  22.6 16.3 %all-to-all-start = ((bf16[128,32,128]{2,1,0:T(8,128)(2,1)}), bf16[128,32,128]{2,1,0:T(8,128)(2,1)S(1)}, u32[]{:S(2)}, u32[]{:S(2)}) async-start(bf16[128,32,128]{2,1,0:T(8,128)(2,1)} %broadcast_select_fusion.1), calls=%async_computation | async-start | bytes 2097152 | tf_op jit(solution)/shard_map/all_to_all | solution.py:23
  39.0 30.1 %all-to-all-done = bf16[128,32,128]{2,1,0:T(8,128)(2,1)S(1)} async-done(((bf16[128,32,128]{2,1,0:T(8,128)(2,1)}), bf16[128,32,128]{2,1,0:T(8,128)(2,1)S(1)}, u32[]{:S(2)}, u32[]{:S(2)}) %all-to-all-start) | async-done | bytes 1048608 | tf_op jit(solution)/shard_map/all_to_all | solution.py:23
  69.1 6.2 %gather_fusion.1 = bf16[2048,128]{1,0:T(8,128)(2,1)S(1)} fusion(bf16[4096,128]{1,0:T(8,128)(2,1)S(1)} %bitcast.126, s32[2048]{0:T(1024)S(1)} %fusion.102), kind=kCustom, calls=%fused_computation.1.clone | custom fusion | bytes 1056768 | tf_op jit(solution)/shard_map/jit(_take)/gather | solution.py:24
  75.4 1.1 broadcast_select_fusion.3
  76.8 9.6 %all-gather.5.cloned.1.call-done = bf16[2048,256]{1,0:T(8,128)(2,1)} async-done(((bf16[2048,128]{1,0:T(8,128)(2,1)}), bf16[2048,256]{1,0:T(8,128)(2,1)}) %all-gather.5.cloned.1.call-update) | async-done | bytes 1048592 | tf_op jit(solution)/shard_map/all_gather | solution.py:60
  86.4 1.7 convert_reduce_fusion.3
  88.1 1.9 fusion.55
  90.0 1.0 convolution_convert_fusion.1
  91.0 3.0 reshape.144
  94.0 6.9 %copy.23 = bf16[2,1024,3,2,64]{1,4,3,2,0:T(8,128)(2,1)S(1)} copy(bf16[2,1024,3,2,64]{4,3,2,1,0:T(2,128)(2,1)} %reshape.144) | data formatting | bytes 3145728 | tf_op jit(solution)/shard_map/while | solution.py:42
  100.9 0.9 broadcast.116.clone2
  101.7 20.2 %while.20 = (s32[]{:T(128)}, bf16[2,1024,128]{2,1,0:T(8,128)(2,1)}, bf16[2,1024,3,2,64]{1,4,3,2,0:T(8,128)(2,1)S(1)}, s32[]{:T(128)}) while((s32[]{:T(128)}, bf16[2,1024,128]{2,1,0:T(8,128)(2,1)}, bf16[2,1024,3,2,64]{1,4,3,2,0:T(8,128)(2,1)S(1)}, s32[]{:T(128)}) %tuple.49), condition=%wide.region_5.8_spmd, body=%wide.region_2.0_spmd.sunk | while | flops 547488768 | bytes 20464184 | solution.py:42
  101.8 4.9 %fusion.126 = (f32[2,1024]{1,0:T(2,128)S(1)}, f32[2,1024,1024]{1,2,0:T(8,128)}) fusion(bf16[1024,3,2,64]{0,3,2,1:T(8,128)(2,1)S(1)} %dynamic-slice_bitcast_fusion.4), kind=kOutput, calls=%fused_computation.148.clone.1 | convolution fusion | flops 274727936 | bytes 8921088 | tf_op jit(solution)/shard_map/while/body/eval_jaxpr/sub | solution.py:36
  106.7 4.2 %fusion.127 = bf16[2,64,1024]{2,1,0:T(8,128)(2,1)S(1)} fusion(f32[2,1024,1024]{1,2,0:T(8,128)} %get-tuple-element.122, f32[2,1024]{1,0:T(2,128)S(1)} %get-tuple-element.123, bf16[1024,3,2,64]{0,3,2,1:T(8,128)(2,1)S(1)} %dynamic-slice_bitcast_fusion.4), kind=kOutput, calls=%fused_computation.11.clone.1 | convolution fusion | flops 272760832 | bytes 8921088 | tf_op jit(solution)/shard_map/while/body/eval_jaxpr/hqk,khd->qhd/dot_general | solution.py:37
  110.9 0.2 copy.44
  111.1 0.7 constant_dynamic-update-slice_fusion.4
  111.9 4.9 %fusion.126 = (f32[2,1024]{1,0:T(2,128)S(1)}, f32[2,1024,1024]{1,2,0:T(8,128)}) fusion(bf16[1024,3,2,64]{0,3,2,1:T(8,128)(2,1)S(1)} %dynamic-slice_bitcast_fusion.4), kind=kOutput, calls=%fused_computation.148.clone.1 | convolution fusion | flops 274727936 | bytes 8921088 | tf_op jit(solution)/shard_map/while/body/eval_jaxpr/sub | solution.py:36
  116.8 4.2 %fusion.127 = bf16[2,64,1024]{2,1,0:T(8,128)(2,1)S(1)} fusion(f32[2,1024,1024]{1,2,0:T(8,128)} %get-tuple-element.122, f32[2,1024]{1,0:T(2,128)S(1)} %get-tuple-element.123, bf16[1024,3,2,64]{0,3,2,1:T(8,128)(2,1)S(1)} %dynamic-slice_bitcast_fusion.4), kind=kOutput, calls=%fused_computation.11.clone.1 | convolution fusion | flops 272760832 | bytes 8921088 | tf_op jit(solution)/shard_map/while/body/eval_jaxpr/hqk,khd->qhd/dot_general | solution.py:37
  121.0 0.2 copy.44
  121.2 0.7 constant_dynamic-update-slice_fusion.4
  121.9 2.9 fusion.98
  124.9 16.2 %reduce-scatter.5.cloned.1.call-done = f32[2048,128]{1,0:T(8,128)} async-done(((f32[2048,256]{1,0:T(8,128)}), f32[2048,128]{1,0:T(8,128)}) %reduce-scatter.5.cloned.1.call-update) | async-done | bytes 1048592 | tf_op jit(solution)/shard_map/reduce_scatter | solution.py:73
  141.1 2.4 add_convert_fusion.3
  143.5 0.2 reduce-scatter.7.cloned.1.call-start
  143.7 15.7 %all-gather.7.cloned.1.call-done = bf16[2048,256]{1,0:T(8,128)(2,1)} async-done(((bf16[2048,128]{1,0:T(8,128)(2,1)}), bf16[2048,256]{1,0:T(8,128)(2,1)}) %all-gather.7.cloned.1.call-update) | async-done | bytes 1048592 | tf_op jit(solution)/shard_map/all_gather | solution.py:75
  159.4 1.7 convert_reduce_fusion.2
  161.1 1.9 fusion.52
  163.0 3.2 fusion.59
  166.6 15.9 %reduce-scatter.7.cloned.1.call-done = f32[2048,128]{1,0:T(8,128)} async-done(((f32[2048,256]{1,0:T(8,128)}), f32[2048,128]{1,0:T(8,128)}) %reduce-scatter.7.cloned.1.call-update) | async-done | bytes 1048592 | tf_op jit(solution)/shard_map/reduce_scatter | solution.py:82
  182.5 1.3 add_convert_fusion.2
  183.8 12.1 %gather_fusion.2 = bf16[4096,128]{1,0:T(8,128)(2,1)S(1)} fusion(bf16[2048,128]{1,0:T(8,128)(2,1)S(1)} %add_convert_fusion.2, s32[4096]{0:T(1024)S(1)} %broadcast_clamp_fusion), kind=kCustom, calls=%fused_computation.2.clone | custom fusion | bytes 2113536 | tf_op jit(solution)/shard_map/jit(_take)/gather | solution.py:22
  196.0 2.0 broadcast_select_fusion
  198.0 13.7 %all-to-all-start.1 = ((bf16[128,32,128]{2,1,0:T(8,128)(2,1)}), bf16[128,32,128]{2,1,0:T(8,128)(2,1)S(1)}, u32[]{:S(2)}, u32[]{:S(2)}) async-start(bf16[128,32,128]{2,1,0:T(8,128)(2,1)} %broadcast_select_fusion), calls=%async_computation.3 | async-start | bytes 2097152 | tf_op jit(solution)/shard_map/all_to_all | solution.py:23
  211.8 30.8 %all-to-all-done.1 = bf16[128,32,128]{2,1,0:T(8,128)(2,1)S(1)} async-done(((bf16[128,32,128]{2,1,0:T(8,128)(2,1)}), bf16[128,32,128]{2,1,0:T(8,128)(2,1)S(1)}, u32[]{:S(2)}, u32[]{:S(2)}) %all-to-all-start.1) | async-done | bytes 1048608 | tf_op jit(solution)/shard_map/all_to_all | solution.py:23
  242.6 6.2 %gather_fusion.3 = bf16[2048,128]{1,0:T(8,128)(2,1)S(1)} fusion(bf16[4096,128]{1,0:T(8,128)(2,1)S(1)} %bitcast.127, s32[2048]{0:T(1024)S(1)} %fusion.103), kind=kCustom, calls=%fused_computation.3.clone | custom fusion | bytes 1056768 | tf_op jit(solution)/shard_map/jit(_take)/gather | solution.py:24
  248.8 1.1 broadcast_select_fusion.2
  250.1 9.0 %all-gather.9.cloned.1.call-done = bf16[2048,256]{1,0:T(8,128)(2,1)} async-done(((bf16[2048,128]{1,0:T(8,128)(2,1)}), bf16[2048,256]{1,0:T(8,128)(2,1)}) %all-gather.9.cloned.1.call-update) | async-done | bytes 1048592 | tf_op jit(solution)/shard_map/all_gather | solution.py:60
  259.2 1.7 convert_reduce_fusion.1
  260.8 1.9 fusion.49
  262.7 1.0 convolution_convert_fusion
  263.7 3.0 reshape.145
  266.8 6.9 %copy.28 = bf16[2,1024,3,2,64]{1,4,3,2,0:T(8,128)(2,1)S(1)} copy(bf16[2,1024,3,2,64]{4,3,2,1,0:T(2,128)(2,1)} %reshape.145) | data formatting | bytes 3145728 | tf_op jit(solution)/shard_map/while | solution.py:42
  273.6 0.9 broadcast.116.clone
  274.5 20.2 %while.21 = (s32[]{:T(128)}, bf16[2,1024,128]{2,1,0:T(8,128)(2,1)}, bf16[2,1024,3,2,64]{1,4,3,2,0:T(8,128)(2,1)S(1)}, s32[]{:T(128)}) while((s32[]{:T(128)}, bf16[2,1024,128]{2,1,0:T(8,128)(2,1)}, bf16[2,1024,3,2,64]{1,4,3,2,0:T(8,128)(2,1)S(1)}, s32[]{:T(128)}) %tuple.52), condition=%wide.region_15.18_spmd, body=%wide.region_12.17_spmd.sunk | while | flops 547488768 | bytes 20464184 | solution.py:42
  274.6 4.9 %fusion.128 = (f32[2,1024]{1,0:T(2,128)S(1)}, f32[2,1024,1024]{1,2,0:T(8,128)}) fusion(bf16[1024,3,2,64]{0,3,2,1:T(8,128)(2,1)S(1)} %dynamic-slice_bitcast_fusion.5), kind=kOutput, calls=%fused_computation.149.clone.1 | convolution fusion | flops 274727936 | bytes 8921088 | tf_op jit(solution)/shard_map/while/body/eval_jaxpr/sub | solution.py:36
  279.5 4.2 %fusion.129 = bf16[2,64,1024]{2,1,0:T(8,128)(2,1)S(1)} fusion(f32[2,1024,1024]{1,2,0:T(8,128)} %get-tuple-element.127, f32[2,1024]{1,0:T(2,128)S(1)} %get-tuple-element.128, bf16[1024,3,2,64]{0,3,2,1:T(8,128)(2,1)S(1)} %dynamic-slice_bitcast_fusion.5), kind=kOutput, calls=%fused_computation.27.clone.1 | convolution fusion | flops 272760832 | bytes 8921088 | tf_op jit(solution)/shard_map/while/body/eval_jaxpr/hqk,khd->qhd/dot_general | solution.py:37
  283.9 0.7 constant_dynamic-update-slice_fusion.5
  284.7 4.9 %fusion.128 = (f32[2,1024]{1,0:T(2,128)S(1)}, f32[2,1024,1024]{1,2,0:T(8,128)}) fusion(bf16[1024,3,2,64]{0,3,2,1:T(8,128)(2,1)S(1)} %dynamic-slice_bitcast_fusion.5), kind=kOutput, calls=%fused_computation.149.clone.1 | convolution fusion | flops 274727936 | bytes 8921088 | tf_op jit(solution)/shard_map/while/body/eval_jaxpr/sub | solution.py:36
  289.6 4.2 %fusion.129 = bf16[2,64,1024]{2,1,0:T(8,128)(2,1)S(1)} fusion(f32[2,1024,1024]{1,2,0:T(8,128)} %get-tuple-element.127, f32[2,1024]{1,0:T(2,128)S(1)} %get-tuple-element.128, bf16[1024,3,2,64]{0,3,2,1:T(8,128)(2,1)S(1)} %dynamic-slice_bitcast_fusion.5), kind=kOutput, calls=%fused_computation.27.clone.1 | convolution fusion | flops 272760832 | bytes 8921088 | tf_op jit(solution)/shard_map/while/body/eval_jaxpr/hqk,khd->qhd/dot_general | solution.py:37
  294.0 0.7 constant_dynamic-update-slice_fusion.5
  294.7 2.9 fusion.96
  297.7 16.2 %reduce-scatter.9.cloned.1.call-done = f32[2048,128]{1,0:T(8,128)} async-done(((f32[2048,256]{1,0:T(8,128)}), f32[2048,128]{1,0:T(8,128)}) %reduce-scatter.9.cloned.1.call-update) | async-done | bytes 1048592 | tf_op jit(solution)/shard_map/reduce_scatter | solution.py:73
  313.9 2.4 add_convert_fusion.1
  316.2 0.3 reduce-scatter.11.cloned.1.call-start
  316.5 15.6 %all-gather.11.cloned.1.call-done = bf16[2048,256]{1,0:T(8,128)(2,1)} async-done(((bf16[2048,128]{1,0:T(8,128)(2,1)}), bf16[2048,256]{1,0:T(8,128)(2,1)}) %all-gather.11.cloned.1.call-update) | async-done | bytes 1048592 | tf_op jit(solution)/shard_map/all_gather | solution.py:75
  332.2 1.7 convert_reduce_fusion
  333.8 1.9 fusion.46
  335.7 3.2 fusion.58
  339.0 16.3 %reduce-scatter.11.cloned.1.call-done = f32[2048,128]{1,0:T(8,128)} async-done(((f32[2048,256]{1,0:T(8,128)}), f32[2048,128]{1,0:T(8,128)}) %reduce-scatter.11.cloned.1.call-update) | async-done | bytes 1048592 | tf_op jit(solution)/shard_map/reduce_scatter | solution.py:82
  355.3 2.1 add_convert_fusion
  (86 shorter events, 2.1 us)
Async XLA Ops:
  6.5 1.9 copy-start
  20.6 18.4 %copy-start.13 = (s32[2,2048]{1,0:T(2,128)S(1)}, s32[2,2048]{1,0:T(2,128)}, u32[]{:S(2)}) copy-start(s32[2,2048]{1,0:T(2,128)} %param.19) | copy-start | bytes 49156
  22.6 46.6 %all-to-all-start = ((bf16[128,32,128]{2,1,0:T(8,128)(2,1)}), bf16[128,32,128]{2,1,0:T(8,128)(2,1)S(1)}, u32[]{:S(2)}, u32[]{:S(2)}) async-start(bf16[128,32,128]{2,1,0:T(8,128)(2,1)} %broadcast_select_fusion.1), calls=%async_computation | async-start | bytes 2097152 | tf_op jit(solution)/shard_map/all_to_all | solution.py:23
  38.9 47.5 %all-gather.5.cloned.1.call-start = ((), (), s32[]{:S(2)}) async-start(), calls=%async_computation.6 | async-start | bytes 1572864 | tf_op jit(solution)/shard_map/all_gather | solution.py:60
  69.1 7.4 %copy-start.11 = (bf16[2,256,3,128]{3,1,2,0:T(8,128)(2,1)S(1)}, bf16[2,256,3,128]{3,1,2,0:T(8,128)(2,1)}, u32[]{:S(2)}) copy-start(bf16[2,256,3,128]{3,1,2,0:T(8,128)(2,1)} %param.20) | copy-start | bytes 1179652
  75.3 14.6 %copy-start.1 = (bf16[2048,128]{1,0:T(8,128)(2,1)}, bf16[2048,128]{1,0:T(8,128)(2,1)S(1)}, u32[]{:S(2)}) copy-start(bf16[2048,128]{1,0:T(8,128)(2,1)S(1)} %gather_fusion.1) | copy-start | bytes 1572868
  75.3 1.4 copy-start.14
  76.5 64.6 %reduce-scatter.5.cloned.1.call-start = ((), (), s32[]{:S(2)}) async-start(), calls=%async_computation.7 | async-start | bytes 3145728 | tf_op jit(solution)/shard_map/reduce_scatter | solution.py:73
  86.4 3.6 copy-start.7
  101.7 20.2 %copy-start.12 = (bf16[2,128,256]{2,1,0:T(8,128)(2,1)S(1)}, bf16[2,128,256]{2,1,0:T(8,128)(2,1)}, u32[]{:S(2)}) copy-start(bf16[2,128,256]{2,1,0:T(8,128)(2,1)} %param.21) | copy-start | bytes 393220
  121.9 19.2 %copy-start.2 = (bf16[2048,128]{1,0:T(8,128)(2,1)S(1)}, bf16[2048,128]{1,0:T(8,128)(2,1)}, u32[]{:S(2)}) copy-start(bf16[2048,128]{1,0:T(8,128)(2,1)} %copy-done.1) | copy-start | bytes 1572868
  124.8 18.9 %copy-start.15 = (f32[2,256]{1,0:T(2,128)S(1)}, f32[2,256]{1,0:T(2,128)}, u32[]{:S(2)}) copy-start(f32[2,256]{1,0:T(2,128)} %param.25) | copy-start | bytes 6148
  124.8 38.1 %copy-start.16 = (bf16[2,512,256]{2,1,0:T(8,128)(2,1)S(1)}, bf16[2,512,256]{2,1,0:T(8,128)(2,1)}, u32[]{:S(2)}) copy-start(bf16[2,512,256]{2,1,0:T(8,128)(2,1)} %param.23) | copy-start | bytes 1572868
  124.8 38.1 %copy-start.18 = (bf16[2,256,512]{2,1,0:T(8,128)(2,1)S(1)}, bf16[2,256,512]{2,1,0:T(8,128)(2,1)}, u32[]{:S(2)}) copy-start(bf16[2,256,512]{2,1,0:T(8,128)(2,1)} %param.22) | copy-start | bytes 1572868
  124.8 34.5 %all-gather.7.cloned.1.call-start = ((), (), s32[]{:S(2)}) async-start(), calls=%async_computation.8 | async-start | bytes 1572864 | tf_op jit(solution)/shard_map/all_gather | solution.py:75
  143.5 39.0 %reduce-scatter.7.cloned.1.call-start = ((), (), s32[]{:S(2)}) async-start(), calls=%async_computation.9 | async-start | bytes 3145728 | tf_op jit(solution)/shard_map/reduce_scatter | solution.py:82
  159.4 3.6 copy-start.9
  166.2 16.3 %copy-start.5 = (bf16[2048,128]{1,0:T(8,128)(2,1)S(1)}, bf16[2048,128]{1,0:T(8,128)(2,1)}, u32[]{:S(2)}) copy-start(bf16[2048,128]{1,0:T(8,128)(2,1)} %add_convert_fusion.3) | copy-start | bytes 1572868
  198.0 44.6 %all-to-all-start.1 = ((bf16[128,32,128]{2,1,0:T(8,128)(2,1)}), bf16[128,32,128]{2,1,0:T(8,128)(2,1)S(1)}, u32[]{:S(2)}, u32[]{:S(2)}) async-start(bf16[128,32,128]{2,1,0:T(8,128)(2,1)} %broadcast_select_fusion), calls=%async_computation.3 | async-start | bytes 2097152 | tf_op jit(solution)/shard_map/all_to_all | solution.py:23
  211.7 47.5 %all-gather.9.cloned.1.call-start = ((), (), s32[]{:S(2)}) async-start(), calls=%async_computation.10 | async-start | bytes 1572864 | tf_op jit(solution)/shard_map/all_gather | solution.py:60
  248.8 15.0 %copy-start.3 = (bf16[2048,128]{1,0:T(8,128)(2,1)}, bf16[2048,128]{1,0:T(8,128)(2,1)S(1)}, u32[]{:S(2)}) copy-start(bf16[2048,128]{1,0:T(8,128)(2,1)S(1)} %gather_fusion.3) | copy-start | bytes 1572868
  249.9 63.9 %reduce-scatter.9.cloned.1.call-start = ((), (), s32[]{:S(2)}) async-start(), calls=%async_computation.11 | async-start | bytes 3145728 | tf_op jit(solution)/shard_map/reduce_scatter | solution.py:73
  259.2 3.6 copy-start.8
  294.7 19.1 %copy-start.4 = (bf16[2048,128]{1,0:T(8,128)(2,1)S(1)}, bf16[2048,128]{1,0:T(8,128)(2,1)}, u32[]{:S(2)}) copy-start(bf16[2048,128]{1,0:T(8,128)(2,1)} %copy-done.3) | copy-start | bytes 1572868
  297.6 38.1 %copy-start.17 = (bf16[2,512,256]{2,1,0:T(8,128)(2,1)S(1)}, bf16[2,512,256]{2,1,0:T(8,128)(2,1)}, u32[]{:S(2)}) copy-start(bf16[2,512,256]{2,1,0:T(8,128)(2,1)} %param.23) | copy-start | bytes 1572868
  297.6 38.1 %copy-start.19 = (bf16[2,256,512]{2,1,0:T(8,128)(2,1)S(1)}, bf16[2,256,512]{2,1,0:T(8,128)(2,1)}, u32[]{:S(2)}) copy-start(bf16[2,256,512]{2,1,0:T(8,128)(2,1)} %param.22) | copy-start | bytes 1572868
  297.6 34.5 %all-gather.11.cloned.1.call-start = ((), (), s32[]{:S(2)}) async-start(), calls=%async_computation.12 | async-start | bytes 1572864 | tf_op jit(solution)/shard_map/all_gather | solution.py:75
  316.2 39.0 %reduce-scatter.11.cloned.1.call-start = ((), (), s32[]{:S(2)}) async-start(), calls=%async_computation.13 | async-start | bytes 3145728 | tf_op jit(solution)/shard_map/reduce_scatter | solution.py:82
  332.2 3.6 copy-start.10
  339.0 16.3 %copy-start.6 = (bf16[2048,128]{1,0:T(8,128)(2,1)S(1)}, bf16[2048,128]{1,0:T(8,128)(2,1)}, u32[]{:S(2)}) copy-start(bf16[2048,128]{1,0:T(8,128)(2,1)} %add_convert_fusion.1) | copy-start | bytes 1572868
Sparse Core Ops, SparseCore 0:
  76.6 9.6 all-gather.4
  124.9 16.1 reduce-scatter.4
  143.6 15.7 all-gather.6
  166.4 16.0 reduce-scatter.6
  250.0 9.0 all-gather.8
  297.7 16.1 reduce-scatter.8
  316.4 15.7 all-gather.10
  339.1 16.1 reduce-scatter.10
where the time goes:
time: 365 us; the launch traced here: 364 us
  waiting for transfers between devices  176 us (48%)
  local copies, waits for them, and re-layouts  63 us (17%)
  matrix products  50.6 us (14%)
  starting transfers between devices  30.8 us (8%)
  other arithmetic  30.1 us (8%)
  between operations  14 us (4%)
    all_to_all x2, waiting for transfers between devices, regroup(): lax.all_to_all(picked, 'pts', split_axis=0, concat_axis=0, tiled=True)  60.9 us
    reduce_scatter x2, waiting for transfers between devices, shards(): lax.psum_scatter(partial_value, 'ch', scatter_dimension=1, tiled=True)  32.4 us
    reduce_scatter x2, waiting for transfers between devices, shards(): lax.psum_scatter(jnp.dot(hidden_act, down_weight[layer_index], preferred_...  32.2 us
    all_gather x2, waiting for transfers between devices, shards(): full_h = lax.all_gather(hstream, 'ch', axis=1, tiled=True)  31.3 us
    all_to_all x2, starting transfers between devices, regroup(): lax.all_to_all(picked, 'pts', split_axis=0, concat_axis=0, tiled=True)  30.1 us
    gather x2, local copies, waits for them, and re-layouts, regroup(): picked = jnp.take(stream, jnp.maximum(send_table, 0), axis=0)  24.3 us
    sub x4, matrix products, one_window(): weights = jax.nn.softmax(scores, axis=-1).astype(jnp.bfloat16)  19.5 us
    all_gather x2, waiting for transfers between devices, shards(): whole_rows = lax.all_gather(stream, 'ch', axis=1, tiled=True)  18.6 us
  transfers between devices with their start and end apart: 10, of which 10 were waited for; matrix products, arithmetic and copies ran while one was open for 0% of the time, Pallas kernels for 0%

commit v1 on v0

v1 whole, which is shorter than its diff:
```python
import math

import jax
import jax.numpy as jnp
from jax import lax
from jax.experimental import pallas as pl
from jax.experimental.pallas import tpu as pltpu
from jax.sharding import PartitionSpec as P

D = 256
HALF = 128
HEAD = 64
WIN = 1024
BLOCKS = 2
SWAP = [(0, 1), (1, 0)]
LANES = 128
ROW_TILE = 512
QUERY_TILE = 256
VMEM = 40 * 1024 * 1024


def swap(value):
    return lax.ppermute(value, "ch", SWAP)


def one_hot_rows(index_row, depth):
    count = index_row.shape[1]
    wide = jnp.concatenate(
        [
            jnp.transpose(jnp.broadcast_to(index_row[:, at : at + LANES], (LANES, LANES)))
            for at in range(0, count, LANES)
        ],
        axis=0,
    )
    block = jnp.right_shift(wide, 7)
    inner = jnp.bitwise_and(wide, LANES - 1)
    lane = lax.broadcasted_iota(jnp.int32, (count, LANES), 1)
    base = jnp.where(inner == lane, 1.0, 0.0).astype(jnp.bfloat16)
    block = block.astype(jnp.float32).astype(jnp.bfloat16)
    zero = jnp.zeros_like(base)
    return jnp.concatenate(
        [jnp.where(block == k, base, zero) for k in range(depth // LANES)], axis=1
    )


def pick_kernel(index_ref, *refs):
    sources, out_ref = refs[:-1], refs[-1]
    total = None
    width = sources[0].shape[0]
    hot = one_hot_rows(index_ref[0], width * len(sources))
    for n, source in enumerate(sources):
        part = jnp.dot(
            hot[:, n * width : (n + 1) * width], source[...], preferred_element_type=jnp.float32
        )
        total = part if total is None else total + part
    out_ref[...] = total.astype(jnp.bfloat16)


def pick(index, *sources):
    count = index.size
    depth = sum(source.shape[0] for source in sources)
    steps = count // ROW_TILE
    return pl.pallas_call(
        pick_kernel,
        grid=(steps,),
        in_specs=[pl.BlockSpec((1, 1, ROW_TILE), lambda i: (i, 0, 0))]
        + [pl.BlockSpec(source.shape, lambda i: (0, 0)) for source in sources],
        out_specs=pl.BlockSpec((ROW_TILE, HALF), lambda i: (i, 0)),
        out_shape=jax.ShapeDtypeStruct((count, HALF), jnp.bfloat16),
        compiler_params=pltpu.CompilerParams(vmem_limit_bytes=VMEM),
        cost_estimate=pl.CostEstimate(
            flops=4 * count * depth * HALF, bytes_accessed=(count + depth) * 256, transcendentals=0
        ),
    )(index.reshape(steps, 1, ROW_TILE), *sources)


def layer_norm(values, gain):
    average = jnp.mean(values, axis=-1, keepdims=True)
    centred = values - average
    spread = jnp.mean(centred * centred, axis=-1, keepdims=True)
    return centred * lax.rsqrt(spread + 1e-05) * gain


def gelu(x):
    inner = x * (math.sqrt(2 / math.pi) + (math.sqrt(2 / math.pi) * 0.044715) * (x * x))
    half = 0.5 * x
    return half + half * jnp.tanh(inner)


def block_kernel(
    core_ref,
    mine_ref,
    got_ref,
    qkv_a,
    qkv_b,
    out_a,
    out_b,
    up_a,
    up_b,
    down_a,
    down_b,
    gain_a,
    gain_m,
    keep_ref,
    give_ref,
    proj_ref,
    attended_ref,
):
    first = core_ref[0] == 0
    mine, got = mine_ref[...], got_ref[...]
    low = jnp.where(first, mine, got)
    high = jnp.where(first, got, mine)
    current = jnp.concatenate([low, high], axis=1)
    normed = layer_norm(current.astype(jnp.float32), gain_a[...]).astype(jnp.bfloat16)
    for n, weight in enumerate((qkv_a, qkv_b)):
        proj_ref[n] = jnp.dot(normed, weight[...], preferred_element_type=jnp.float32).astype(
            jnp.bfloat16
        )
    factor = math.log2(math.e) / math.sqrt(HEAD)
    for n in range(2):
        keys = proj_ref[n, :, HALF : 2 * HALF]
        values = proj_ref[n, :, 2 * HALF :]
        low_wide = lax.broadcasted_iota(jnp.int32, (WIN, HALF), 1) < HEAD
        one = jnp.ones_like(values)
        rights = (jnp.where(low_wide, values, one), jnp.where(low_wide, one, values))
        for at in range(0, WIN, QUERY_TILE):
            query = proj_ref[n, at : at + QUERY_TILE, :HALF]
            low_lane = lax.broadcasted_iota(jnp.int32, (QUERY_TILE, HALF), 1) < HEAD
            zero = jnp.zeros_like(query)
            lefts = (jnp.where(low_lane, query, zero), jnp.where(low_lane, zero, query))
            sums = []
            for left, right in zip(lefts, rights):
                scores = lax.dot_general(
                    left, keys, (((1,), (1,)), ((), ())), preferred_element_type=jnp.float32
                )
                top = jnp.max(scores, axis=1, keepdims=True)
                weights = jnp.exp2((scores - top) * factor).astype(jnp.bfloat16)
                sums.append(jnp.dot(weights, right, preferred_element_type=jnp.float32))
            top_part = jnp.where(low_lane, sums[0], sums[1])
            bottom = jnp.where(
                low_lane, pltpu.roll(sums[0], HEAD, 1), pltpu.roll(sums[1], HEAD, 1)
            )
            attended_ref[n, at : at + QUERY_TILE, :] = (top_part / bottom).astype(jnp.bfloat16)
    added = jnp.dot(attended_ref[0], out_a[...], preferred_element_type=jnp.float32) + jnp.dot(
        attended_ref[1], out_b[...], preferred_element_type=jnp.float32
    )
    hstream = (current.astype(jnp.float32) + added).astype(jnp.bfloat16)
    normed_two = layer_norm(hstream.astype(jnp.float32), gain_m[...]).astype(jnp.bfloat16)
    result = hstream.astype(jnp.float32)
    for up, down in ((up_a, down_a), (up_b, down_b)):
        hidden = gelu(jnp.dot(normed_two, up[...], preferred_element_type=jnp.float32))
        result = result + jnp.dot(
            hidden.astype(jnp.bfloat16), down[...], preferred_element_type=jnp.float32
        )
    result = result.astype(jnp.bfloat16)
    low, high = result[:, :HALF], result[:, HALF:]
    keep_ref[...] = jnp.where(first, low, high)
    give_ref[...] = jnp.where(first, high, low)


def window_block(core, mine, got, weights, gain_attn, gain_mlp):
    half = jax.ShapeDtypeStruct((WIN, HALF), jnp.bfloat16)
    whole = pl.BlockSpec(memory_space=pltpu.VMEM)
    return pl.pallas_call(
        block_kernel,
        in_specs=[pl.BlockSpec(memory_space=pltpu.SMEM)] + [whole] * (4 + len(weights)),
        out_specs=[whole, whole],
        out_shape=[half, half],
        scratch_shapes=[
            pltpu.VMEM((2, WIN, 3 * HALF), jnp.bfloat16),
            pltpu.VMEM((2, WIN, HALF), jnp.bfloat16),
        ],
        compiler_params=pltpu.CompilerParams(vmem_limit_bytes=VMEM),
        cost_estimate=pl.CostEstimate(
            flops=6_000_000_000, bytes_accessed=3_000_000, transcendentals=5_000_000
        ),
    )(core, mine, got, *weights, gain_attn, gain_mlp)


def shards(
    stream,
    send_rows,
    recv_slots,
    qkv_weight,
    out_weight,
    up_weight,
    down_weight,
    gain_attn,
    gain_mlp,
):
    core = lax.axis_index("ch")
    core_word = core.astype(jnp.int32).reshape(1)
    qkv = qkv_weight.reshape(BLOCKS, D, 3 * HALF)
    owned = (qkv, out_weight, up_weight, down_weight)
    fetched = tuple(swap(array) for array in owned)
    sources = (stream,)
    flip = 0
    for layer in range(BLOCKS):
        index = jnp.maximum(send_rows[layer], 0) ^ flip
        picked = pick(index, *sources)
        moved = lax.all_to_all(
            picked.reshape(-1, 32, HALF), "pts", split_axis=0, concat_axis=0, tiled=True
        ).reshape(-1, HALF)
        slots = recv_slots[layer].reshape(2, WIN)
        theirs = lax.dynamic_index_in_dim(slots, 1 - core, 0, keepdims=False)
        ours = lax.dynamic_index_in_dim(slots, core, 0, keepdims=False)
        got = swap(pick(theirs, moved))
        mine = pick(ours, moved)
        weights = []
        for own, other in zip(owned, fetched):
            weights += [own[layer], other[layer]]
        keep, give = window_block(
            core_word, mine, got, weights, gain_attn[layer : layer + 1], gain_mlp[layer : layer + 1]
        )
        back = swap(give)
        sources = (keep, back)
        flip = core * WIN
    result = jnp.zeros((2 * WIN, HALF), jnp.bfloat16)
    result = lax.dynamic_update_slice(result, keep, (core * WIN, 0))
    return lax.dynamic_update_slice(result, back, ((1 - core) * WIN, 0))


def solution(mesh):
    in_specs = (
        P("pts", "ch"),
        P(None, "pts", None),
        P(None, "pts"),
        P(None, None, None, "ch"),
        P(None, "ch", None),
        P(None, None, "ch"),
        P(None, "ch", None),
        P(),
        P(),
    )
    out_specs = P("pts", "ch")
    return jax.shard_map(shards, mesh=mesh, in_specs=in_specs, out_specs=out_specs, check_vma=False)
```

time: 365 us -> 145 us (0.40)
  waiting for transfers between devices: 176 us -> 54.3 us
  local copies, waits for them, and re-layouts: 63 us -> 12.2 us
  matrix products: 50.6 us -> 0 us
  Pallas kernels: 0 us -> 46.5 us
  other arithmetic: 30.1 us -> 1.34 us
  between operations: 14 us -> 0.33 us
    reduce_scatter x4 -> x0, waiting for transfers between devices: 64.6 us -> none  [the longest x2 32.4 us: shards(): lax.psum_scatter(partial_value, 'ch', scatter_dimension=1, tiled=True)]
    all_gather x4 -> x0, waiting for transfers between devices: 49.9 us -> none  [the longest x2 31.3 us: shards(): full_h = lax.all_gather(hstream, 'ch', axis=1, tiled=True)]
    pallas_call x0 -> x8, Pallas kernels: none -> 46.5 us  [the longest x6 24.2 us: pick(): pl.pallas_call(pick_kernel, grid=(steps,), in_specs=[pl.BlockSpec((1, 1,...]
    gather x4 -> x0, local copies, waits for them, and re-layouts: 36.6 us -> none  [the longest x2 24.3 us: regroup(): picked = jnp.take(stream, jnp.maximum(send_table, 0), axis=0)]
    dot_general x10 -> x0, matrix products: 31.1 us -> none  [the longest x4 16.9 us: one_window(): jnp.einsum('hqk,khd->qhd', weights, window_rows[:, 2], preferred_element_...]
    sub x4 -> x0, matrix products: 19.5 us -> none  [one_window(): weights = jax.nn.softmax(scores, axis=-1).astype(jnp.bfloat16)]
    reduce_sum x8 -> x0, other arithmetic: 14.1 us -> none  [the longest x4 7.45 us: layer_norm(): spread = jnp.mean(centred * centred, axis=-1, keepdims=True)]
    while x2 -> x0, local copies, waits for them, and re-layouts: 13.7 us -> none  [attend(): return lax.map(one_window, windows).reshape(points, local_width)]
  transfers between devices with their start and end apart: 10 -> 10, of which waited for: 10 -> 4; matrix products, arithmetic and copies ran while one was open for 0% -> 7% of each run, Pallas kernels for 0% -> 5%
where the time goes in v1:
time: 145 us; the launch traced here: 144 us
  waiting for transfers between devices  54.3 us (37%)
  Pallas kernels  46.5 us (32%)
  starting transfers between devices  29.5 us (20%)
  local copies, waits for them, and re-layouts  12.2 us (8%)
    all_to_all x2, waiting for transfers between devices, shards(): lax.all_to_all(picked.reshape(-1, 32, HALF), 'pts', split_axis=0, concat_...  51.6 us
    pallas_call x6, Pallas kernels, pick(): pl.pallas_call(pick_kernel, grid=(steps,), in_specs=[pl.BlockSpec((1, 1,...  24.2 us
    all_to_all x2, starting transfers between devices, shards(): lax.all_to_all(picked.reshape(-1, 32, HALF), 'pts', split_axis=0, concat_...  22.8 us
    pallas_call x2, Pallas kernels, window_block(): pl.pallas_call(block_kernel, in_specs=[pl.BlockSpec(memory_space=pltpu.SM...  22.3 us
    squeeze x9, local copies, waits for them, and re-layouts, shards(): weights += [own[layer], other[layer]]  6.93 us
    ppermute x8, starting transfers between devices, swap(): return lax.ppermute(value, 'ch', SWAP)  6.71 us
  transfers between devices with their start and end apart: 10, of which 4 were waited for; matrix products, arithmetic and copies ran while one was open for 7% of the time, Pallas kernels for 5%

profile of v1, /device:TPU:1, one launch (start us, length us, event | category | flops | bytes accessed | tf_op | source)
XLA Modules:
  0.0 144.2 jit_solution(11314078793404981637)
XLA Ops:
  0.0 1.3 slice_maximum_fusion
  1.3 0.1 copy.16
  1.4 0.1 max.27.index_ref
  1.5 0.0 copy-start.4
  1.5 1.0 copy-done.4
  2.6 6.8 %shard_map.91 = bf16[4096,128]{1,0:T(8,128)(2,1)} custom-call(s32[8,1,512]{2,1,0:T(1,128)S(1)} %max.27.index_ref, bf16[2048,128]{1,0:T(8,128)(2,1)S(1)} %copy-done.4), custom_call_target="tpu_custom_call" | custom-call | flops 4294967296 | bytes 1572864 | tf_op jit(solution)/shard_map/pallas_call | solution.py:63
  9.4 16.5 %all-to-all-start = ((bf16[128,32,128]{2,1,0:T(8,128)(2,1)}), bf16[128,32,128]{2,1,0:T(8,128)(2,1)S(1)}, u32[]{:S(2)}, u32[]{:S(2)}) async-start(bf16[128,32,128]{2,1,0:T(8,128)(2,1)} %bitcast.3), calls=%async_computation | async-start | bytes 2097152 | tf_op jit(solution)/shard_map/all_to_all | solution.py:201
  25.9 0.0 copy-done.7
  25.9 0.2 copy.18
  26.1 0.0 copy-start.8
  26.1 0.0 copy-start.12
  26.1 0.0 copy-start.13
  26.1 0.2 copy.20
  26.3 1.0 collective-permute-start.1
  27.4 0.1 collective-permute-start.4
  27.5 0.4 collective-permute-start.3
  27.9 0.0 copy-done.8
  27.9 0.1 collective-permute-start.2
  28.0 0.0 copy-done.12
  28.0 0.6 fusion.1
  28.6 0.6 slice_bitcast_fusion.12
  29.2 0.7 fusion
  29.9 1.1 slice_bitcast_fusion.4
  31.0 0.0 copy-start.11
  31.0 1.1 slice_bitcast_fusion.5
  32.1 0.6 slice_reduce_fusion
  32.7 0.2 copy.21.qkv_a
  32.9 0.0 collective-permute-done.2
  32.9 0.7 slice_bitcast_fusion.10
  33.6 0.0 collective-permute-done.1
  33.6 1.1 slice_bitcast_fusion.8
  34.6 0.0 collective-permute-done.4
  34.7 1.1 slice_bitcast_fusion
  35.7 20.4 %all-to-all-done = bf16[128,32,128]{2,1,0:T(8,128)(2,1)S(1)} async-done(((bf16[128,32,128]{2,1,0:T(8,128)(2,1)}), bf16[128,32,128]{2,1,0:T(8,128)(2,1)S(1)}, u32[]{:S(2)}, u32[]{:S(2)}) %all-to-all-start) | async-done | bytes 1048608 | tf_op jit(solution)/shard_map/all_to_all | solution.py:201
  56.1 2.6 %shard_map.93 = bf16[1024,128]{1,0:T(8,128)(2,1)S(1)} custom-call(s32[2,1,512]{2,1,0:T(1,128)S(1)} %bitcast.45, bf16[4096,128]{1,0:T(8,128)(2,1)S(1)} %bitcast.40), custom_call_target="tpu_custom_call" | custom-call | flops 2147483648 | bytes 1310720 | tf_op jit(solution)/shard_map/pallas_call | solution.py:63
  58.8 2.9 %collective-permute-start = (bf16[1024,128]{1,0:T(8,128)(2,1)S(1)}, bf16[1024,128]{1,0:T(8,128)(2,1)S(1)}, u32[]{:S(2)}, u32[]{:S(2)}) collective-permute-start(bf16[1024,128]{1,0:T(8,128)(2,1)S(1)} %shard_map.93), channel_id=1, source_target_pairs={{0,1},{1,0},{2,3},{3,2},{4,5},{5,4},{6,7},{7,6},{8,9},{9,8},{10,11... | collective-permute-start | bytes 786440 | tf_op jit(solution)/shard_map/ppermute | solution.py:23
  61.7 0.0 collective-permute-done.3
  61.7 1.1 slice_bitcast_fusion.1
  62.7 0.0 copy-start.1
  62.8 0.0 copy-start.2
  62.8 2.6 %shard_map.92.mine_ref = bf16[1024,128]{1,0:T(8,128)(2,1)S(1)} custom-call(s32[2,1,512]{2,1,0:T(1,128)S(1)} %bitcast.44, bf16[4096,128]{1,0:T(8,128)(2,1)S(1)} %bitcast.41), custom_call_target="tpu_custom_call" | custom-call | flops 2147483648 | bytes 1310720 | tf_op jit(solution)/shard_map/pallas_call | solution.py:63
  65.4 0.0 collective-permute-done.got_ref
  65.5 0.6 copy-done.3
  66.1 11.1 %shard_map.94 = (bf16[1024,128]{1,0:T(8,128)(2,1)S(1)}, bf16[1024,128]{1,0:T(8,128)(2,1)S(1)}) custom-call(s32[1]{0:T(128)} %bitcast.core_ref, bf16[1024,128]{1,0:T(8,128)(2,1)S(1)} %shard_map.92.mine_ref, bf16[1024,128]{1,0:T(8,128)(2,1)S(1)} %collective-permute-done.got_ref, bf16[256,384]{1,0:T(8,128)(2,1)S(1)} %copy.21.qkv_a, ...), custom_call_target="tpu_custom_call" | custom-call | flops 6000000000 | bytes 3000000 | tf_op jit(solution)/shard_map/pallas_call | solution.py:164
  77.2 0.1 collective-permute-start.5
  77.3 0.0 copy-done.9
  77.4 0.1 copy.15
  77.4 0.1 xor.19.index_ref
  77.6 1.3 collective-permute-done.5.refs_1_
  78.9 6.8 %shard_map.95 = bf16[4096,128]{1,0:T(8,128)(2,1)} custom-call(s32[8,1,512]{2,1,0:T(1,128)S(1)} %xor.19.index_ref, bf16[1024,128]{1,0:T(8,128)(2,1)S(1)} %get-tuple-element.9.refs_0_, bf16[1024,128]{1,0:T(8,128)(2,1)S(1)} %collective-permute-done.5.refs_1_), custom_call_target="tpu_custom_call" | custom-call | flops 4294967296 | bytes 1572864 | tf_op jit(solution)/shard_map/pallas_call | solution.py:63
  85.7 6.3 %all-to-all-start.1 = ((bf16[128,32,128]{2,1,0:T(8,128)(2,1)}), bf16[128,32,128]{2,1,0:T(8,128)(2,1)S(1)}, u32[]{:S(2)}, u32[]{:S(2)}) async-start(bf16[128,32,128]{2,1,0:T(8,128)(2,1)} %bitcast.15), calls=%async_computation.1 | async-start | bytes 2097152 | tf_op jit(solution)/shard_map/all_to_all | solution.py:201
  92.1 31.2 %all-to-all-done.1 = bf16[128,32,128]{2,1,0:T(8,128)(2,1)S(1)} async-done(((bf16[128,32,128]{2,1,0:T(8,128)(2,1)}), bf16[128,32,128]{2,1,0:T(8,128)(2,1)S(1)}, u32[]{:S(2)}, u32[]{:S(2)}) %all-to-all-start.1) | async-done | bytes 1048608 | tf_op jit(solution)/shard_map/all_to_all | solution.py:201
  123.3 2.6 %shard_map.97 = bf16[1024,128]{1,0:T(8,128)(2,1)S(1)} custom-call(s32[2,1,512]{2,1,0:T(1,128)S(1)} %bitcast.47, bf16[4096,128]{1,0:T(8,128)(2,1)S(1)} %bitcast.42), custom_call_target="tpu_custom_call" | custom-call | flops 2147483648 | bytes 1310720 | tf_op jit(solution)/shard_map/pallas_call | solution.py:63
  125.9 1.9 %collective-permute-start.6 = (bf16[1024,128]{1,0:T(8,128)(2,1)S(1)}, bf16[1024,128]{1,0:T(8,128)(2,1)S(1)}, u32[]{:S(2)}, u32[]{:S(2)}) collective-permute-start(bf16[1024,128]{1,0:T(8,128)(2,1)S(1)} %shard_map.97), channel_id=1, source_target_pairs={{0,1},{1,0},{2,3},{3,2},{4,5},{5,4},{6,7},{7,6},{8,9},{9,8},{10,11... | collective-permute-start | bytes 786440 | tf_op jit(solution)/shard_map/ppermute | solution.py:23
  127.9 0.2 copy.24.qkv_a
  128.0 0.0 copy-start
  128.0 2.6 %shard_map.96.mine_ref = bf16[1024,128]{1,0:T(8,128)(2,1)S(1)} custom-call(s32[2,1,512]{2,1,0:T(1,128)S(1)} %bitcast.46, bf16[4096,128]{1,0:T(8,128)(2,1)S(1)} %bitcast.43), custom_call_target="tpu_custom_call" | custom-call | flops 2147483648 | bytes 1310720 | tf_op jit(solution)/shard_map/pallas_call | solution.py:63
  130.7 0.0 collective-permute-done.6.got_ref
  130.7 11.1 %shard_map.98 = (bf16[1024,128]{1,0:T(8,128)(2,1)S(1)}, bf16[1024,128]{1,0:T(8,128)(2,1)S(1)}) custom-call(s32[1]{0:T(128)} %bitcast.core_ref, bf16[1024,128]{1,0:T(8,128)(2,1)S(1)} %shard_map.96.mine_ref, bf16[1024,128]{1,0:T(8,128)(2,1)S(1)} %collective-permute-done.6.got_ref, bf16[256,384]{1,0:T(8,128)(2,1)S(1)} %copy.24.qkv_a, ...), custom_call_target="tpu_custom_call" | custom-call | flops 6000000000 | bytes 3000000 | tf_op jit(solution)/shard_map/pallas_call | solution.py:164
  141.8 0.1 collective-permute-start.7
  142.0 0.1 broadcast_in_dim.3
  142.1 0.0 copy-start.6
  142.1 1.4 collective-permute-done.7
  143.5 0.7 constant_dynamic-update-slice_fusion
  (18 shorter events, 0.1 us)
Async XLA Ops:
  1.5 1.0 copy-start.4
  9.4 16.5 %copy-start.7 = (bf16[2,256,3,128]{3,1,2,0:T(8,128)(2,1)S(1)}, bf16[2,256,3,128]{3,1,2,0:T(8,128)(2,1)}, u32[]{:S(2)}) copy-start(bf16[2,256,3,128]{3,1,2,0:T(8,128)(2,1)} %param.12) | copy-start | bytes 1179652
  9.4 46.7 %all-to-all-start = ((bf16[128,32,128]{2,1,0:T(8,128)(2,1)}), bf16[128,32,128]{2,1,0:T(8,128)(2,1)S(1)}, u32[]{:S(2)}, u32[]{:S(2)}) async-start(bf16[128,32,128]{2,1,0:T(8,128)(2,1)} %bitcast.3), calls=%async_computation | async-start | bytes 2097152 | tf_op jit(solution)/shard_map/all_to_all | solution.py:201
  26.1 1.8 %copy-start.8 = (bf16[2,128,256]{2,1,0:T(8,128)(2,1)S(1)}, bf16[2,128,256]{2,1,0:T(8,128)(2,1)}, u32[]{:S(2)}) copy-start(bf16[2,128,256]{2,1,0:T(8,128)(2,1)} %param.13) | copy-start | bytes 393220
  26.1 1.9 %copy-start.12 = (f32[2,256]{1,0:T(2,128)S(1)}, f32[2,256]{1,0:T(2,128)}, u32[]{:S(2)}) copy-start(f32[2,256]{1,0:T(2,128)} %param.17) | copy-start | bytes 6148
  26.1 1.9 %copy-start.13 = (f32[2,256]{1,0:T(2,128)S(1)}, f32[2,256]{1,0:T(2,128)}, u32[]{:S(2)}) copy-start(f32[2,256]{1,0:T(2,128)} %param.16) | copy-start | bytes 6148
  26.3 7.2 %collective-permute-start.1 = (bf16[2,256,384]{2,1,0:T(8,128)(2,1)S(1)}, bf16[2,256,384]{2,1,0:T(8,128)(2,1)}, u32[]{:S(2)}, u32[]{:S(2)}) collective-permute-start(bf16[2,256,384]{2,1,0:T(8,128)(2,1)S(1)} %copy.20), channel_id=1, source_target_pairs={{0,1},{1,0},{2,3},{3,2},{4,5},{5,4},{6,7},{7,6},{8,9},{9,8},{10,11... | collective-permute-start | bytes 1179656 | tf_op jit(solution)/shard_map/ppermute | solution.py:23
  27.4 7.3 %collective-permute-start.4 = (bf16[2,512,256]{2,1,0:T(8,128)(2,1)}, bf16[2,512,256]{2,1,0:T(8,128)(2,1)}, u32[]{:S(2)}, u32[]{:S(2)}) collective-permute-start(bf16[2,512,256]{2,1,0:T(8,128)(2,1)} %param.15), channel_id=1, source_target_pairs={{0,1},{1,0},{2,3},{3,2},{4,5},{5,4},{6,7},{7,6},{8,9},{9,8},{10,11... | collective-permute-start | bytes 1572872 | tf_op jit(solution)/shard_map/ppermute | solution.py:23
  27.5 34.2 %collective-permute-start.3 = (bf16[2,256,512]{2,1,0:T(8,128)(2,1)}, bf16[2,256,512]{2,1,0:T(8,128)(2,1)}, u32[]{:S(2)}, u32[]{:S(2)}) collective-permute-start(bf16[2,256,512]{2,1,0:T(8,128)(2,1)} %param.14), channel_id=1, source_target_pairs={{0,1},{1,0},{2,3},{3,2},{4,5},{5,4},{6,7},{7,6},{8,9},{9,8},{10,11... | collective-permute-start | bytes 1572872 | tf_op jit(solution)/shard_map/ppermute | solution.py:23
  27.9 5.0 %collective-permute-start.2 = (bf16[2,128,256]{2,1,0:T(8,128)(2,1)S(1)}, bf16[2,128,256]{2,1,0:T(8,128)(2,1)S(1)}, u32[]{:S(2)}, u32[]{:S(2)}) collective-permute-start(bf16[2,128,256]{2,1,0:T(8,128)(2,1)S(1)} %copy-done.8), channel_id=1, source_target_pairs={{0,1},{1,0},{2,3},{3,2},{4,5},{5,4},{6,7},{7,6},{8,9},{9,8},{10,11... | collective-permute-start | bytes 393224 | tf_op jit(solution)/shard_map/ppermute | solution.py:23
  31.0 1.1 copy-start.11
  58.8 6.6 %collective-permute-start = (bf16[1024,128]{1,0:T(8,128)(2,1)S(1)}, bf16[1024,128]{1,0:T(8,128)(2,1)S(1)}, u32[]{:S(2)}, u32[]{:S(2)}) collective-permute-start(bf16[1024,128]{1,0:T(8,128)(2,1)S(1)} %shard_map.93), channel_id=1, source_target_pairs={{0,1},{1,0},{2,3},{3,2},{4,5},{5,4},{6,7},{7,6},{8,9},{9,8},{10,11... | collective-permute-start | bytes 786440 | tf_op jit(solution)/shard_map/ppermute | solution.py:23
  62.7 2.7 %copy-start.1 = (bf16[128,256]{1,0:T(8,128)(2,1)S(1)}, bf16[128,256]{1,0:T(8,128)(2,1)}, u32[]{:S(2)}) copy-start(bf16[128,256]{1,0:T(8,128)(2,1)} %get-tuple-element.30.out_a) | copy-start | bytes 196612
  62.8 2.7 %copy-start.2 = (bf16[128,256]{1,0:T(8,128)(2,1)S(1)}, bf16[128,256]{1,0:T(8,128)(2,1)}, u32[]{:S(2)}) copy-start(bf16[128,256]{1,0:T(8,128)(2,1)} %get-tuple-element.28.out_b) | copy-start | bytes 196612
  65.4 0.7 copy-start.3
  66.1 11.3 %copy-start.9 = (s32[1,128,32]{1,2,0:T(8,128)S(1)}, s32[1,128,32]{1,2,0:T(8,128)}, u32[]{:S(2)}) copy-start(s32[1,128,32]{1,2,0:T(8,128)} %get-tuple-element.32) | copy-start | bytes 49156
  77.2 1.6 %collective-permute-start.5 = (bf16[1024,128]{1,0:T(8,128)(2,1)S(1)}, bf16[1024,128]{1,0:T(8,128)(2,1)S(1)}, u32[]{:S(2)}, u32[]{:S(2)}) collective-permute-start(bf16[1024,128]{1,0:T(8,128)(2,1)S(1)} %get-tuple-element.10), channel_id=1, source_target_pairs={{0,1},{1,0},{2,3},{3,2},{4,5},{5,4},{6,7},{7,6},{8,9},{9,8},{10,11... | collective-permute-start | bytes 786440 | tf_op jit(solution)/shard_map/ppermute | solution.py:23
  85.7 6.3 %copy-start.10 = (s32[2048]{0:T(1024)S(1)}, s32[2048]{0:T(1024)}, u32[]{:S(2)}) copy-start(s32[2048]{0:T(1024)} %get-tuple-element.14) | copy-start | bytes 24580
  85.7 37.6 %all-to-all-start.1 = ((bf16[128,32,128]{2,1,0:T(8,128)(2,1)}), bf16[128,32,128]{2,1,0:T(8,128)(2,1)S(1)}, u32[]{:S(2)}, u32[]{:S(2)}) async-start(bf16[128,32,128]{2,1,0:T(8,128)(2,1)} %bitcast.15), calls=%async_computation.1 | async-start | bytes 2097152 | tf_op jit(solution)/shard_map/all_to_all | solution.py:201
  123.3 4.6 %copy-start.5 = (bf16[1,256,3,128]{1,3,2,0:T(8,128)(2,1)S(1)}, bf16[1,256,3,128]{1,3,2,0:T(8,128)(2,1)}, u32[]{:S(2)}) copy-start(bf16[1,256,3,128]{1,3,2,0:T(8,128)(2,1)} %get-tuple-element.25) | copy-start | bytes 589828
  125.9 4.8 %collective-permute-start.6 = (bf16[1024,128]{1,0:T(8,128)(2,1)S(1)}, bf16[1024,128]{1,0:T(8,128)(2,1)S(1)}, u32[]{:S(2)}, u32[]{:S(2)}) collective-permute-start(bf16[1024,128]{1,0:T(8,128)(2,1)S(1)} %shard_map.97), channel_id=1, source_target_pairs={{0,1},{1,0},{2,3},{3,2},{4,5},{5,4},{6,7},{7,6},{8,9},{9,8},{10,11... | collective-permute-start | bytes 786440 | tf_op jit(solution)/shard_map/ppermute | solution.py:23
  128.0 2.7 %copy-start = (bf16[128,256]{1,0:T(8,128)(2,1)S(1)}, bf16[128,256]{1,0:T(8,128)(2,1)}, u32[]{:S(2)}) copy-start(bf16[128,256]{1,0:T(8,128)(2,1)} %get-tuple-element.27.out_b) | copy-start | bytes 196612
  141.8 1.6 %collective-permute-start.7 = (bf16[1024,128]{1,0:T(8,128)(2,1)S(1)}, bf16[1024,128]{1,0:T(8,128)(2,1)S(1)}, u32[]{:S(2)}, u32[]{:S(2)}) collective-permute-start(bf16[1024,128]{1,0:T(8,128)(2,1)S(1)} %get-tuple-element.12), channel_id=1, source_target_pairs={{0,1},{1,0},{2,3},{3,2},{4,5},{5,4},{6,7},{7,6},{8,9},{9,8},{10,11... | collective-permute-start | bytes 786440 | tf_op jit(solution)/shard_map/ppermute | solution.py:23
  142.1 1.4 copy-start.6

commit v2 on v1

--- a/solution.py
+++ b/solution.py
@@ -13,9 +13,7 @@
 WIN = 1024
 BLOCKS = 2
 SWAP = [(0, 1), (1, 0)]
-LANES = 128
-ROW_TILE = 512
-QUERY_TILE = 256
+QUERY_TILE = 1024
 VMEM = 40 * 1024 * 1024
 
 
@@ -23,55 +21,44 @@
     return lax.ppermute(value, "ch", SWAP)
 
 
-def one_hot_rows(index_row, depth):
-    count = index_row.shape[1]
-    wide = jnp.concatenate(
-        [
-            jnp.transpose(jnp.broadcast_to(index_row[:, at : at + LANES], (LANES, LANES)))
-            for at in range(0, count, LANES)
-        ],
-        axis=0,
-    )
-    block = jnp.right_shift(wide, 7)
-    inner = jnp.bitwise_and(wide, LANES - 1)
-    lane = lax.broadcasted_iota(jnp.int32, (count, LANES), 1)
-    base = jnp.where(inner == lane, 1.0, 0.0).astype(jnp.bfloat16)
-    block = block.astype(jnp.float32).astype(jnp.bfloat16)
-    zero = jnp.zeros_like(base)
-    return jnp.concatenate(
-        [jnp.where(block == k, base, zero) for k in range(depth // LANES)], axis=1
-    )
-
-
 def pick_kernel(index_ref, *refs):
     sources, out_ref = refs[:-1], refs[-1]
+    index = index_ref[0].astype(jnp.int16)
     total = None
-    width = sources[0].shape[0]
-    hot = one_hot_rows(index_ref[0], width * len(sources))
-    for n, source in enumerate(sources):
-        part = jnp.dot(
-            hot[:, n * width : (n + 1) * width], source[...], preferred_element_type=jnp.float32
+    start = 0
+    for source in sources:
+        shape = (source.shape[0], index.shape[1])
+        row = lax.broadcasted_iota(jnp.int16, shape, 0) + jnp.int16(start)
+        hot = jnp.where(
+            jnp.broadcast_to(index, shape) == row,
+            jnp.ones(shape, jnp.bfloat16),
+            jnp.zeros(shape, jnp.bfloat16),
+        )
+        part = lax.dot_general(
+            source[...], hot, (((0,), (0,)), ((), ())), preferred_element_type=jnp.float32
         )
         total = part if total is None else total + part
-    out_ref[...] = total.astype(jnp.bfloat16)
+        start += shape[0]
+    out_ref[...] = total.T.astype(jnp.bfloat16)
 
 
 def pick(index, *sources):
     count = index.size
     depth = sum(source.shape[0] for source in sources)
-    steps = count // ROW_TILE
+    tile = min(count, 2048)
+    steps = count // tile
     return pl.pallas_call(
         pick_kernel,
         grid=(steps,),
-        in_specs=[pl.BlockSpec((1, 1, ROW_TILE), lambda i: (i, 0, 0))]
+        in_specs=[pl.BlockSpec((1, 1, tile), lambda i: (i, 0, 0))]
         + [pl.BlockSpec(source.shape, lambda i: (0, 0)) for source in sources],
-        out_specs=pl.BlockSpec((ROW_TILE, HALF), lambda i: (i, 0)),
+        out_specs=pl.BlockSpec((tile, HALF), lambda i: (i, 0)),
         out_shape=jax.ShapeDtypeStruct((count, HALF), jnp.bfloat16),
         compiler_params=pltpu.CompilerParams(vmem_limit_bytes=VMEM),
         cost_estimate=pl.CostEstimate(
             flops=4 * count * depth * HALF, bytes_accessed=(count + depth) * 256, transcendentals=0
         ),
-    )(index.reshape(steps, 1, ROW_TILE), *sources)
+    )(index.reshape(steps, 1, tile), *sources)
 
 
 def layer_norm(values, gain):
@@ -103,7 +90,6 @@
     gain_m,
     keep_ref,
     give_ref,
-    proj_ref,
     attended_ref,
 ):
     first = core_ref[0] == 0
@@ -112,37 +98,48 @@
     high = jnp.where(first, got, mine)
     current = jnp.concatenate([low, high], axis=1)
     normed = layer_norm(current.astype(jnp.float32), gain_a[...]).astype(jnp.bfloat16)
+    factor = math.log2(math.e) / math.sqrt(HEAD)
+    over_rows = (((0,), (1,)), ((), ()))
+    units = []
     for n, weight in enumerate((qkv_a, qkv_b)):
-        proj_ref[n] = jnp.dot(normed, weight[...], preferred_element_type=jnp.float32).astype(
-            jnp.bfloat16
-        )
-    factor = math.log2(math.e) / math.sqrt(HEAD)
-    for n in range(2):
-        keys = proj_ref[n, :, HALF : 2 * HALF]
-        values = proj_ref[n, :, 2 * HALF :]
-        low_wide = lax.broadcasted_iota(jnp.int32, (WIN, HALF), 1) < HEAD
-        one = jnp.ones_like(values)
-        rights = (jnp.where(low_wide, values, one), jnp.where(low_wide, one, values))
-        for at in range(0, WIN, QUERY_TILE):
-            query = proj_ref[n, at : at + QUERY_TILE, :HALF]
-            low_lane = lax.broadcasted_iota(jnp.int32, (QUERY_TILE, HALF), 1) < HEAD
-            zero = jnp.zeros_like(query)
-            lefts = (jnp.where(low_lane, query, zero), jnp.where(low_lane, zero, query))
-            sums = []
-            for left, right in zip(lefts, rights):
-                scores = lax.dot_general(
-                    left, keys, (((1,), (1,)), ((), ())), preferred_element_type=jnp.float32
-                )
-                top = jnp.max(scores, axis=1, keepdims=True)
-                weights = jnp.exp2((scores - top) * factor).astype(jnp.bfloat16)
-                sums.append(jnp.dot(weights, right, preferred_element_type=jnp.float32))
-            top_part = jnp.where(low_lane, sums[0], sums[1])
-            bottom = jnp.where(
-                low_lane, pltpu.roll(sums[0], HEAD, 1), pltpu.roll(sums[1], HEAD, 1)
-            )
-            attended_ref[n, at : at + QUERY_TILE, :] = (top_part / bottom).astype(jnp.bfloat16)
-    added = jnp.dot(attended_ref[0], out_a[...], preferred_element_type=jnp.float32) + jnp.dot(
-        attended_ref[1], out_b[...], preferred_element_type=jnp.float32
+        queries = lax.dot_general(
+            weight[:, :HALF], normed, over_rows, preferred_element_type=jnp.float32
+        ).astype(jnp.bfloat16)
+        keys = jnp.dot(
+            normed, weight[:, HALF : 2 * HALF], preferred_element_type=jnp.float32
+        ).astype(jnp.bfloat16)
+        values = lax.dot_general(
+            weight[:, 2 * HALF :], normed, over_rows, preferred_element_type=jnp.float32
+        ).astype(jnp.bfloat16)
+        zero = jnp.zeros((HEAD, WIN), jnp.bfloat16)
+        ones = jnp.ones((16, WIN), jnp.bfloat16)
+        for h in range(2):
+            rows = slice(h * HEAD, (h + 1) * HEAD)
+            pair = [zero, zero]
+            pair[h] = queries[rows]
+            query = jnp.concatenate(pair, axis=0)
+            value = jnp.concatenate([values[rows], ones], axis=0)
+            for at in range(0, WIN, QUERY_TILE):
+                units.append((keys, query[:, at : at + QUERY_TILE], value, n * HALF + h * HEAD, at))
+
+    def score(unit):
+        return jnp.dot(unit[0], unit[1], preferred_element_type=jnp.float32)
+
+    def finish(unit, scores):
+        top = jnp.max(scores, axis=0, keepdims=True)
+        weights = jnp.exp2((scores - top) * factor).astype(jnp.bfloat16)
+        sums = jnp.dot(unit[2], weights, preferred_element_type=jnp.float32)
+        attended_ref[unit[3] : unit[3] + HEAD, unit[4] : unit[4] + QUERY_TILE] = (
+            sums[:HEAD] / sums[HEAD : HEAD + 1]
+        ).astype(jnp.bfloat16)
+
+    ahead = score(units[0])
+    for i, unit in enumerate(units):
+        now, ahead = ahead, (score(units[i + 1]) if i + 1 < len(units) else None)
+        finish(unit, now)
+    out_weight = jnp.concatenate([out_a[...], out_b[...]], axis=0)
+    added = lax.dot_general(
+        attended_ref[...], out_weight, (((0,), (0,)), ((), ())), preferred_element_type=jnp.float32
     )
     hstream = (current.astype(jnp.float32) + added).astype(jnp.bfloat16)
     normed_two = layer_norm(hstream.astype(jnp.float32), gain_m[...]).astype(jnp.bfloat16)
@@ -167,8 +164,7 @@
         out_specs=[whole, whole],
         out_shape=[half, half],
         scratch_shapes=[
-            pltpu.VMEM((2, WIN, 3 * HALF), jnp.bfloat16),
-            pltpu.VMEM((2, WIN, HALF), jnp.bfloat16),
+            pltpu.VMEM((D, WIN), jnp.bfloat16),
         ],
         compiler_params=pltpu.CompilerParams(vmem_limit_bytes=VMEM),
         cost_estimate=pl.CostEstimate(

time: 145 us -> 128 us (0.88)
  Pallas kernels: 46.5 us -> 29.3 us
    pallas_call x6, Pallas kernels: 24.2 us -> 12.5 us  [pick(): pl.pallas_call(pick_kernel, grid=(steps,), in_specs=[pl.BlockSpec((1, 1,...]
    pallas_call x2, Pallas kernels: 22.3 us -> 16.8 us  [window_block(): pl.pallas_call(block_kernel, in_specs=[pl.BlockSpec(memory_space=pltpu.SM...]
  transfers between devices with their start and end apart: 10 -> 10, of which waited for: 4 -> 4; matrix products, arithmetic and copies ran while one was open for 7% -> 8% of each run, Pallas kernels for 5% -> 3%
where the time goes in v2:
time: 128 us; the launch traced here: 127 us
  waiting for transfers between devices  54.3 us (42%)
  starting transfers between devices  29.5 us (23%)
  Pallas kernels  29.3 us (23%)
  local copies, waits for them, and re-layouts  12.2 us (10%)
  other arithmetic  1.34 us (1%)
    all_to_all x2, waiting for transfers between devices, shards(): lax.all_to_all(picked.reshape(-1, 32, HALF), 'pts', split_axis=0, concat_...  51.6 us
    all_to_all x2, starting transfers between devices, shards(): lax.all_to_all(picked.reshape(-1, 32, HALF), 'pts', split_axis=0, concat_...  23 us
    pallas_call x2, Pallas kernels, window_block(): pl.pallas_call(block_kernel, in_specs=[pl.BlockSpec(memory_space=pltpu.SM...  16.8 us
    pallas_call x6, Pallas kernels, pick(): pl.pallas_call(pick_kernel, grid=(steps,), in_specs=[pl.BlockSpec((1, 1,...  12.5 us
    squeeze x9, local copies, waits for them, and re-layouts, shards(): weights += [own[layer], other[layer]]  6.93 us
    ppermute x8, starting transfers between devices, swap(): return lax.ppermute(value, 'ch', SWAP)  6.53 us
    ppermute x8, waiting for transfers between devices, swap(): return lax.ppermute(value, 'ch', SWAP)  2.69 us
  transfers between devices with their start and end apart: 10, of which 4 were waited for; matrix products, arithmetic and copies ran while one was open for 8% of the time, Pallas kernels for 3%

profile of v2, /device:TPU:1, one launch (start us, length us, event | category | flops | bytes accessed | tf_op | source)
XLA Modules:
  0.0 127.0 jit_solution(5598803558560402862)
XLA Ops:
  0.0 1.3 %slice_maximum_fusion = (s32[1,128,32]{1,2,0:T(8,128)S(1)}, s32[1,128,32]{1,2,0:T(8,128)}) fusion(s32[2,128,32]{1,2,0:T(8,128)} %param.10, s32[]{:T(128)S(6)} %mul.7), kind=kLoop, calls=%fused_computation.14 | loop fusion | flops 12288 | bytes 65540 | tf_op jit(solution)/shard_map/max | solution.py:195
  1.3 0.1 copy.16
  1.4 0.1 max.27.index_ref
  1.5 0.0 copy-start.4
  1.5 1.0 copy-done.4
  2.6 3.5 %shard_map.91 = bf16[4096,128]{1,0:T(8,128)(2,1)} custom-call(s32[2,1,2048]{2,1,0:T(1,128)S(1)} %max.27.index_ref, bf16[2048,128]{1,0:T(8,128)(2,1)S(1)} %copy-done.4), custom_call_target="tpu_custom_call" | custom-call | flops 4294967296 | bytes 1572864 | tf_op jit(solution)/shard_map/pallas_call | solution.py:50
  6.1 16.5 %all-to-all-start = ((bf16[128,32,128]{2,1,0:T(8,128)(2,1)}), bf16[128,32,128]{2,1,0:T(8,128)(2,1)S(1)}, u32[]{:S(2)}, u32[]{:S(2)}) async-start(bf16[128,32,128]{2,1,0:T(8,128)(2,1)} %bitcast.3), calls=%async_computation | async-start | bytes 2097152 | tf_op jit(solution)/shard_map/all_to_all | solution.py:197
  22.6 0.0 copy-done.7
  22.6 0.2 copy.18
  22.8 0.0 copy-start.8
  22.8 0.0 copy-start.12
  22.8 0.0 copy-start.13
  22.8 0.2 copy.20
  23.0 1.0 collective-permute-start.1
  24.1 0.1 collective-permute-start.4
  24.2 0.4 collective-permute-start.3
  24.6 0.0 copy-done.8
  24.6 0.1 collective-permute-start.2
  24.7 0.0 copy-done.12
  24.7 0.0 copy-done.13
  24.7 0.6 fusion.1
  25.3 0.6 slice_bitcast_fusion.12
  25.9 0.7 fusion
  26.6 1.1 slice_bitcast_fusion.4
  27.7 0.0 copy-start.11
  27.7 1.1 slice_bitcast_fusion.5
  28.8 0.0 copy-done.11
  28.8 0.6 slice_reduce_fusion
  29.4 0.2 copy.21.qkv_a
  29.6 0.0 collective-permute-done.2
  29.6 0.7 slice_bitcast_fusion.10
  30.3 0.0 collective-permute-done.1
  30.3 1.1 slice_bitcast_fusion.8
  31.3 0.0 collective-permute-done.4
  31.4 1.1 slice_bitcast_fusion
  32.4 20.4 %all-to-all-done = bf16[128,32,128]{2,1,0:T(8,128)(2,1)S(1)} async-done(((bf16[128,32,128]{2,1,0:T(8,128)(2,1)}), bf16[128,32,128]{2,1,0:T(8,128)(2,1)S(1)}, u32[]{:S(2)}, u32[]{:S(2)}) %all-to-all-start) | async-done | bytes 1048608 | tf_op jit(solution)/shard_map/all_to_all | solution.py:197
  52.8 1.4 %shard_map.93 = bf16[1024,128]{1,0:T(8,128)(2,1)S(1)} custom-call(s32[1,1,1024]{2,1,0:T(1,128)S(1)} %get-tuple-element.35.index_ref, bf16[4096,128]{1,0:T(8,128)(2,1)S(1)} %bitcast.44), custom_call_target="tpu_custom_call" | custom-call | flops 2147483648 | bytes 1310720 | tf_op jit(solution)/shard_map/pallas_call | solution.py:50
  54.2 2.9 %collective-permute-start = (bf16[1024,128]{1,0:T(8,128)(2,1)S(1)}, bf16[1024,128]{1,0:T(8,128)(2,1)S(1)}, u32[]{:S(2)}, u32[]{:S(2)}) collective-permute-start(bf16[1024,128]{1,0:T(8,128)(2,1)S(1)} %shard_map.93), channel_id=1, source_target_pairs={{0,1},{1,0},{2,3},{3,2},{4,5},{5,4},{6,7},{7,6},{8,9},{9,8},{10,11... | collective-permute-start | bytes 786440 | tf_op jit(solution)/shard_map/ppermute | solution.py:21
  57.1 0.0 collective-permute-done.3
  57.1 1.1 slice_bitcast_fusion.1
  58.2 0.0 copy-start.1
  58.2 1.4 %shard_map.92.mine_ref = bf16[1024,128]{1,0:T(8,128)(2,1)S(1)} custom-call(s32[1,1,1024]{2,1,0:T(1,128)S(1)} %get-tuple-element.36.index_ref, bf16[4096,128]{1,0:T(8,128)(2,1)S(1)} %bitcast.45), custom_call_target="tpu_custom_call" | custom-call | flops 2147483648 | bytes 1310720 | tf_op jit(solution)/shard_map/pallas_call | solution.py:50
  59.6 0.0 collective-permute-done.got_ref
  59.6 0.6 copy-done.3
  60.2 8.4 %shard_map.94 = (bf16[1024,128]{1,0:T(8,128)(2,1)S(1)}, bf16[1024,128]{1,0:T(8,128)(2,1)S(1)}) custom-call(s32[1]{0:T(128)} %bitcast.core_ref, bf16[1024,128]{1,0:T(8,128)(2,1)S(1)} %shard_map.92.mine_ref, bf16[1024,128]{1,0:T(8,128)(2,1)S(1)} %collective-permute-done.got_ref, bf16[256,384]{1,0:T(8,128)(2,1)S(1)} %copy.21.qkv_a, ...), custom_call_target="tpu_custom_call" | custom-call | flops 6000000000 | bytes 3000000 | tf_op jit(solution)/shard_map/pallas_call | solution.py:161
  68.6 0.1 collective-permute-start.5
  68.8 0.1 copy.15
  68.9 0.1 xor.19.index_ref
  69.0 1.3 %collective-permute-done.5.refs_1_ = bf16[1024,128]{1,0:T(8,128)(2,1)S(1)} collective-permute-done((bf16[1024,128]{1,0:T(8,128)(2,1)S(1)}, bf16[1024,128]{1,0:T(8,128)(2,1)S(1)}, u32[]{:S(2)}, u32[]{:S(2)}) %collective-permute-start.5) | collective-permute-done | bytes 262176 | tf_op jit(solution)/shard_map/ppermute | solution.py:21
  70.3 3.5 %shard_map.95 = bf16[4096,128]{1,0:T(8,128)(2,1)} custom-call(s32[2,1,2048]{2,1,0:T(1,128)S(1)} %xor.19.index_ref, bf16[1024,128]{1,0:T(8,128)(2,1)S(1)} %get-tuple-element.9.refs_0_, bf16[1024,128]{1,0:T(8,128)(2,1)S(1)} %collective-permute-done.5.refs_1_), custom_call_target="tpu_custom_call" | custom-call | flops 4294967296 | bytes 1572864 | tf_op jit(solution)/shard_map/pallas_call | solution.py:50
  73.8 6.5 %all-to-all-start.1 = ((bf16[128,32,128]{2,1,0:T(8,128)(2,1)}), bf16[128,32,128]{2,1,0:T(8,128)(2,1)S(1)}, u32[]{:S(2)}, u32[]{:S(2)}) async-start(bf16[128,32,128]{2,1,0:T(8,128)(2,1)} %bitcast.15), calls=%async_computation.1 | async-start | bytes 2097152 | tf_op jit(solution)/shard_map/all_to_all | solution.py:197
  80.4 31.2 %all-to-all-done.1 = bf16[128,32,128]{2,1,0:T(8,128)(2,1)S(1)} async-done(((bf16[128,32,128]{2,1,0:T(8,128)(2,1)}), bf16[128,32,128]{2,1,0:T(8,128)(2,1)S(1)}, u32[]{:S(2)}, u32[]{:S(2)}) %all-to-all-start.1) | async-done | bytes 1048608 | tf_op jit(solution)/shard_map/all_to_all | solution.py:197
  111.6 1.4 %shard_map.97 = bf16[1024,128]{1,0:T(8,128)(2,1)S(1)} custom-call(s32[1,1,1024]{2,1,0:T(1,128)S(1)} %get-tuple-element.33.index_ref, bf16[4096,128]{1,0:T(8,128)(2,1)S(1)} %bitcast.46), custom_call_target="tpu_custom_call" | custom-call | flops 2147483648 | bytes 1310720 | tf_op jit(solution)/shard_map/pallas_call | solution.py:50
  113.0 1.7 %collective-permute-start.6 = (bf16[1024,128]{1,0:T(8,128)(2,1)S(1)}, bf16[1024,128]{1,0:T(8,128)(2,1)S(1)}, u32[]{:S(2)}, u32[]{:S(2)}) collective-permute-start(bf16[1024,128]{1,0:T(8,128)(2,1)S(1)} %shard_map.97), channel_id=1, source_target_pairs={{0,1},{1,0},{2,3},{3,2},{4,5},{5,4},{6,7},{7,6},{8,9},{9,8},{10,11... | collective-permute-start | bytes 786440 | tf_op jit(solution)/shard_map/ppermute | solution.py:21
  114.7 0.2 copy.24.qkv_a
  114.8 0.0 copy-start
  114.9 1.4 %shard_map.96.mine_ref = bf16[1024,128]{1,0:T(8,128)(2,1)S(1)} custom-call(s32[1,1,1024]{2,1,0:T(1,128)S(1)} %get-tuple-element.34.index_ref, bf16[4096,128]{1,0:T(8,128)(2,1)S(1)} %bitcast.47), custom_call_target="tpu_custom_call" | custom-call | flops 2147483648 | bytes 1310720 | tf_op jit(solution)/shard_map/pallas_call | solution.py:50
  116.2 0.0 collective-permute-done.6.got_ref
  116.2 8.4 %shard_map.98 = (bf16[1024,128]{1,0:T(8,128)(2,1)S(1)}, bf16[1024,128]{1,0:T(8,128)(2,1)S(1)}) custom-call(s32[1]{0:T(128)} %bitcast.core_ref, bf16[1024,128]{1,0:T(8,128)(2,1)S(1)} %shard_map.96.mine_ref, bf16[1024,128]{1,0:T(8,128)(2,1)S(1)} %collective-permute-done.6.got_ref, bf16[256,384]{1,0:T(8,128)(2,1)S(1)} %copy.24.qkv_a, ...), custom_call_target="tpu_custom_call" | custom-call | flops 6000000000 | bytes 3000000 | tf_op jit(solution)/shard_map/pallas_call | solution.py:161
  124.7 0.1 collective-permute-start.7
  124.8 0.1 broadcast_in_dim.3
  124.9 0.0 copy-start.6
  124.9 1.4 %collective-permute-done.7 = bf16[1024,128]{1,0:T(8,128)(2,1)S(1)} collective-permute-done((bf16[1024,128]{1,0:T(8,128)(2,1)S(1)}, bf16[1024,128]{1,0:T(8,128)(2,1)S(1)}, u32[]{:S(2)}, u32[]{:S(2)}) %collective-permute-start.7) | collective-permute-done | bytes 262176 | tf_op jit(solution)/shard_map/ppermute | solution.py:21
  126.3 0.7 constant_dynamic-update-slice_fusion
  (18 shorter events, 0.1 us)
Async XLA Ops:
  1.5 1.0 copy-start.4
  6.1 16.5 %copy-start.7 = (bf16[2,256,3,128]{3,1,2,0:T(8,128)(2,1)S(1)}, bf16[2,256,3,128]{3,1,2,0:T(8,128)(2,1)}, u32[]{:S(2)}) copy-start(bf16[2,256,3,128]{3,1,2,0:T(8,128)(2,1)} %param.12) | copy-start | bytes 1179652
  6.1 46.7 %all-to-all-start = ((bf16[128,32,128]{2,1,0:T(8,128)(2,1)}), bf16[128,32,128]{2,1,0:T(8,128)(2,1)S(1)}, u32[]{:S(2)}, u32[]{:S(2)}) async-start(bf16[128,32,128]{2,1,0:T(8,128)(2,1)} %bitcast.3), calls=%async_computation | async-start | bytes 2097152 | tf_op jit(solution)/shard_map/all_to_all | solution.py:197
  22.8 1.8 %copy-start.8 = (bf16[2,128,256]{2,1,0:T(8,128)(2,1)S(1)}, bf16[2,128,256]{2,1,0:T(8,128)(2,1)}, u32[]{:S(2)}) copy-start(bf16[2,128,256]{2,1,0:T(8,128)(2,1)} %param.13) | copy-start | bytes 393220
  22.8 1.9 %copy-start.12 = (f32[2,256]{1,0:T(2,128)S(1)}, f32[2,256]{1,0:T(2,128)}, u32[]{:S(2)}) copy-start(f32[2,256]{1,0:T(2,128)} %param.17) | copy-start | bytes 6148
  22.8 1.9 %copy-start.13 = (f32[2,256]{1,0:T(2,128)S(1)}, f32[2,256]{1,0:T(2,128)}, u32[]{:S(2)}) copy-start(f32[2,256]{1,0:T(2,128)} %param.16) | copy-start | bytes 6148
  23.0 7.2 %collective-permute-start.1 = (bf16[2,256,384]{2,1,0:T(8,128)(2,1)S(1)}, bf16[2,256,384]{2,1,0:T(8,128)(2,1)}, u32[]{:S(2)}, u32[]{:S(2)}) collective-permute-start(bf16[2,256,384]{2,1,0:T(8,128)(2,1)S(1)} %copy.20), channel_id=1, source_target_pairs={{0,1},{1,0},{2,3},{3,2},{4,5},{5,4},{6,7},{7,6},{8,9},{9,8},{10,11... | collective-permute-start | bytes 1179656 | tf_op jit(solution)/shard_map/ppermute | solution.py:21
  24.1 7.3 %collective-permute-start.4 = (bf16[2,512,256]{2,1,0:T(8,128)(2,1)}, bf16[2,512,256]{2,1,0:T(8,128)(2,1)}, u32[]{:S(2)}, u32[]{:S(2)}) collective-permute-start(bf16[2,512,256]{2,1,0:T(8,128)(2,1)} %param.15), channel_id=1, source_target_pairs={{0,1},{1,0},{2,3},{3,2},{4,5},{5,4},{6,7},{7,6},{8,9},{9,8},{10,11... | collective-permute-start | bytes 1572872 | tf_op jit(solution)/shard_map/ppermute | solution.py:21
  24.2 32.9 %collective-permute-start.3 = (bf16[2,256,512]{2,1,0:T(8,128)(2,1)}, bf16[2,256,512]{2,1,0:T(8,128)(2,1)}, u32[]{:S(2)}, u32[]{:S(2)}) collective-permute-start(bf16[2,256,512]{2,1,0:T(8,128)(2,1)} %param.14), channel_id=1, source_target_pairs={{0,1},{1,0},{2,3},{3,2},{4,5},{5,4},{6,7},{7,6},{8,9},{9,8},{10,11... | collective-permute-start | bytes 1572872 | tf_op jit(solution)/shard_map/ppermute | solution.py:21
  24.6 5.0 %collective-permute-start.2 = (bf16[2,128,256]{2,1,0:T(8,128)(2,1)S(1)}, bf16[2,128,256]{2,1,0:T(8,128)(2,1)S(1)}, u32[]{:S(2)}, u32[]{:S(2)}) collective-permute-start(bf16[2,128,256]{2,1,0:T(8,128)(2,1)S(1)} %copy-done.8), channel_id=1, source_target_pairs={{0,1},{1,0},{2,3},{3,2},{4,5},{5,4},{6,7},{7,6},{8,9},{9,8},{10,11... | collective-permute-start | bytes 393224 | tf_op jit(solution)/shard_map/ppermute | solution.py:21
  27.7 1.1 copy-start.11
  54.2 5.4 %collective-permute-start = (bf16[1024,128]{1,0:T(8,128)(2,1)S(1)}, bf16[1024,128]{1,0:T(8,128)(2,1)S(1)}, u32[]{:S(2)}, u32[]{:S(2)}) collective-permute-start(bf16[1024,128]{1,0:T(8,128)(2,1)S(1)} %shard_map.93), channel_id=1, source_target_pairs={{0,1},{1,0},{2,3},{3,2},{4,5},{5,4},{6,7},{7,6},{8,9},{9,8},{10,11... | collective-permute-start | bytes 786440 | tf_op jit(solution)/shard_map/ppermute | solution.py:21
  58.2 1.4 %copy-start.1 = (bf16[128,256]{1,0:T(8,128)(2,1)S(1)}, bf16[128,256]{1,0:T(8,128)(2,1)}, u32[]{:S(2)}) copy-start(bf16[128,256]{1,0:T(8,128)(2,1)} %get-tuple-element.30.out_a) | copy-start | bytes 196612
  58.2 1.4 %copy-start.2 = (bf16[128,256]{1,0:T(8,128)(2,1)S(1)}, bf16[128,256]{1,0:T(8,128)(2,1)}, u32[]{:S(2)}) copy-start(bf16[128,256]{1,0:T(8,128)(2,1)} %get-tuple-element.28.out_b) | copy-start | bytes 196612
  59.6 0.7 copy-start.3
  60.2 8.5 %copy-start.9 = (s32[1,128,32]{1,2,0:T(8,128)S(1)}, s32[1,128,32]{1,2,0:T(8,128)}, u32[]{:S(2)}) copy-start(s32[1,128,32]{1,2,0:T(8,128)} %get-tuple-element.32) | copy-start | bytes 49156
  68.6 1.6 %collective-permute-start.5 = (bf16[1024,128]{1,0:T(8,128)(2,1)S(1)}, bf16[1024,128]{1,0:T(8,128)(2,1)S(1)}, u32[]{:S(2)}, u32[]{:S(2)}) collective-permute-start(bf16[1024,128]{1,0:T(8,128)(2,1)S(1)} %get-tuple-element.10), channel_id=1, source_target_pairs={{0,1},{1,0},{2,3},{3,2},{4,5},{5,4},{6,7},{7,6},{8,9},{9,8},{10,11... | collective-permute-start | bytes 786440 | tf_op jit(solution)/shard_map/ppermute | solution.py:21
  73.8 6.6 %copy-start.10 = (s32[2048]{0:T(1024)S(1)}, s32[2048]{0:T(1024)}, u32[]{:S(2)}) copy-start(s32[2048]{0:T(1024)} %get-tuple-element.14) | copy-start | bytes 24580
  73.8 37.8 %all-to-all-start.1 = ((bf16[128,32,128]{2,1,0:T(8,128)(2,1)}), bf16[128,32,128]{2,1,0:T(8,128)(2,1)S(1)}, u32[]{:S(2)}, u32[]{:S(2)}) async-start(bf16[128,32,128]{2,1,0:T(8,128)(2,1)} %bitcast.15), calls=%async_computation.1 | async-start | bytes 2097152 | tf_op jit(solution)/shard_map/all_to_all | solution.py:197
  111.6 3.1 %copy-start.5 = (bf16[1,256,3,128]{1,3,2,0:T(8,128)(2,1)S(1)}, bf16[1,256,3,128]{1,3,2,0:T(8,128)(2,1)}, u32[]{:S(2)}) copy-start(bf16[1,256,3,128]{1,3,2,0:T(8,128)(2,1)} %get-tuple-element.25) | copy-start | bytes 589828
  113.0 3.3 %collective-permute-start.6 = (bf16[1024,128]{1,0:T(8,128)(2,1)S(1)}, bf16[1024,128]{1,0:T(8,128)(2,1)S(1)}, u32[]{:S(2)}, u32[]{:S(2)}) collective-permute-start(bf16[1024,128]{1,0:T(8,128)(2,1)S(1)} %shard_map.97), channel_id=1, source_target_pairs={{0,1},{1,0},{2,3},{3,2},{4,5},{5,4},{6,7},{7,6},{8,9},{9,8},{10,11... | collective-permute-start | bytes 786440 | tf_op jit(solution)/shard_map/ppermute | solution.py:21
  114.8 1.4 %copy-start = (bf16[128,256]{1,0:T(8,128)(2,1)S(1)}, bf16[128,256]{1,0:T(8,128)(2,1)}, u32[]{:S(2)}) copy-start(bf16[128,256]{1,0:T(8,128)(2,1)} %get-tuple-element.27.out_b) | copy-start | bytes 196612
  124.7 1.6 %collective-permute-start.7 = (bf16[1024,128]{1,0:T(8,128)(2,1)S(1)}, bf16[1024,128]{1,0:T(8,128)(2,1)S(1)}, u32[]{:S(2)}, u32[]{:S(2)}) collective-permute-start(bf16[1024,128]{1,0:T(8,128)(2,1)S(1)} %get-tuple-element.12), channel_id=1, source_target_pairs={{0,1},{1,0},{2,3},{3,2},{4,5},{5,4},{6,7},{7,6},{8,9},{9,8},{10,11... | collective-permute-start | bytes 786440 | tf_op jit(solution)/shard_map/ppermute | solution.py:21
  124.9 1.4 %copy-start.6 = (bf16[2048,128]{1,0:T(8,128)(2,1)}, bf16[2048,128]{1,0:T(8,128)(2,1)S(1)}, u32[]{:S(2)}) copy-start(bf16[2048,128]{1,0:T(8,128)(2,1)S(1)} %constant_dynamic-update-slice_fusion.1) | copy-start | bytes 1572868

commit v3 on v2

--- a/solution.py
+++ b/solution.py
@@ -1,3 +1,4 @@
+import functools
 import math
 
 import jax
@@ -21,9 +22,12 @@
     return lax.ppermute(value, "ch", SWAP)
 
 
-def pick_kernel(index_ref, *refs):
+def pick_kernel(flips, core_ref, index_ref, *refs):
     sources, out_ref = refs[:-1], refs[-1]
-    index = index_ref[0].astype(jnp.int16)
+    index = index_ref[0, 0]
+    if flips:
+        index = jnp.bitwise_xor(index, core_ref[0] * WIN)
+    index = index.astype(jnp.int16)
     total = None
     start = 0
     for source in sources:
@@ -42,23 +46,31 @@
     out_ref[...] = total.T.astype(jnp.bfloat16)
 
 
-def pick(index, *sources):
-    count = index.size
+def pick(core, table, layer, part, *sources, flips=False):
+    tile = table.shape[3]
+    steps = table.shape[1] if part is None else 1
     depth = sum(source.shape[0] for source in sources)
-    tile = min(count, 2048)
-    steps = count // tile
+
+    def block(i, word):
+        return (layer, i if part is None else part(word[0]), 0, 0)
+
     return pl.pallas_call(
-        pick_kernel,
-        grid=(steps,),
-        in_specs=[pl.BlockSpec((1, 1, tile), lambda i: (i, 0, 0))]
-        + [pl.BlockSpec(source.shape, lambda i: (0, 0)) for source in sources],
-        out_specs=pl.BlockSpec((tile, HALF), lambda i: (i, 0)),
-        out_shape=jax.ShapeDtypeStruct((count, HALF), jnp.bfloat16),
+        functools.partial(pick_kernel, flips),
+        grid_spec=pltpu.PrefetchScalarGridSpec(
+            num_scalar_prefetch=1,
+            grid=(steps,),
+            in_specs=[pl.BlockSpec((1, 1, 1, tile), block)]
+            + [pl.BlockSpec(source.shape, lambda i, word: (0, 0)) for source in sources],
+            out_specs=pl.BlockSpec((tile, HALF), lambda i, word: (i, 0)),
+        ),
+        out_shape=jax.ShapeDtypeStruct((steps * tile, HALF), jnp.bfloat16),
         compiler_params=pltpu.CompilerParams(vmem_limit_bytes=VMEM),
         cost_estimate=pl.CostEstimate(
-            flops=4 * count * depth * HALF, bytes_accessed=(count + depth) * 256, transcendentals=0
+            flops=4 * steps * tile * depth * HALF,
+            bytes_accessed=(steps * tile + depth) * 256,
+            transcendentals=0,
         ),
-    )(index.reshape(steps, 1, tile), *sources)
+    )(core, table, *sources)
 
 
 def layer_norm(values, gain):
@@ -75,6 +87,7 @@
 
 
 def block_kernel(
+    layer,
     core_ref,
     mine_ref,
     got_ref,
@@ -97,19 +110,19 @@
     low = jnp.where(first, mine, got)
     high = jnp.where(first, got, mine)
     current = jnp.concatenate([low, high], axis=1)
-    normed = layer_norm(current.astype(jnp.float32), gain_a[...]).astype(jnp.bfloat16)
+    normed = layer_norm(current.astype(jnp.float32), gain_a[layer : layer + 1]).astype(jnp.bfloat16)
     factor = math.log2(math.e) / math.sqrt(HEAD)
     over_rows = (((0,), (1,)), ((), ()))
     units = []
     for n, weight in enumerate((qkv_a, qkv_b)):
         queries = lax.dot_general(
-            weight[:, :HALF], normed, over_rows, preferred_element_type=jnp.float32
+            weight[layer, 0], normed, over_rows, preferred_element_type=jnp.float32
         ).astype(jnp.bfloat16)
         keys = jnp.dot(
-            normed, weight[:, HALF : 2 * HALF], preferred_element_type=jnp.float32
+            normed, weight[layer, 1], preferred_element_type=jnp.float32
         ).astype(jnp.bfloat16)
         values = lax.dot_general(
-            weight[:, 2 * HALF :], normed, over_rows, preferred_element_type=jnp.float32
+            weight[layer, 2], normed, over_rows, preferred_element_type=jnp.float32
         ).astype(jnp.bfloat16)
         zero = jnp.zeros((HEAD, WIN), jnp.bfloat16)
         ones = jnp.ones((16, WIN), jnp.bfloat16)
@@ -137,32 +150,39 @@
     for i, unit in enumerate(units):
         now, ahead = ahead, (score(units[i + 1]) if i + 1 < len(units) else None)
         finish(unit, now)
-    out_weight = jnp.concatenate([out_a[...], out_b[...]], axis=0)
+    out_weight = jnp.concatenate([out_a[layer], out_b[layer]], axis=0)
     added = lax.dot_general(
         attended_ref[...], out_weight, (((0,), (0,)), ((), ())), preferred_element_type=jnp.float32
     )
     hstream = (current.astype(jnp.float32) + added).astype(jnp.bfloat16)
-    normed_two = layer_norm(hstream.astype(jnp.float32), gain_m[...]).astype(jnp.bfloat16)
+    normed_two = layer_norm(hstream.astype(jnp.float32), gain_m[layer : layer + 1]).astype(jnp.bfloat16)
     result = hstream.astype(jnp.float32)
     for up, down in ((up_a, down_a), (up_b, down_b)):
-        hidden = gelu(jnp.dot(normed_two, up[...], preferred_element_type=jnp.float32))
+        hidden = gelu(jnp.dot(normed_two, up[layer], preferred_element_type=jnp.float32))
         result = result + jnp.dot(
-            hidden.astype(jnp.bfloat16), down[...], preferred_element_type=jnp.float32
+            hidden.astype(jnp.bfloat16), down[layer], preferred_element_type=jnp.float32
         )
     result = result.astype(jnp.bfloat16)
     low, high = result[:, :HALF], result[:, HALF:]
-    keep_ref[...] = jnp.where(first, low, high)
+    kept = jnp.where(first, low, high)
+    if keep_ref.shape[0] == WIN:
+        keep_ref[...] = kept
+    else:
+        keep_ref[pl.ds(pl.multiple_of(core_ref[0] * WIN, WIN), WIN), :] = kept
     give_ref[...] = jnp.where(first, high, low)
 
 
-def window_block(core, mine, got, weights, gain_attn, gain_mlp):
-    half = jax.ShapeDtypeStruct((WIN, HALF), jnp.bfloat16)
+def window_block(layer, core, mine, got, weights, gain_attn, gain_mlp):
+    kept = WIN if layer + 1 < BLOCKS else 2 * WIN
     whole = pl.BlockSpec(memory_space=pltpu.VMEM)
     return pl.pallas_call(
-        block_kernel,
+        functools.partial(block_kernel, layer),
         in_specs=[pl.BlockSpec(memory_space=pltpu.SMEM)] + [whole] * (4 + len(weights)),
         out_specs=[whole, whole],
-        out_shape=[half, half],
+        out_shape=[
+            jax.ShapeDtypeStruct((kept, HALF), jnp.bfloat16),
+            jax.ShapeDtypeStruct((WIN, HALF), jnp.bfloat16),
+        ],
         scratch_shapes=[
             pltpu.VMEM((D, WIN), jnp.bfloat16),
         ],
@@ -184,36 +204,25 @@
     gain_attn,
     gain_mlp,
 ):
-    core = lax.axis_index("ch")
-    core_word = core.astype(jnp.int32).reshape(1)
-    qkv = qkv_weight.reshape(BLOCKS, D, 3 * HALF)
-    owned = (qkv, out_weight, up_weight, down_weight)
-    fetched = tuple(swap(array) for array in owned)
+    core = lax.axis_index("ch").astype(jnp.int32)
+    word = core.reshape(1)
+    weights = []
+    for array in (qkv_weight.transpose(0, 2, 1, 3), out_weight, up_weight, down_weight):
+        weights += [array, swap(array)]
+    send_table = send_rows.reshape(BLOCKS, 2, 1, -1)
+    recv_table = recv_slots.reshape(BLOCKS, 2, 1, WIN)
     sources = (stream,)
-    flip = 0
     for layer in range(BLOCKS):
-        index = jnp.maximum(send_rows[layer], 0) ^ flip
-        picked = pick(index, *sources)
+        picked = pick(word, send_table, layer, None, *sources, flips=layer > 0)
         moved = lax.all_to_all(
             picked.reshape(-1, 32, HALF), "pts", split_axis=0, concat_axis=0, tiled=True
         ).reshape(-1, HALF)
-        slots = recv_slots[layer].reshape(2, WIN)
-        theirs = lax.dynamic_index_in_dim(slots, 1 - core, 0, keepdims=False)
-        ours = lax.dynamic_index_in_dim(slots, core, 0, keepdims=False)
-        got = swap(pick(theirs, moved))
-        mine = pick(ours, moved)
-        weights = []
-        for own, other in zip(owned, fetched):
-            weights += [own[layer], other[layer]]
-        keep, give = window_block(
-            core_word, mine, got, weights, gain_attn[layer : layer + 1], gain_mlp[layer : layer + 1]
-        )
+        got = swap(pick(word, recv_table, layer, lambda own: 1 - own, moved))
+        mine = pick(word, recv_table, layer, lambda own: own, moved)
+        keep, give = window_block(layer, word, mine, got, weights, gain_attn, gain_mlp)
         back = swap(give)
         sources = (keep, back)
-        flip = core * WIN
-    result = jnp.zeros((2 * WIN, HALF), jnp.bfloat16)
-    result = lax.dynamic_update_slice(result, keep, (core * WIN, 0))
-    return lax.dynamic_update_slice(result, back, ((1 - core) * WIN, 0))
+    return lax.dynamic_update_slice(keep, back, ((1 - core) * WIN, 0))
 
 
 def solution(mesh):

time: 128 us -> 126 us (0.984)
  blocking collectives: 0 us -> 37 us
  waiting for transfers between devices: 54.3 us -> 31.4 us
  local copies, waits for them, and re-layouts: 12.2 us -> 2.79 us
  starting transfers between devices: 29.5 us -> 23.2 us
  Pallas kernels: 29.3 us -> 31.3 us
  other arithmetic: 1.34 us -> 0 us
    all_to_all x0 -> x1, blocking collectives: none -> 37 us  [shards(): lax.all_to_all(picked.reshape(-1, 32, HALF), 'pts', split_axis=0, concat_...]
    all_to_all x2 -> x1, waiting for transfers between devices: 51.6 us -> 28.7 us  [shards(): lax.all_to_all(picked.reshape(-1, 32, HALF), 'pts', split_axis=0, concat_...]
    squeeze x9 -> x0, local copies, waits for them, and re-layouts: 6.93 us -> none  [shards(): weights += [own[layer], other[layer]]]
    all_to_all x2 -> x1, starting transfers between devices: 23 us -> 16.5 us  [shards(): lax.all_to_all(picked.reshape(-1, 32, HALF), 'pts', split_axis=0, concat_...]
    pallas_call x8, Pallas kernels: 29.3 us -> 31.3 us  [the longest x2 19.7 us: window_block(): pl.pallas_call(functools.partial(block_kernel, layer), in_specs=[pl.Block...]
    slice x3 -> x0, local copies, waits for them, and re-layouts: 1.9 us -> none  [the longest x1 0.7 us: shards(): weights += [own[layer], other[layer]]]
    max x1 -> x0, other arithmetic: 1.34 us -> none  [shards(): index = jnp.maximum(send_rows[layer], 0) ^ flip]
  transfers between devices with their start and end apart: 10 -> 9, of which waited for: 4 -> 3; matrix products, arithmetic and copies ran while one was open for 8% -> 0% of each run, Pallas kernels for 3% -> 3%
where the time goes in v3:
time: 126 us
  blocking collectives  37 us (29%)
  waiting for transfers between devices  31.4 us (25%)
  Pallas kernels  31.3 us (25%)
  starting transfers between devices  23.2 us (18%)
  local copies, waits for them, and re-layouts  2.79 us (2%)
    all_to_all x1, blocking collectives, shards(): lax.all_to_all(picked.reshape(-1, 32, HALF), 'pts', split_axis=0, concat_...  37 us
    all_to_all x1, waiting for transfers between devices, shards(): lax.all_to_all(picked.reshape(-1, 32, HALF), 'pts', split_axis=0, concat_...  28.7 us
    pallas_call x2, Pallas kernels, window_block(): pl.pallas_call(functools.partial(block_kernel, layer), in_specs=[pl.Block...  19.7 us
    all_to_all x1, starting transfers between devices, shards(): lax.all_to_all(picked.reshape(-1, 32, HALF), 'pts', split_axis=0, concat_...  16.5 us
    pallas_call x6, Pallas kernels, pick(): pl.pallas_call(functools.partial(pick_kernel, flips), grid_spec=pltpu.Pre...  11.7 us
    ppermute x8, starting transfers between devices, swap(): return lax.ppermute(value, 'ch', SWAP)  6.74 us
    ppermute x8, waiting for transfers between devices, swap(): return lax.ppermute(value, 'ch', SWAP)  2.7 us
  transfers between devices with their start and end apart: 9, of which 3 were waited for; matrix products, arithmetic and copies ran while one was open for 0% of the time, Pallas kernels for 3%

profile of v3, /device:TPU:1, one launch (start us, length us, event | category | flops | bytes accessed | tf_op | source)
XLA Modules:
  0.0 125.9 jit_solution(8827213771092141833)
XLA Ops:
  0.0 0.9 copy.11
  0.9 0.1 reshape.28.index_ref
  1.0 0.0 copy-start
  1.0 1.0 copy-done
  2.0 3.5 %shard_map.91 = bf16[4096,128]{1,0:T(8,128)(2,1)} custom-call(s32[1]{0:T(128)} %bitcast.core_ref, s32[2,2,1,2048]{3,2,1,0:T(1,128)S(1)} %reshape.28.index_ref, bf16[2048,128]{1,0:T(8,128)(2,1)S(1)} %copy-done), custom_call_target="tpu_custom_call" | custom-call | flops 4294967296 | bytes 1572864 | tf_op jit(solution)/shard_map/pallas_call | solution.py:57
  5.6 0.0 copy-start.1
  5.6 0.0 copy-start.2
  5.6 0.0 copy-start.7
  5.6 16.5 %all-to-all-start = ((bf16[128,32,128]{2,1,0:T(8,128)(2,1)}), bf16[128,32,128]{2,1,0:T(8,128)(2,1)S(1)}, u32[]{:S(2)}, u32[]{:S(2)}) async-start(bf16[128,32,128]{2,1,0:T(8,128)(2,1)} %bitcast.1), calls=%async_computation | async-start | bytes 2097152 | tf_op jit(solution)/shard_map/all_to_all | solution.py:217
  22.0 0.0 copy-done.1
  22.1 1.0 collective-permute-start.3
  23.1 0.0 copy-done.2
  23.1 0.1 collective-permute-start.4
  23.2 0.4 collective-permute-start.1
  23.6 0.0 copy-done.7
  23.6 28.7 %all-to-all-done = bf16[128,32,128]{2,1,0:T(8,128)(2,1)S(1)} async-done(((bf16[128,32,128]{2,1,0:T(8,128)(2,1)}), bf16[128,32,128]{2,1,0:T(8,128)(2,1)S(1)}, u32[]{:S(2)}, u32[]{:S(2)}) %all-to-all-start) | async-done | bytes 1048608 | tf_op jit(solution)/shard_map/all_to_all | solution.py:217
  52.3 0.0 copy-start.4
  52.3 1.4 %shard_map.93 = bf16[1024,128]{1,0:T(8,128)(2,1)S(1)} custom-call(s32[1]{0:T(128)} %bitcast.core_ref, s32[2,2,1,1024]{3,2,1,0:T(1,128)S(1)} %reshape.22.index_ref, bf16[4096,128]{1,0:T(8,128)(2,1)S(1)} %bitcast.6), custom_call_target="tpu_custom_call" | custom-call | flops 2147483648 | bytes 1310720 | tf_op jit(solution)/shard_map/pallas_call | solution.py:57
  53.7 0.0 copy-start.3
  53.7 0.0 copy-start.5
  53.7 0.0 copy-start.6
  53.7 2.7 %collective-permute-start = (bf16[1024,128]{1,0:T(8,128)(2,1)S(1)}, bf16[1024,128]{1,0:T(8,128)(2,1)S(1)}, u32[]{:S(2)}, u32[]{:S(2)}) collective-permute-start(bf16[1024,128]{1,0:T(8,128)(2,1)S(1)} %shard_map.93), channel_id=1, source_target_pairs={{0,1},{1,0},{2,3},{3,2},{4,5},{5,4},{6,7},{7,6},{8,9},{9,8},{10,11... | collective-permute-start | bytes 786440 | tf_op jit(solution)/shard_map/ppermute | solution.py:22
  56.4 0.0 copy-done.4
  56.4 0.3 collective-permute-start.2
  56.7 1.4 %shard_map.92.mine_ref = bf16[1024,128]{1,0:T(8,128)(2,1)S(1)} custom-call(s32[1]{0:T(128)} %bitcast.core_ref, s32[2,2,1,1024]{3,2,1,0:T(1,128)S(1)} %reshape.22.index_ref, bf16[4096,128]{1,0:T(8,128)(2,1)S(1)} %bitcast.7), custom_call_target="tpu_custom_call" | custom-call | flops 2147483648 | bytes 1310720 | tf_op jit(solution)/shard_map/pallas_call | solution.py:57
  58.1 0.0 collective-permute-done.2.out_b
  58.1 0.0 collective-permute-done.1.qkv_b
  58.1 0.0 collective-permute-done.3.up_b
  58.1 0.0 collective-permute-done.4.down_b
  58.1 0.0 collective-permute-done.got_ref
  58.1 0.0 copy-done.3
  58.1 0.0 copy-done.5
  58.1 0.0 copy-done.6
  58.2 9.4 %shard_map.94 = (bf16[1024,128]{1,0:T(8,128)(2,1)S(1)}, bf16[1024,128]{1,0:T(8,128)(2,1)S(1)}) custom-call(s32[1]{0:T(128)} %bitcast.core_ref, bf16[1024,128]{1,0:T(8,128)(2,1)S(1)} %shard_map.92.mine_ref, bf16[1024,128]{1,0:T(8,128)(2,1)S(1)} %collective-permute-done.got_ref, bf16[2,3,256,128]{3,2,1,0:T(8,128)(2,1)S(1)} %bitcast.12, ...), custom_call_target="tpu_custom_call" | custom-call | flops 6000000000 | bytes 3000000 | tf_op jit(solution)/shard_map/pallas_call | solution.py:178
  67.6 0.3 collective-permute-start.5
  67.9 1.3 %collective-permute-done.5.refs_1_ = bf16[1024,128]{1,0:T(8,128)(2,1)S(1)} collective-permute-done((bf16[1024,128]{1,0:T(8,128)(2,1)S(1)}, bf16[1024,128]{1,0:T(8,128)(2,1)S(1)}, u32[]{:S(2)}, u32[]{:S(2)}) %collective-permute-start.5) | collective-permute-done | bytes 262176 | tf_op jit(solution)/shard_map/ppermute | solution.py:22
  69.2 2.7 %shard_map.95 = bf16[4096,128]{1,0:T(8,128)(2,1)S(1)} custom-call(s32[1]{0:T(128)} %bitcast.core_ref, s32[2,2,1,2048]{3,2,1,0:T(1,128)S(1)} %reshape.28.index_ref, bf16[1024,128]{1,0:T(8,128)(2,1)S(1)} %get-tuple-element.9.refs_0_, bf16[1024,128]{1,0:T(8,128)(2,1)S(1)} %collective-permute-done.5.refs_1_), custom_call_target="tpu_custom_call" | custom-call | flops 4294967296 | bytes 1572864 | tf_op jit(solution)/shard_map/pallas_call | solution.py:57
  72.0 37.0 %all_to_all.10 = bf16[128,32,128]{2,1,0:T(8,128)(2,1)S(1)} all-to-all(bf16[128,32,128]{2,1,0:T(8,128)(2,1)S(1)} %bitcast.10), channel_id=1, replica_groups=mesh['pts'=128,'ch'=2] {'pts'}, dimensions={0} | all-to-all | bytes 2097152 | tf_op jit(solution)/shard_map/all_to_all | solution.py:217
  109.0 1.4 %shard_map.97 = bf16[1024,128]{1,0:T(8,128)(2,1)S(1)} custom-call(s32[1]{0:T(128)} %bitcast.core_ref, s32[2,2,1,1024]{3,2,1,0:T(1,128)S(1)} %reshape.22.index_ref, bf16[4096,128]{1,0:T(8,128)(2,1)S(1)} %bitcast.8), custom_call_target="tpu_custom_call" | custom-call | flops 2147483648 | bytes 1310720 | tf_op jit(solution)/shard_map/pallas_call | solution.py:57
  110.3 1.7 %collective-permute-start.6 = (bf16[1024,128]{1,0:T(8,128)(2,1)S(1)}, bf16[1024,128]{1,0:T(8,128)(2,1)S(1)}, u32[]{:S(2)}, u32[]{:S(2)}) collective-permute-start(bf16[1024,128]{1,0:T(8,128)(2,1)S(1)} %shard_map.97), channel_id=1, source_target_pairs={{0,1},{1,0},{2,3},{3,2},{4,5},{5,4},{6,7},{7,6},{8,9},{9,8},{10,11... | collective-permute-start | bytes 786440 | tf_op jit(solution)/shard_map/ppermute | solution.py:22
  112.0 1.4 %shard_map.96.mine_ref = bf16[1024,128]{1,0:T(8,128)(2,1)S(1)} custom-call(s32[1]{0:T(128)} %bitcast.core_ref, s32[2,2,1,1024]{3,2,1,0:T(1,128)S(1)} %reshape.22.index_ref, bf16[4096,128]{1,0:T(8,128)(2,1)S(1)} %bitcast.9), custom_call_target="tpu_custom_call" | custom-call | flops 2147483648 | bytes 1310720 | tf_op jit(solution)/shard_map/pallas_call | solution.py:57
  113.4 0.0 collective-permute-done.6.got_ref
  113.4 10.2 %shard_map.98 = (bf16[2048,128]{1,0:T(8,128)(2,1)}, bf16[1024,128]{1,0:T(8,128)(2,1)S(1)}) custom-call(s32[1]{0:T(128)} %bitcast.core_ref, bf16[1024,128]{1,0:T(8,128)(2,1)S(1)} %shard_map.96.mine_ref, bf16[1024,128]{1,0:T(8,128)(2,1)S(1)} %collective-permute-done.6.got_ref, bf16[2,3,256,128]{3,2,1,0:T(8,128)(2,1)S(1)} %bitcast.13, ...), custom_call_target="tpu_custom_call" | custom-call | flops 6000000000 | bytes 3000000 | tf_op jit(solution)/shard_map/pallas_call | solution.py:178
  123.6 0.2 collective-permute-start.7
  123.8 1.4 %collective-permute-done.7 = bf16[1024,128]{1,0:T(8,128)(2,1)S(1)} collective-permute-done((bf16[1024,128]{1,0:T(8,128)(2,1)S(1)}, bf16[1024,128]{1,0:T(8,128)(2,1)S(1)}, u32[]{:S(2)}, u32[]{:S(2)}) %collective-permute-start.7) | collective-permute-done | bytes 262176 | tf_op jit(solution)/shard_map/ppermute | solution.py:22
  125.2 0.7 constant_dynamic-update-slice_fusion
  (1 shorter events, 0.0 us)
Async XLA Ops:
  1.0 1.0 copy-start
  5.6 16.5 %copy-start.1 = (bf16[2,256,512]{2,1,0:T(8,128)(2,1)S(1)}, bf16[2,256,512]{2,1,0:T(8,128)(2,1)}, u32[]{:S(2)}) copy-start(bf16[2,256,512]{2,1,0:T(8,128)(2,1)} %up_a.3) | copy-start | bytes 1572868
  5.6 17.5 %copy-start.2 = (bf16[2,512,256]{2,1,0:T(8,128)(2,1)S(1)}, bf16[2,512,256]{2,1,0:T(8,128)(2,1)}, u32[]{:S(2)}) copy-start(bf16[2,512,256]{2,1,0:T(8,128)(2,1)} %down_a.3) | copy-start | bytes 1572868
  5.6 18.0 %copy-start.7 = (s32[2,2048]{1,0:T(2,128)S(1)}, s32[2,2048]{1,0:T(2,128)}, u32[]{:S(2)}) copy-start(s32[2,2048]{1,0:T(2,128)} %param.11) | copy-start | bytes 49156
  5.6 46.7 %all-to-all-start = ((bf16[128,32,128]{2,1,0:T(8,128)(2,1)}), bf16[128,32,128]{2,1,0:T(8,128)(2,1)S(1)}, u32[]{:S(2)}, u32[]{:S(2)}) async-start(bf16[128,32,128]{2,1,0:T(8,128)(2,1)} %bitcast.1), calls=%async_computation | async-start | bytes 2097152 | tf_op jit(solution)/shard_map/all_to_all | solution.py:217
  22.1 36.0 %collective-permute-start.3 = (bf16[2,256,512]{2,1,0:T(8,128)(2,1)S(1)}, bf16[2,256,512]{2,1,0:T(8,128)(2,1)S(1)}, u32[]{:S(2)}, u32[]{:S(2)}) collective-permute-start(bf16[2,256,512]{2,1,0:T(8,128)(2,1)S(1)} %copy-done.1), channel_id=1, source_target_pairs={{0,1},{1,0},{2,3},{3,2},{4,5},{5,4},{6,7},{7,6},{8,9},{9,8},{10,11... | collective-permute-start | bytes 1572872 | tf_op jit(solution)/shard_map/ppermute | solution.py:22
  23.1 35.0 %collective-permute-start.4 = (bf16[2,512,256]{2,1,0:T(8,128)(2,1)S(1)}, bf16[2,512,256]{2,1,0:T(8,128)(2,1)S(1)}, u32[]{:S(2)}, u32[]{:S(2)}) collective-permute-start(bf16[2,512,256]{2,1,0:T(8,128)(2,1)S(1)} %copy-done.2), channel_id=1, source_target_pairs={{0,1},{1,0},{2,3},{3,2},{4,5},{5,4},{6,7},{7,6},{8,9},{9,8},{10,11... | collective-permute-start | bytes 1572872 | tf_op jit(solution)/shard_map/ppermute | solution.py:22
  23.2 34.9 %collective-permute-start.1 = (bf16[2,3,256,128]{3,2,1,0:T(8,128)(2,1)}, bf16[2,3,256,128]{3,2,1,0:T(8,128)(2,1)}, u32[]{:S(2)}, u32[]{:S(2)}) collective-permute-start(bf16[2,3,256,128]{3,2,1,0:T(8,128)(2,1)} %bitcast.11), channel_id=1, source_target_pairs={{0,1},{1,0},{2,3},{3,2},{4,5},{5,4},{6,7},{7,6},{8,9},{9,8},{10,11... | collective-permute-start | bytes 1179656 | tf_op jit(solution)/shard_map/ppermute | solution.py:22
  52.3 4.1 %copy-start.4 = (bf16[2,128,256]{2,1,0:T(8,128)(2,1)S(1)}, bf16[2,128,256]{2,1,0:T(8,128)(2,1)}, u32[]{:S(2)}) copy-start(bf16[2,128,256]{2,1,0:T(8,128)(2,1)} %out_a.3) | copy-start | bytes 393220
  53.7 4.5 %copy-start.3 = (bf16[2,256,3,128]{3,1,2,0:T(8,128)(2,1)S(1)}, bf16[2,256,3,128]{3,1,2,0:T(8,128)(2,1)}, u32[]{:S(2)}) copy-start(bf16[2,256,3,128]{3,1,2,0:T(8,128)(2,1)} %param.12) | copy-start | bytes 1179652
  53.7 4.5 %copy-start.5 = (f32[2,256]{1,0:T(2,128)S(1)}, f32[2,256]{1,0:T(2,128)}, u32[]{:S(2)}) copy-start(f32[2,256]{1,0:T(2,128)} %gain_a.3) | copy-start | bytes 6148
  53.7 4.5 %copy-start.6 = (f32[2,256]{1,0:T(2,128)S(1)}, f32[2,256]{1,0:T(2,128)}, u32[]{:S(2)}) copy-start(f32[2,256]{1,0:T(2,128)} %gain_m.3) | copy-start | bytes 6148
  53.7 4.4 %collective-permute-start = (bf16[1024,128]{1,0:T(8,128)(2,1)S(1)}, bf16[1024,128]{1,0:T(8,128)(2,1)S(1)}, u32[]{:S(2)}, u32[]{:S(2)}) collective-permute-start(bf16[1024,128]{1,0:T(8,128)(2,1)S(1)} %shard_map.93), channel_id=1, source_target_pairs={{0,1},{1,0},{2,3},{3,2},{4,5},{5,4},{6,7},{7,6},{8,9},{9,8},{10,11... | collective-permute-start | bytes 786440 | tf_op jit(solution)/shard_map/ppermute | solution.py:22
  56.4 1.7 %collective-permute-start.2 = (bf16[2,128,256]{2,1,0:T(8,128)(2,1)S(1)}, bf16[2,128,256]{2,1,0:T(8,128)(2,1)S(1)}, u32[]{:S(2)}, u32[]{:S(2)}) collective-permute-start(bf16[2,128,256]{2,1,0:T(8,128)(2,1)S(1)} %copy-done.4), channel_id=1, source_target_pairs={{0,1},{1,0},{2,3},{3,2},{4,5},{5,4},{6,7},{7,6},{8,9},{9,8},{10,11... | collective-permute-start | bytes 393224 | tf_op jit(solution)/shard_map/ppermute | solution.py:22
  67.6 1.6 %collective-permute-start.5 = (bf16[1024,128]{1,0:T(8,128)(2,1)S(1)}, bf16[1024,128]{1,0:T(8,128)(2,1)S(1)}, u32[]{:S(2)}, u32[]{:S(2)}) collective-permute-start(bf16[1024,128]{1,0:T(8,128)(2,1)S(1)} %get-tuple-element.10), channel_id=1, source_target_pairs={{0,1},{1,0},{2,3},{3,2},{4,5},{5,4},{6,7},{7,6},{8,9},{9,8},{10,11... | collective-permute-start | bytes 786440 | tf_op jit(solution)/shard_map/ppermute | solution.py:22
  110.3 3.1 %collective-permute-start.6 = (bf16[1024,128]{1,0:T(8,128)(2,1)S(1)}, bf16[1024,128]{1,0:T(8,128)(2,1)S(1)}, u32[]{:S(2)}, u32[]{:S(2)}) collective-permute-start(bf16[1024,128]{1,0:T(8,128)(2,1)S(1)} %shard_map.97), channel_id=1, source_target_pairs={{0,1},{1,0},{2,3},{3,2},{4,5},{5,4},{6,7},{7,6},{8,9},{9,8},{10,11... | collective-permute-start | bytes 786440 | tf_op jit(solution)/shard_map/ppermute | solution.py:22
  123.6 1.5 %collective-permute-start.7 = (bf16[1024,128]{1,0:T(8,128)(2,1)S(1)}, bf16[1024,128]{1,0:T(8,128)(2,1)S(1)}, u32[]{:S(2)}, u32[]{:S(2)}) collective-permute-start(bf16[1024,128]{1,0:T(8,128)(2,1)S(1)} %get-tuple-element.12), channel_id=1, source_target_pairs={{0,1},{1,0},{2,3},{3,2},{4,5},{5,4},{6,7},{7,6},{8,9},{9,8},{10,11... | collective-permute-start | bytes 786440 | tf_op jit(solution)/shard_map/ppermute | solution.py:22

commit v4 on v3

--- a/solution.py
+++ b/solution.py
@@ -22,46 +22,47 @@
     return lax.ppermute(value, "ch", SWAP)
 
 
-def pick_kernel(flips, core_ref, index_ref, *refs):
-    sources, out_ref = refs[:-1], refs[-1]
+def pick_kernel(flips, start, core_ref, index_ref, source_ref, *refs):
+    out_ref = refs[-1]
     index = index_ref[0, 0]
     if flips:
         index = jnp.bitwise_xor(index, core_ref[0] * WIN)
     index = index.astype(jnp.int16)
-    total = None
-    start = 0
-    for source in sources:
-        shape = (source.shape[0], index.shape[1])
-        row = lax.broadcasted_iota(jnp.int16, shape, 0) + jnp.int16(start)
-        hot = jnp.where(
-            jnp.broadcast_to(index, shape) == row,
-            jnp.ones(shape, jnp.bfloat16),
-            jnp.zeros(shape, jnp.bfloat16),
-        )
-        part = lax.dot_general(
-            source[...], hot, (((0,), (0,)), ((), ())), preferred_element_type=jnp.float32
-        )
-        total = part if total is None else total + part
-        start += shape[0]
-    out_ref[...] = total.T.astype(jnp.bfloat16)
-
-
-def pick(core, table, layer, part, *sources, flips=False):
+    shape = (source_ref.shape[0], index.shape[1])
+    row = lax.broadcasted_iota(jnp.int16, shape, 0) + jnp.int16(start)
+    hot = jnp.where(
+        jnp.broadcast_to(index, shape) == row,
+        jnp.ones(shape, jnp.bfloat16),
+        jnp.zeros(shape, jnp.bfloat16),
+    )
+    found = lax.dot_general(
+        source_ref[...], hot, (((0,), (0,)), ((), ())), preferred_element_type=jnp.float32
+    )
+    found = found.T.astype(jnp.bfloat16)
+    out_ref[...] = found if len(refs) == 1 else found + refs[0][...]
+
+
+def pick(core, table, layer, part, source, others=None, start=0, flips=False):
     tile = table.shape[3]
     steps = table.shape[1] if part is None else 1
-    depth = sum(source.shape[0] for source in sources)
+    depth = source.shape[0]
+    rows = pl.BlockSpec((tile, HALF), lambda i, word: (i, 0))
 
     def block(i, word):
         return (layer, i if part is None else part(word[0]), 0, 0)
 
+    more = [] if others is None else [others]
     return pl.pallas_call(
-        functools.partial(pick_kernel, flips),
+        functools.partial(pick_kernel, flips, start),
         grid_spec=pltpu.PrefetchScalarGridSpec(
             num_scalar_prefetch=1,
             grid=(steps,),
-            in_specs=[pl.BlockSpec((1, 1, 1, tile), block)]
-            + [pl.BlockSpec(source.shape, lambda i, word: (0, 0)) for source in sources],
-            out_specs=pl.BlockSpec((tile, HALF), lambda i, word: (i, 0)),
+            in_specs=[
+                pl.BlockSpec((1, 1, 1, tile), block),
+                pl.BlockSpec(source.shape, lambda i, word: (0, 0)),
+            ]
+            + [rows] * len(more),
+            out_specs=rows,
         ),
         out_shape=jax.ShapeDtypeStruct((steps * tile, HALF), jnp.bfloat16),
         compiler_params=pltpu.CompilerParams(vmem_limit_bytes=VMEM),
@@ -70,7 +71,7 @@
             bytes_accessed=(steps * tile + depth) * 256,
             transcendentals=0,
         ),
-    )(core, table, *sources)
+    )(core, table, source, *more)
 
 
 def layer_norm(values, gain):
@@ -104,7 +105,11 @@
     keep_ref,
     give_ref,
     attended_ref,
+    qkv_ref,
+    arrived,
 ):
+    fetch = pltpu.make_async_copy(qkv_b.at[layer], qkv_ref, arrived)
+    fetch.start()
     first = core_ref[0] == 0
     mine, got = mine_ref[...], got_ref[...]
     low = jnp.where(first, mine, got)
@@ -114,15 +119,17 @@
     factor = math.log2(math.e) / math.sqrt(HEAD)
     over_rows = (((0,), (1,)), ((), ()))
     units = []
-    for n, weight in enumerate((qkv_a, qkv_b)):
+    for n, weight in enumerate((qkv_a.at[layer], qkv_ref)):
+        if n == 1:
+            fetch.wait()
         queries = lax.dot_general(
-            weight[layer, 0], normed, over_rows, preferred_element_type=jnp.float32
+            weight[0], normed, over_rows, preferred_element_type=jnp.float32
         ).astype(jnp.bfloat16)
         keys = jnp.dot(
-            normed, weight[layer, 1], preferred_element_type=jnp.float32
+            normed, weight[1], preferred_element_type=jnp.float32
         ).astype(jnp.bfloat16)
         values = lax.dot_general(
-            weight[layer, 2], normed, over_rows, preferred_element_type=jnp.float32
+            weight[2], normed, over_rows, preferred_element_type=jnp.float32
         ).astype(jnp.bfloat16)
         zero = jnp.zeros((HEAD, WIN), jnp.bfloat16)
         ones = jnp.ones((16, WIN), jnp.bfloat16)
@@ -156,35 +163,40 @@
     )
     hstream = (current.astype(jnp.float32) + added).astype(jnp.bfloat16)
     normed_two = layer_norm(hstream.astype(jnp.float32), gain_m[layer : layer + 1]).astype(jnp.bfloat16)
-    result = hstream.astype(jnp.float32)
-    for up, down in ((up_a, down_a), (up_b, down_b)):
-        hidden = gelu(jnp.dot(normed_two, up[layer], preferred_element_type=jnp.float32))
-        result = result + jnp.dot(
-            hidden.astype(jnp.bfloat16), down[layer], preferred_element_type=jnp.float32
-        )
+    parts = []
+    for at in range(0, WIN, 512):
+        rows = slice(at, at + 512)
+        total = hstream[rows].astype(jnp.float32)
+        for up, down in ((up_a, down_a), (up_b, down_b)):
+            hidden = gelu(
+                jnp.dot(normed_two[rows], up[layer], preferred_element_type=jnp.float32)
+            )
+            total = total + jnp.dot(
+                hidden.astype(jnp.bfloat16), down[layer], preferred_element_type=jnp.float32
+            )
+        parts.append(total)
+    result = jnp.concatenate(parts, axis=0)
     result = result.astype(jnp.bfloat16)
     low, high = result[:, :HALF], result[:, HALF:]
-    kept = jnp.where(first, low, high)
-    if keep_ref.shape[0] == WIN:
-        keep_ref[...] = kept
-    else:
-        keep_ref[pl.ds(pl.multiple_of(core_ref[0] * WIN, WIN), WIN), :] = kept
+    keep_ref[...] = jnp.where(first, low, high)
     give_ref[...] = jnp.where(first, high, low)
 
 
 def window_block(layer, core, mine, got, weights, gain_attn, gain_mlp):
-    kept = WIN if layer + 1 < BLOCKS else 2 * WIN
+    half = jax.ShapeDtypeStruct((WIN, HALF), jnp.bfloat16)
     whole = pl.BlockSpec(memory_space=pltpu.VMEM)
     return pl.pallas_call(
         functools.partial(block_kernel, layer),
-        in_specs=[pl.BlockSpec(memory_space=pltpu.SMEM)] + [whole] * (4 + len(weights)),
+        in_specs=[pl.BlockSpec(memory_space=pltpu.SMEM)]
+        + [whole] * 3
+        + [pl.BlockSpec(memory_space=pl.ANY)]
+        + [whole] * len(weights),
         out_specs=[whole, whole],
-        out_shape=[
-            jax.ShapeDtypeStruct((kept, HALF), jnp.bfloat16),
-            jax.ShapeDtypeStruct((WIN, HALF), jnp.bfloat16),
-        ],
+        out_shape=[half, half],
         scratch_shapes=[
             pltpu.VMEM((D, WIN), jnp.bfloat16),
+            pltpu.VMEM((3, D, HALF), jnp.bfloat16),
+            pltpu.SemaphoreType.DMA(()),
         ],
         compiler_params=pltpu.CompilerParams(vmem_limit_bytes=VMEM),
         cost_estimate=pl.CostEstimate(
@@ -211,9 +223,8 @@
         weights += [array, swap(array)]
     send_table = send_rows.reshape(BLOCKS, 2, 1, -1)
     recv_table = recv_slots.reshape(BLOCKS, 2, 1, WIN)
-    sources = (stream,)
+    picked = pick(word, send_table, 0, None, stream)
     for layer in range(BLOCKS):
-        picked = pick(word, send_table, layer, None, *sources, flips=layer > 0)
         moved = lax.all_to_all(
             picked.reshape(-1, 32, HALF), "pts", split_axis=0, concat_axis=0, tiled=True
         ).reshape(-1, HALF)
@@ -221,8 +232,14 @@
         mine = pick(word, recv_table, layer, lambda own: own, moved)
         keep, give = window_block(layer, word, mine, got, weights, gain_attn, gain_mlp)
         back = swap(give)
-        sources = (keep, back)
-    return lax.dynamic_update_slice(keep, back, ((1 - core) * WIN, 0))
+        if layer + 1 < BLOCKS:
+            picked = pick(word, send_table, layer + 1, None, keep, flips=True)
+            picked = pick(
+                word, send_table, layer + 1, None, back, others=picked, start=WIN, flips=True
+            )
+    result = jnp.zeros((2 * WIN, HALF), jnp.bfloat16)
+    result = lax.optimization_barrier(lax.dynamic_update_slice(result, keep, (core * WIN, 0)))
+    return lax.dynamic_update_slice(result, back, ((1 - core) * WIN, 0))
 
 
 def solution(mesh):

time: 126 us -> 124 us (0.984)
  Pallas kernels: 31.3 us -> 29.8 us
  waiting for transfers between devices: 31.4 us -> 29.9 us
    pallas_call x2, Pallas kernels: 19.7 us -> 17.5 us  [window_block(): pl.pallas_call(functools.partial(block_kernel, layer), in_specs=[pl.Block...]
    ppermute x8, waiting for transfers between devices: 2.7 us -> 1.27 us  [swap(): return lax.ppermute(value, 'ch', SWAP)]
    pallas_call x6 -> x7, Pallas kernels: 11.7 us -> 12.3 us  [pick(): pl.pallas_call(functools.partial(pick_kernel, flips, start), grid_spec=pl...]
  transfers between devices with their start and end apart: 9 -> 9, of which waited for: 3 -> 2; matrix products, arithmetic and copies ran while one was open for 0% -> 0% of each run, Pallas kernels for 3% -> 5%
where the time goes in v4:
time: 124 us; the launch traced here: 123 us
  blocking collectives  36.8 us (30%)
  waiting for transfers between devices  29.9 us (24%)
  Pallas kernels  29.8 us (24%)
  starting transfers between devices  23.5 us (19%)
  local copies, waits for them, and re-layouts  2.91 us (2%)
    all_to_all x1, blocking collectives, shards(): lax.all_to_all(picked.reshape(-1, 32, HALF), 'pts', split_axis=0, concat_...  36.8 us
    all_to_all x1, waiting for transfers between devices, shards(): lax.all_to_all(picked.reshape(-1, 32, HALF), 'pts', split_axis=0, concat_...  28.7 us
    pallas_call x2, Pallas kernels, window_block(): pl.pallas_call(functools.partial(block_kernel, layer), in_specs=[pl.Block...  17.5 us
    all_to_all x1, starting transfers between devices, shards(): lax.all_to_all(picked.reshape(-1, 32, HALF), 'pts', split_axis=0, concat_...  16.5 us
    pallas_call x7, Pallas kernels, pick(): pl.pallas_call(functools.partial(pick_kernel, flips, start), grid_spec=pl...  12.3 us
    ppermute x8, starting transfers between devices, swap(): return lax.ppermute(value, 'ch', SWAP)  7.03 us
  transfers between devices with their start and end apart: 9, of which 2 were waited for; matrix products, arithmetic and copies ran while one was open for 0% of the time, Pallas kernels for 5%

profile of v4, /device:TPU:1, one launch (start us, length us, event | category | flops | bytes accessed | tf_op | source)
XLA Modules:
  0.0 123.2 jit_solution(13102447655832837518)
XLA Ops:
  0.0 0.9 copy.11
  0.9 0.1 reshape.28.index_ref
  1.0 0.0 copy-start
  1.0 1.0 copy-done
  2.0 3.5 %shard_map.91 = bf16[4096,128]{1,0:T(8,128)(2,1)} custom-call(s32[1]{0:T(128)} %bitcast.core_ref, s32[2,2,1,2048]{3,2,1,0:T(1,128)S(1)} %reshape.28.index_ref, bf16[2048,128]{1,0:T(8,128)(2,1)S(1)} %copy-done), custom_call_target="tpu_custom_call" | custom-call | flops 4294967296 | bytes 1572864 | tf_op jit(solution)/shard_map/pallas_call | solution.py:55
  5.6 0.0 copy-start.1
  5.6 0.0 copy-start.2
  5.6 0.0 copy-start.8
  5.6 16.5 %all-to-all-start = ((bf16[128,32,128]{2,1,0:T(8,128)(2,1)}), bf16[128,32,128]{2,1,0:T(8,128)(2,1)S(1)}, u32[]{:S(2)}, u32[]{:S(2)}) async-start(bf16[128,32,128]{2,1,0:T(8,128)(2,1)} %bitcast.1), calls=%async_computation | async-start | bytes 2097152 | tf_op jit(solution)/shard_map/all_to_all | solution.py:228
  22.0 0.0 copy-done.1
  22.1 1.0 collective-permute-start.3
  23.1 0.0 copy-done.2
  23.1 0.1 collective-permute-start.4
  23.2 0.4 collective-permute-start.1
  23.6 0.0 copy-done.8
  23.6 28.7 %all-to-all-done = bf16[128,32,128]{2,1,0:T(8,128)(2,1)S(1)} async-done(((bf16[128,32,128]{2,1,0:T(8,128)(2,1)}), bf16[128,32,128]{2,1,0:T(8,128)(2,1)S(1)}, u32[]{:S(2)}, u32[]{:S(2)}) %all-to-all-start) | async-done | bytes 1048608 | tf_op jit(solution)/shard_map/all_to_all | solution.py:228
  52.3 0.0 copy-start.4
  52.3 1.4 %shard_map.93 = bf16[1024,128]{1,0:T(8,128)(2,1)S(1)} custom-call(s32[1]{0:T(128)} %bitcast.core_ref, s32[2,2,1,1024]{3,2,1,0:T(1,128)S(1)} %reshape.22.index_ref, bf16[4096,128]{1,0:T(8,128)(2,1)S(1)} %bitcast.6), custom_call_target="tpu_custom_call" | custom-call | flops 2147483648 | bytes 1310720 | tf_op jit(solution)/shard_map/pallas_call | solution.py:55
  53.7 0.0 copy-start.3
  53.7 0.0 copy-start.5
  53.7 0.0 copy-start.6
  53.7 2.7 %collective-permute-start = (bf16[1024,128]{1,0:T(8,128)(2,1)S(1)}, bf16[1024,128]{1,0:T(8,128)(2,1)S(1)}, u32[]{:S(2)}, u32[]{:S(2)}) collective-permute-start(bf16[1024,128]{1,0:T(8,128)(2,1)S(1)} %shard_map.93), channel_id=1, source_target_pairs={{0,1},{1,0},{2,3},{3,2},{4,5},{5,4},{6,7},{7,6},{8,9},{9,8},{10,11... | collective-permute-start | bytes 786440 | tf_op jit(solution)/shard_map/ppermute | solution.py:22
  56.4 0.0 copy-done.4
  56.4 0.3 collective-permute-start.2
  56.7 1.4 %shard_map.92.mine_ref = bf16[1024,128]{1,0:T(8,128)(2,1)S(1)} custom-call(s32[1]{0:T(128)} %bitcast.core_ref, s32[2,2,1,1024]{3,2,1,0:T(1,128)S(1)} %reshape.22.index_ref, bf16[4096,128]{1,0:T(8,128)(2,1)S(1)} %bitcast.7), custom_call_target="tpu_custom_call" | custom-call | flops 2147483648 | bytes 1310720 | tf_op jit(solution)/shard_map/pallas_call | solution.py:55
  58.1 0.0 collective-permute-done.2.out_b
  58.1 0.0 collective-permute-done.1.qkv_b
  58.1 0.0 collective-permute-done.3.up_b
  58.1 0.0 collective-permute-done.4.down_b
  58.1 0.0 collective-permute-done.got_ref
  58.1 0.0 copy-done.3
  58.1 0.0 copy-done.5
  58.1 0.0 copy-done.6
  58.1 8.8 %shard_map.94 = (bf16[1024,128]{1,0:T(8,128)(2,1)S(1)}, bf16[1024,128]{1,0:T(8,128)(2,1)S(1)}) custom-call(s32[1]{0:T(128)} %bitcast.core_ref, bf16[1024,128]{1,0:T(8,128)(2,1)S(1)} %shard_map.92.mine_ref, bf16[1024,128]{1,0:T(8,128)(2,1)S(1)} %collective-permute-done.got_ref, bf16[2,3,256,128]{3,2,1,0:T(8,128)(2,1)S(1)} %bitcast.12, ...), custom_call_target="tpu_custom_call" | custom-call | flops 6000000000 | bytes 3000000 | tf_op jit(solution)/shard_map/pallas_call | solution.py:188
  66.9 0.3 collective-permute-start.5
  67.2 1.7 %shard_map.95.refs_0_ = bf16[4096,128]{1,0:T(8,128)(2,1)S(1)} custom-call(s32[1]{0:T(128)} %bitcast.core_ref, s32[2,2,1,2048]{3,2,1,0:T(1,128)S(1)} %reshape.28.index_ref, bf16[1024,128]{1,0:T(8,128)(2,1)S(1)} %get-tuple-element.10.source_ref), custom_call_target="tpu_custom_call" | custom-call | flops 2147483648 | bytes 1310720 | tf_op jit(solution)/shard_map/pallas_call | solution.py:55
  68.9 0.0 collective-permute-done.5.source_ref
  68.9 1.7 %shard_map.96 = bf16[4096,128]{1,0:T(8,128)(2,1)S(1)} custom-call(s32[1]{0:T(128)} %bitcast.core_ref, s32[2,2,1,2048]{3,2,1,0:T(1,128)S(1)} %reshape.28.index_ref, bf16[1024,128]{1,0:T(8,128)(2,1)S(1)} %collective-permute-done.5.source_ref, bf16[4096,128]{1,0:T(8,128)(2,1)S(1)} %shard_map.95.refs_0_), custom_call_target="tpu_custom_call" | custom-call | flops 2147483648 | bytes 1310720 | tf_op jit(solution)/shard_map/pallas_call | solution.py:55
  70.6 36.8 %all_to_all.10 = bf16[128,32,128]{2,1,0:T(8,128)(2,1)S(1)} all-to-all(bf16[128,32,128]{2,1,0:T(8,128)(2,1)S(1)} %bitcast.10), channel_id=1, replica_groups=mesh['pts'=128,'ch'=2] {'pts'}, dimensions={0} | all-to-all | bytes 2097152 | tf_op jit(solution)/shard_map/all_to_all | solution.py:228
  107.4 1.4 %shard_map.98 = bf16[1024,128]{1,0:T(8,128)(2,1)S(1)} custom-call(s32[1]{0:T(128)} %bitcast.core_ref, s32[2,2,1,1024]{3,2,1,0:T(1,128)S(1)} %reshape.22.index_ref, bf16[4096,128]{1,0:T(8,128)(2,1)S(1)} %bitcast.8), custom_call_target="tpu_custom_call" | custom-call | flops 2147483648 | bytes 1310720 | tf_op jit(solution)/shard_map/pallas_call | solution.py:55
  108.7 1.9 %collective-permute-start.6 = (bf16[1024,128]{1,0:T(8,128)(2,1)S(1)}, bf16[1024,128]{1,0:T(8,128)(2,1)S(1)}, u32[]{:S(2)}, u32[]{:S(2)}) collective-permute-start(bf16[1024,128]{1,0:T(8,128)(2,1)S(1)} %shard_map.98), channel_id=1, source_target_pairs={{0,1},{1,0},{2,3},{3,2},{4,5},{5,4},{6,7},{7,6},{8,9},{9,8},{10,11... | collective-permute-start | bytes 786440 | tf_op jit(solution)/shard_map/ppermute | solution.py:22
  110.7 1.4 %shard_map.97.mine_ref = bf16[1024,128]{1,0:T(8,128)(2,1)S(1)} custom-call(s32[1]{0:T(128)} %bitcast.core_ref, s32[2,2,1,1024]{3,2,1,0:T(1,128)S(1)} %reshape.22.index_ref, bf16[4096,128]{1,0:T(8,128)(2,1)S(1)} %bitcast.9), custom_call_target="tpu_custom_call" | custom-call | flops 2147483648 | bytes 1310720 | tf_op jit(solution)/shard_map/pallas_call | solution.py:55
  112.0 0.0 collective-permute-done.6.got_ref
  112.0 8.8 %shard_map.99 = (bf16[1024,128]{1,0:T(8,128)(2,1)S(1)}, bf16[1024,128]{1,0:T(8,128)(2,1)S(1)}) custom-call(s32[1]{0:T(128)} %bitcast.core_ref, bf16[1024,128]{1,0:T(8,128)(2,1)S(1)} %shard_map.97.mine_ref, bf16[1024,128]{1,0:T(8,128)(2,1)S(1)} %collective-permute-done.6.got_ref, bf16[2,3,256,128]{3,2,1,0:T(8,128)(2,1)S(1)} %bitcast.13, ...), custom_call_target="tpu_custom_call" | custom-call | flops 6000000000 | bytes 3000000 | tf_op jit(solution)/shard_map/pallas_call | solution.py:188
  120.8 0.2 collective-permute-start.7
  121.1 0.1 broadcast_in_dim.3
  121.2 0.0 copy-start.7
  121.2 1.3 %collective-permute-done.7 = bf16[1024,128]{1,0:T(8,128)(2,1)S(1)} collective-permute-done((bf16[1024,128]{1,0:T(8,128)(2,1)S(1)}, bf16[1024,128]{1,0:T(8,128)(2,1)S(1)}, u32[]{:S(2)}, u32[]{:S(2)}) %collective-permute-start.7) | collective-permute-done | bytes 262176 | tf_op jit(solution)/shard_map/ppermute | solution.py:22
  122.4 0.0 copy-done.7
  122.4 0.7 constant_dynamic-update-slice_fusion
  (2 shorter events, 0.1 us)
Async XLA Ops:
  1.0 1.0 copy-start
  5.6 16.5 %copy-start.1 = (bf16[2,256,512]{2,1,0:T(8,128)(2,1)S(1)}, bf16[2,256,512]{2,1,0:T(8,128)(2,1)}, u32[]{:S(2)}) copy-start(bf16[2,256,512]{2,1,0:T(8,128)(2,1)} %up_a.3) | copy-start | bytes 1572868
  5.6 17.5 %copy-start.2 = (bf16[2,512,256]{2,1,0:T(8,128)(2,1)S(1)}, bf16[2,512,256]{2,1,0:T(8,128)(2,1)}, u32[]{:S(2)}) copy-start(bf16[2,512,256]{2,1,0:T(8,128)(2,1)} %down_a.3) | copy-start | bytes 1572868
  5.6 18.0 %copy-start.8 = (s32[2,2048]{1,0:T(2,128)S(1)}, s32[2,2048]{1,0:T(2,128)}, u32[]{:S(2)}) copy-start(s32[2,2048]{1,0:T(2,128)} %param.11) | copy-start | bytes 49156
  5.6 46.7 %all-to-all-start = ((bf16[128,32,128]{2,1,0:T(8,128)(2,1)}), bf16[128,32,128]{2,1,0:T(8,128)(2,1)S(1)}, u32[]{:S(2)}, u32[]{:S(2)}) async-start(bf16[128,32,128]{2,1,0:T(8,128)(2,1)} %bitcast.1), calls=%async_computation | async-start | bytes 2097152 | tf_op jit(solution)/shard_map/all_to_all | solution.py:228
  22.1 36.0 %collective-permute-start.3 = (bf16[2,256,512]{2,1,0:T(8,128)(2,1)S(1)}, bf16[2,256,512]{2,1,0:T(8,128)(2,1)S(1)}, u32[]{:S(2)}, u32[]{:S(2)}) collective-permute-start(bf16[2,256,512]{2,1,0:T(8,128)(2,1)S(1)} %copy-done.1), channel_id=1, source_target_pairs={{0,1},{1,0},{2,3},{3,2},{4,5},{5,4},{6,7},{7,6},{8,9},{9,8},{10,11... | collective-permute-start | bytes 1572872 | tf_op jit(solution)/shard_map/ppermute | solution.py:22
  23.1 35.0 %collective-permute-start.4 = (bf16[2,512,256]{2,1,0:T(8,128)(2,1)S(1)}, bf16[2,512,256]{2,1,0:T(8,128)(2,1)S(1)}, u32[]{:S(2)}, u32[]{:S(2)}) collective-permute-start(bf16[2,512,256]{2,1,0:T(8,128)(2,1)S(1)} %copy-done.2), channel_id=1, source_target_pairs={{0,1},{1,0},{2,3},{3,2},{4,5},{5,4},{6,7},{7,6},{8,9},{9,8},{10,11... | collective-permute-start | bytes 1572872 | tf_op jit(solution)/shard_map/ppermute | solution.py:22
  23.2 34.9 %collective-permute-start.1 = (bf16[2,3,256,128]{3,2,1,0:T(8,128)(2,1)}, bf16[2,3,256,128]{3,2,1,0:T(8,128)(2,1)}, u32[]{:S(2)}, u32[]{:S(2)}) collective-permute-start(bf16[2,3,256,128]{3,2,1,0:T(8,128)(2,1)} %bitcast.11), channel_id=1, source_target_pairs={{0,1},{1,0},{2,3},{3,2},{4,5},{5,4},{6,7},{7,6},{8,9},{9,8},{10,11... | collective-permute-start | bytes 1179656 | tf_op jit(solution)/shard_map/ppermute | solution.py:22
  52.3 4.1 %copy-start.4 = (bf16[2,128,256]{2,1,0:T(8,128)(2,1)S(1)}, bf16[2,128,256]{2,1,0:T(8,128)(2,1)}, u32[]{:S(2)}) copy-start(bf16[2,128,256]{2,1,0:T(8,128)(2,1)} %out_a.3) | copy-start | bytes 393220
  53.7 4.5 %copy-start.3 = (bf16[2,256,3,128]{3,1,2,0:T(8,128)(2,1)S(1)}, bf16[2,256,3,128]{3,1,2,0:T(8,128)(2,1)}, u32[]{:S(2)}) copy-start(bf16[2,256,3,128]{3,1,2,0:T(8,128)(2,1)} %param.12) | copy-start | bytes 1179652
  53.7 4.5 %copy-start.5 = (f32[2,256]{1,0:T(2,128)S(1)}, f32[2,256]{1,0:T(2,128)}, u32[]{:S(2)}) copy-start(f32[2,256]{1,0:T(2,128)} %gain_a.3) | copy-start | bytes 6148
  53.7 4.5 %copy-start.6 = (f32[2,256]{1,0:T(2,128)S(1)}, f32[2,256]{1,0:T(2,128)}, u32[]{:S(2)}) copy-start(f32[2,256]{1,0:T(2,128)} %gain_m.3) | copy-start | bytes 6148
  53.7 4.4 %collective-permute-start = (bf16[1024,128]{1,0:T(8,128)(2,1)S(1)}, bf16[1024,128]{1,0:T(8,128)(2,1)S(1)}, u32[]{:S(2)}, u32[]{:S(2)}) collective-permute-start(bf16[1024,128]{1,0:T(8,128)(2,1)S(1)} %shard_map.93), channel_id=1, source_target_pairs={{0,1},{1,0},{2,3},{3,2},{4,5},{5,4},{6,7},{7,6},{8,9},{9,8},{10,11... | collective-permute-start | bytes 786440 | tf_op jit(solution)/shard_map/ppermute | solution.py:22
  56.4 1.7 %collective-permute-start.2 = (bf16[2,128,256]{2,1,0:T(8,128)(2,1)S(1)}, bf16[2,128,256]{2,1,0:T(8,128)(2,1)S(1)}, u32[]{:S(2)}, u32[]{:S(2)}) collective-permute-start(bf16[2,128,256]{2,1,0:T(8,128)(2,1)S(1)} %copy-done.4), channel_id=1, source_target_pairs={{0,1},{1,0},{2,3},{3,2},{4,5},{5,4},{6,7},{7,6},{8,9},{9,8},{10,11... | collective-permute-start | bytes 393224 | tf_op jit(solution)/shard_map/ppermute | solution.py:22
  66.9 2.0 %collective-permute-start.5 = (bf16[1024,128]{1,0:T(8,128)(2,1)S(1)}, bf16[1024,128]{1,0:T(8,128)(2,1)S(1)}, u32[]{:S(2)}, u32[]{:S(2)}) collective-permute-start(bf16[1024,128]{1,0:T(8,128)(2,1)S(1)} %get-tuple-element.9), channel_id=1, source_target_pairs={{0,1},{1,0},{2,3},{3,2},{4,5},{5,4},{6,7},{7,6},{8,9},{9,8},{10,11... | collective-permute-start | bytes 786440 | tf_op jit(solution)/shard_map/ppermute | solution.py:22
  108.7 3.3 %collective-permute-start.6 = (bf16[1024,128]{1,0:T(8,128)(2,1)S(1)}, bf16[1024,128]{1,0:T(8,128)(2,1)S(1)}, u32[]{:S(2)}, u32[]{:S(2)}) collective-permute-start(bf16[1024,128]{1,0:T(8,128)(2,1)S(1)} %shard_map.98), channel_id=1, source_target_pairs={{0,1},{1,0},{2,3},{3,2},{4,5},{5,4},{6,7},{7,6},{8,9},{9,8},{10,11... | collective-permute-start | bytes 786440 | tf_op jit(solution)/shard_map/ppermute | solution.py:22
  120.8 1.6 %collective-permute-start.7 = (bf16[1024,128]{1,0:T(8,128)(2,1)S(1)}, bf16[1024,128]{1,0:T(8,128)(2,1)S(1)}, u32[]{:S(2)}, u32[]{:S(2)}) collective-permute-start(bf16[1024,128]{1,0:T(8,128)(2,1)S(1)} %get-tuple-element.12), channel_id=1, source_target_pairs={{0,1},{1,0},{2,3},{3,2},{4,5},{5,4},{6,7},{7,6},{8,9},{9,8},{10,11... | collective-permute-start | bytes 786440 | tf_op jit(solution)/shard_map/ppermute | solution.py:22
  121.2 1.3 %copy-start.7 = (bf16[2048,128]{1,0:T(8,128)(2,1)}, bf16[2048,128]{1,0:T(8,128)(2,1)S(1)}, u32[]{:S(2)}) copy-start(bf16[2048,128]{1,0:T(8,128)(2,1)S(1)} %constant_dynamic-update-slice_fusion.1) | copy-start | bytes 1572868

commit v5 on v4

--- a/solution.py
+++ b/solution.py
@@ -14,7 +14,7 @@
 WIN = 1024
 BLOCKS = 2
 SWAP = [(0, 1), (1, 0)]
-QUERY_TILE = 1024
+QUERY_TILE = 512
 VMEM = 40 * 1024 * 1024
 
 
@@ -153,6 +153,7 @@
             sums[:HEAD] / sums[HEAD : HEAD + 1]
         ).astype(jnp.bfloat16)
 
+    units.sort(key=lambda unit: unit[4])
     ahead = score(units[0])
     for i, unit in enumerate(units):
         now, ahead = ahead, (score(units[i + 1]) if i + 1 < len(units) else None)
@@ -218,16 +219,17 @@
 ):
     core = lax.axis_index("ch").astype(jnp.int32)
     word = core.reshape(1)
-    weights = []
-    for array in (qkv_weight.transpose(0, 2, 1, 3), out_weight, up_weight, down_weight):
-        weights += [array, swap(array)]
-    send_table = send_rows.reshape(BLOCKS, 2, 1, -1)
+    owned = (qkv_weight.transpose(0, 2, 1, 3), out_weight, up_weight, down_weight)
+    send_table = send_rows.reshape(BLOCKS, 1, 1, -1)
     recv_table = recv_slots.reshape(BLOCKS, 2, 1, WIN)
     picked = pick(word, send_table, 0, None, stream)
     for layer in range(BLOCKS):
         moved = lax.all_to_all(
             picked.reshape(-1, 32, HALF), "pts", split_axis=0, concat_axis=0, tiled=True
         ).reshape(-1, HALF)
+        if layer == 0:
+            moved, *owned = lax.optimization_barrier((moved, *owned))
+            weights = [part for array in owned for part in (array, swap(array))]
         got = swap(pick(word, recv_table, layer, lambda own: 1 - own, moved))
         mine = pick(word, recv_table, layer, lambda own: own, moved)
         keep, give = window_block(layer, word, mine, got, weights, gain_attn, gain_mlp)

time: 124 us -> 122 us (0.984)
  blocking collectives: 36.8 us -> 83.5 us
  waiting for transfers between devices: 29.9 us -> 1.29 us
  starting transfers between devices: 23.5 us -> 6.14 us
  Pallas kernels: 29.8 us -> 27.2 us
    all_to_all x1 -> x2, blocking collectives: 36.8 us -> 83.5 us  [shards(): lax.all_to_all(picked.reshape(-1, 32, HALF), 'pts', split_axis=0, concat_...]
    all_to_all x1 -> x0, waiting for transfers between devices: 28.7 us -> none  [shards(): lax.all_to_all(picked.reshape(-1, 32, HALF), 'pts', split_axis=0, concat_...]
    all_to_all x1 -> x0, starting transfers between devices: 16.5 us -> none  [shards(): lax.all_to_all(picked.reshape(-1, 32, HALF), 'pts', split_axis=0, concat_...]
    pallas_call x7, Pallas kernels: 12.3 us -> 10.6 us  [pick(): pl.pallas_call(functools.partial(pick_kernel, flips, start), grid_spec=pl...]
  transfers between devices with their start and end apart: 9 -> 8, of which waited for: 2 -> 1; matrix products, arithmetic and copies ran while one was open for 0% -> 0% of each run, Pallas kernels for 5% -> 4%
where the time goes in v5:
time: 122 us; the launch traced here: 121 us
  blocking collectives  83.5 us (68%)
  Pallas kernels  27.2 us (22%)
  starting transfers between devices  6.14 us (5%)
  local copies, waits for them, and re-layouts  2.92 us (2%)
  waiting for transfers between devices  1.29 us (1%)
    all_to_all x2, blocking collectives, shards(): lax.all_to_all(picked.reshape(-1, 32, HALF), 'pts', split_axis=0, concat_...  83.5 us
    pallas_call x2, Pallas kernels, window_block(): pl.pallas_call(functools.partial(block_kernel, layer), in_specs=[pl.Block...  16.6 us
    pallas_call x7, Pallas kernels, pick(): pl.pallas_call(functools.partial(pick_kernel, flips, start), grid_spec=pl...  10.6 us
    ppermute x8, starting transfers between devices, swap(): return lax.ppermute(value, 'ch', SWAP)  6.14 us
  transfers between devices with their start and end apart: 8, of which 1 were waited for; matrix products, arithmetic and copies ran while one was open for 0% of the time, Pallas kernels for 4%

profile of v5, /device:TPU:1, one launch (start us, length us, event | category | flops | bytes accessed | tf_op | source)
XLA Modules:
  0.0 121.3 jit_solution(158368380711135640)
XLA Ops:
  0.0 0.9 copy.11
  0.9 0.1 reshape.28.index_ref
  1.0 0.0 copy-start
  1.0 1.0 copy-done
  2.0 2.4 %shard_map.91 = bf16[4096,128]{1,0:T(8,128)(2,1)S(1)} custom-call(s32[1]{0:T(128)} %bitcast.core_ref, s32[2,1,1,4096]{3,2,1,0:T(1,128)S(1)} %reshape.28.index_ref, bf16[2048,128]{1,0:T(8,128)(2,1)S(1)} %copy-done), custom_call_target="tpu_custom_call" | custom-call | flops 4294967296 | bytes 1572864 | tf_op jit(solution)/shard_map/pallas_call | solution.py:55
  4.5 0.0 copy-start.1
  4.5 0.0 copy-start.2
  4.5 0.0 copy-start.8
  4.5 46.5 %all_to_all.10 = bf16[128,32,128]{2,1,0:T(8,128)(2,1)S(1)} all-to-all(bf16[128,32,128]{2,1,0:T(8,128)(2,1)S(1)} %bitcast.11), channel_id=1, replica_groups=mesh['pts'=128,'ch'=2] {'pts'}, dimensions={0} | all-to-all | bytes 2097152 | tf_op jit(solution)/shard_map/all_to_all | solution.py:227
  51.1 0.0 copy-done.1
  51.1 2.6 %collective-permute-start.3 = (bf16[2,256,512]{2,1,0:T(8,128)(2,1)S(1)}, bf16[2,256,512]{2,1,0:T(8,128)(2,1)S(1)}, u32[]{:S(2)}, u32[]{:S(2)}) collective-permute-start(bf16[2,256,512]{2,1,0:T(8,128)(2,1)S(1)} %copy-done.1), channel_id=1, source_target_pairs={{0,1},{1,0},{2,3},{3,2},{4,5},{5,4},{6,7},{7,6},{8,9},{9,8},{10,11... | collective-permute-start | bytes 1572872 | tf_op jit(solution)/shard_map/ppermute | solution.py:22
  53.7 0.0 copy-done.2
  53.7 0.1 collective-permute-start.4
  53.8 0.0 copy-done.8
  53.8 0.0 copy-start.4
  53.8 0.5 collective-permute-start.1
  54.3 1.4 %shard_map.93 = bf16[1024,128]{1,0:T(8,128)(2,1)S(1)} custom-call(s32[1]{0:T(128)} %bitcast.core_ref, s32[2,2,1,1024]{3,2,1,0:T(1,128)S(1)} %reshape.22.index_ref, bf16[4096,128]{1,0:T(8,128)(2,1)S(1)} %bitcast.6), custom_call_target="tpu_custom_call" | custom-call | flops 2147483648 | bytes 1310720 | tf_op jit(solution)/shard_map/pallas_call | solution.py:55
  55.7 0.0 copy-start.3
  55.7 0.0 copy-start.5
  55.7 0.0 copy-start.6
  55.7 0.2 collective-permute-start
  55.9 0.0 copy-done.4
  55.9 0.4 collective-permute-start.2
  56.3 1.4 %shard_map.92.mine_ref = bf16[1024,128]{1,0:T(8,128)(2,1)S(1)} custom-call(s32[1]{0:T(128)} %bitcast.core_ref, s32[2,2,1,1024]{3,2,1,0:T(1,128)S(1)} %reshape.22.index_ref, bf16[4096,128]{1,0:T(8,128)(2,1)S(1)} %bitcast.7), custom_call_target="tpu_custom_call" | custom-call | flops 2147483648 | bytes 1310720 | tf_op jit(solution)/shard_map/pallas_call | solution.py:55
  57.7 0.0 collective-permute-done.2.out_b
  57.7 0.0 collective-permute-done.got_ref
  57.7 0.0 collective-permute-done.1.qkv_b
  57.7 0.0 collective-permute-done.3.up_b
  57.7 0.0 collective-permute-done.4.down_b
  57.7 0.0 copy-done.3
  57.7 0.0 copy-done.5
  57.8 0.0 copy-done.6
  57.8 8.3 %shard_map.94 = (bf16[1024,128]{1,0:T(8,128)(2,1)S(1)}, bf16[1024,128]{1,0:T(8,128)(2,1)S(1)}) custom-call(s32[1]{0:T(128)} %bitcast.core_ref, bf16[1024,128]{1,0:T(8,128)(2,1)S(1)} %shard_map.92.mine_ref, bf16[1024,128]{1,0:T(8,128)(2,1)S(1)} %collective-permute-done.got_ref, bf16[2,3,256,128]{3,2,1,0:T(8,128)(2,1)S(1)} %bitcast.13, ...), custom_call_target="tpu_custom_call" | custom-call | flops 6000000000 | bytes 3000000 | tf_op jit(solution)/shard_map/pallas_call | solution.py:189
  66.1 0.4 collective-permute-start.5
  66.4 1.4 %shard_map.95.refs_0_ = bf16[4096,128]{1,0:T(8,128)(2,1)S(1)} custom-call(s32[1]{0:T(128)} %bitcast.core_ref, s32[2,1,1,4096]{3,2,1,0:T(1,128)S(1)} %reshape.28.index_ref, bf16[1024,128]{1,0:T(8,128)(2,1)S(1)} %get-tuple-element.20.source_ref), custom_call_target="tpu_custom_call" | custom-call | flops 2147483648 | bytes 1310720 | tf_op jit(solution)/shard_map/pallas_call | solution.py:55
  67.8 0.0 collective-permute-done.5.source_ref
  67.8 1.4 %shard_map.96 = bf16[4096,128]{1,0:T(8,128)(2,1)S(1)} custom-call(s32[1]{0:T(128)} %bitcast.core_ref, s32[2,1,1,4096]{3,2,1,0:T(1,128)S(1)} %reshape.28.index_ref, bf16[1024,128]{1,0:T(8,128)(2,1)S(1)} %collective-permute-done.5.source_ref, bf16[4096,128]{1,0:T(8,128)(2,1)S(1)} %shard_map.95.refs_0_), custom_call_target="tpu_custom_call" | custom-call | flops 2147483648 | bytes 1310720 | tf_op jit(solution)/shard_map/pallas_call | solution.py:55
  69.2 37.0 %all_to_all.11 = bf16[128,32,128]{2,1,0:T(8,128)(2,1)S(1)} all-to-all(bf16[128,32,128]{2,1,0:T(8,128)(2,1)S(1)} %bitcast.10), channel_id=1, replica_groups=mesh['pts'=128,'ch'=2] {'pts'}, dimensions={0} | all-to-all | bytes 2097152 | tf_op jit(solution)/shard_map/all_to_all | solution.py:227
  106.2 1.4 %shard_map.98 = bf16[1024,128]{1,0:T(8,128)(2,1)S(1)} custom-call(s32[1]{0:T(128)} %bitcast.core_ref, s32[2,2,1,1024]{3,2,1,0:T(1,128)S(1)} %reshape.22.index_ref, bf16[4096,128]{1,0:T(8,128)(2,1)S(1)} %bitcast.8), custom_call_target="tpu_custom_call" | custom-call | flops 2147483648 | bytes 1310720 | tf_op jit(solution)/shard_map/pallas_call | solution.py:55
  107.6 1.7 %collective-permute-start.6 = (bf16[1024,128]{1,0:T(8,128)(2,1)S(1)}, bf16[1024,128]{1,0:T(8,128)(2,1)S(1)}, u32[]{:S(2)}, u32[]{:S(2)}) collective-permute-start(bf16[1024,128]{1,0:T(8,128)(2,1)S(1)} %shard_map.98), channel_id=1, source_target_pairs={{0,1},{1,0},{2,3},{3,2},{4,5},{5,4},{6,7},{7,6},{8,9},{9,8},{10,11... | collective-permute-start | bytes 786440 | tf_op jit(solution)/shard_map/ppermute | solution.py:22
  109.3 1.4 %shard_map.97.mine_ref = bf16[1024,128]{1,0:T(8,128)(2,1)S(1)} custom-call(s32[1]{0:T(128)} %bitcast.core_ref, s32[2,2,1,1024]{3,2,1,0:T(1,128)S(1)} %reshape.22.index_ref, bf16[4096,128]{1,0:T(8,128)(2,1)S(1)} %bitcast.9), custom_call_target="tpu_custom_call" | custom-call | flops 2147483648 | bytes 1310720 | tf_op jit(solution)/shard_map/pallas_call | solution.py:55
  110.7 0.0 collective-permute-done.6.got_ref
  110.7 8.3 %shard_map.99 = (bf16[1024,128]{1,0:T(8,128)(2,1)S(1)}, bf16[1024,128]{1,0:T(8,128)(2,1)S(1)}) custom-call(s32[1]{0:T(128)} %bitcast.core_ref, bf16[1024,128]{1,0:T(8,128)(2,1)S(1)} %shard_map.97.mine_ref, bf16[1024,128]{1,0:T(8,128)(2,1)S(1)} %collective-permute-done.6.got_ref, bf16[2,3,256,128]{3,2,1,0:T(8,128)(2,1)S(1)} %bitcast.14, ...), custom_call_target="tpu_custom_call" | custom-call | flops 6000000000 | bytes 3000000 | tf_op jit(solution)/shard_map/pallas_call | solution.py:189
  119.0 0.2 collective-permute-start.7
  119.2 0.1 broadcast_in_dim.3
  119.3 0.0 copy-start.7
  119.3 1.3 %collective-permute-done.7 = bf16[1024,128]{1,0:T(8,128)(2,1)S(1)} collective-permute-done((bf16[1024,128]{1,0:T(8,128)(2,1)S(1)}, bf16[1024,128]{1,0:T(8,128)(2,1)S(1)}, u32[]{:S(2)}, u32[]{:S(2)}) %collective-permute-start.7) | collective-permute-done | bytes 262176 | tf_op jit(solution)/shard_map/ppermute | solution.py:22
  120.6 0.0 copy-done.7
  120.6 0.7 constant_dynamic-update-slice_fusion
  (2 shorter events, 0.1 us)
Async XLA Ops:
  1.0 1.0 copy-start
  4.5 46.6 %copy-start.1 = (bf16[2,256,512]{2,1,0:T(8,128)(2,1)S(1)}, bf16[2,256,512]{2,1,0:T(8,128)(2,1)}, u32[]{:S(2)}) copy-start(bf16[2,256,512]{2,1,0:T(8,128)(2,1)} %up_a.1) | copy-start | bytes 1572868
  4.5 49.2 %copy-start.2 = (bf16[2,512,256]{2,1,0:T(8,128)(2,1)S(1)}, bf16[2,512,256]{2,1,0:T(8,128)(2,1)}, u32[]{:S(2)}) copy-start(bf16[2,512,256]{2,1,0:T(8,128)(2,1)} %down_a.1) | copy-start | bytes 1572868
  4.5 49.3 %copy-start.8 = (s32[2,2048]{1,0:T(2,128)S(1)}, s32[2,2048]{1,0:T(2,128)}, u32[]{:S(2)}) copy-start(s32[2,2048]{1,0:T(2,128)} %param.11) | copy-start | bytes 49156
  51.1 6.7 %collective-permute-start.3 = (bf16[2,256,512]{2,1,0:T(8,128)(2,1)S(1)}, bf16[2,256,512]{2,1,0:T(8,128)(2,1)S(1)}, u32[]{:S(2)}, u32[]{:S(2)}) collective-permute-start(bf16[2,256,512]{2,1,0:T(8,128)(2,1)S(1)} %copy-done.1), channel_id=1, source_target_pairs={{0,1},{1,0},{2,3},{3,2},{4,5},{5,4},{6,7},{7,6},{8,9},{9,8},{10,11... | collective-permute-start | bytes 1572872 | tf_op jit(solution)/shard_map/ppermute | solution.py:22
  53.7 4.0 %collective-permute-start.4 = (bf16[2,512,256]{2,1,0:T(8,128)(2,1)S(1)}, bf16[2,512,256]{2,1,0:T(8,128)(2,1)S(1)}, u32[]{:S(2)}, u32[]{:S(2)}) collective-permute-start(bf16[2,512,256]{2,1,0:T(8,128)(2,1)S(1)} %copy-done.2), channel_id=1, source_target_pairs={{0,1},{1,0},{2,3},{3,2},{4,5},{5,4},{6,7},{7,6},{8,9},{9,8},{10,11... | collective-permute-start | bytes 1572872 | tf_op jit(solution)/shard_map/ppermute | solution.py:22
  53.8 2.1 %copy-start.4 = (bf16[2,128,256]{2,1,0:T(8,128)(2,1)S(1)}, bf16[2,128,256]{2,1,0:T(8,128)(2,1)}, u32[]{:S(2)}) copy-start(bf16[2,128,256]{2,1,0:T(8,128)(2,1)} %out_a.1) | copy-start | bytes 393220
  53.8 3.9 %collective-permute-start.1 = (bf16[2,3,256,128]{3,2,1,0:T(8,128)(2,1)}, bf16[2,3,256,128]{3,2,1,0:T(8,128)(2,1)S(1)}, u32[]{:S(2)}, u32[]{:S(2)}) collective-permute-start(bf16[2,3,256,128]{3,2,1,0:T(8,128)(2,1)} %bitcast.12), channel_id=1, source_target_pairs={{0,1},{1,0},{2,3},{3,2},{4,5},{5,4},{6,7},{7,6},{8,9},{9,8},{10,11... | collective-permute-start | bytes 1179656 | tf_op jit(solution)/shard_map/ppermute | solution.py:22
  55.7 2.1 %copy-start.3 = (bf16[2,256,3,128]{3,1,2,0:T(8,128)(2,1)S(1)}, bf16[2,256,3,128]{3,1,2,0:T(8,128)(2,1)}, u32[]{:S(2)}) copy-start(bf16[2,256,3,128]{3,1,2,0:T(8,128)(2,1)} %param.12) | copy-start | bytes 1179652
  55.7 2.0 %copy-start.5 = (f32[2,256]{1,0:T(2,128)S(1)}, f32[2,256]{1,0:T(2,128)}, u32[]{:S(2)}) copy-start(f32[2,256]{1,0:T(2,128)} %gain_a.3) | copy-start | bytes 6148
  55.7 2.0 %copy-start.6 = (f32[2,256]{1,0:T(2,128)S(1)}, f32[2,256]{1,0:T(2,128)}, u32[]{:S(2)}) copy-start(f32[2,256]{1,0:T(2,128)} %gain_m.3) | copy-start | bytes 6148
  55.7 2.0 %collective-permute-start = (bf16[1024,128]{1,0:T(8,128)(2,1)S(1)}, bf16[1024,128]{1,0:T(8,128)(2,1)S(1)}, u32[]{:S(2)}, u32[]{:S(2)}) collective-permute-start(bf16[1024,128]{1,0:T(8,128)(2,1)S(1)} %shard_map.93), channel_id=1, source_target_pairs={{0,1},{1,0},{2,3},{3,2},{4,5},{5,4},{6,7},{7,6},{8,9},{9,8},{10,11... | collective-permute-start | bytes 786440 | tf_op jit(solution)/shard_map/ppermute | solution.py:22
  55.9 1.8 %collective-permute-start.2 = (bf16[2,128,256]{2,1,0:T(8,128)(2,1)S(1)}, bf16[2,128,256]{2,1,0:T(8,128)(2,1)S(1)}, u32[]{:S(2)}, u32[]{:S(2)}) collective-permute-start(bf16[2,128,256]{2,1,0:T(8,128)(2,1)S(1)} %copy-done.4), channel_id=1, source_target_pairs={{0,1},{1,0},{2,3},{3,2},{4,5},{5,4},{6,7},{7,6},{8,9},{9,8},{10,11... | collective-permute-start | bytes 393224 | tf_op jit(solution)/shard_map/ppermute | solution.py:22
  66.1 1.8 %collective-permute-start.5 = (bf16[1024,128]{1,0:T(8,128)(2,1)S(1)}, bf16[1024,128]{1,0:T(8,128)(2,1)S(1)}, u32[]{:S(2)}, u32[]{:S(2)}) collective-permute-start(bf16[1024,128]{1,0:T(8,128)(2,1)S(1)} %get-tuple-element.19), channel_id=1, source_target_pairs={{0,1},{1,0},{2,3},{3,2},{4,5},{5,4},{6,7},{7,6},{8,9},{9,8},{10,11... | collective-permute-start | bytes 786440 | tf_op jit(solution)/shard_map/ppermute | solution.py:22
  107.6 3.1 %collective-permute-start.6 = (bf16[1024,128]{1,0:T(8,128)(2,1)S(1)}, bf16[1024,128]{1,0:T(8,128)(2,1)S(1)}, u32[]{:S(2)}, u32[]{:S(2)}) collective-permute-start(bf16[1024,128]{1,0:T(8,128)(2,1)S(1)} %shard_map.98), channel_id=1, source_target_pairs={{0,1},{1,0},{2,3},{3,2},{4,5},{5,4},{6,7},{7,6},{8,9},{9,8},{10,11... | collective-permute-start | bytes 786440 | tf_op jit(solution)/shard_map/ppermute | solution.py:22
  119.0 1.6 %collective-permute-start.7 = (bf16[1024,128]{1,0:T(8,128)(2,1)S(1)}, bf16[1024,128]{1,0:T(8,128)(2,1)S(1)}, u32[]{:S(2)}, u32[]{:S(2)}) collective-permute-start(bf16[1024,128]{1,0:T(8,128)(2,1)S(1)} %get-tuple-element.22), channel_id=1, source_target_pairs={{0,1},{1,0},{2,3},{3,2},{4,5},{5,4},{6,7},{7,6},{8,9},{9,8},{10,11... | collective-permute-start | bytes 786440 | tf_op jit(solution)/shard_map/ppermute | solution.py:22
  119.3 1.3 %copy-start.7 = (bf16[2048,128]{1,0:T(8,128)(2,1)}, bf16[2048,128]{1,0:T(8,128)(2,1)S(1)}, u32[]{:S(2)}) copy-start(bf16[2048,128]{1,0:T(8,128)(2,1)S(1)} %constant_dynamic-update-slice_fusion.1) | copy-start | bytes 1572868

commit v6 on v5

--- a/solution.py
+++ b/solution.py
@@ -22,9 +22,23 @@
     return lax.ppermute(value, "ch", SWAP)
 
 
+def message_order(table):
+    slots, chips = table.shape
+    lane = lax.broadcasted_iota(jnp.int32, table.shape, 1)
+    slot = lax.broadcasted_iota(jnp.int32, table.shape, 0)
+    wanted = jnp.bitwise_and(lane, slots - 1) == slot
+    group = jnp.right_shift(lane, slots.bit_length() - 1)
+    each = chips // slots
+    parts = []
+    for first in range(0, chips, each):
+        spread = jnp.take_along_axis(table, group + first, axis=1, mode="promise_in_bounds")
+        parts.append(jnp.sum(jnp.where(wanted, spread, 0), axis=0, keepdims=True))
+    return jnp.concatenate(parts, axis=1)
+
+
 def pick_kernel(flips, start, core_ref, index_ref, source_ref, *refs):
     out_ref = refs[-1]
-    index = index_ref[0, 0]
+    index = index_ref[0, 0] if len(index_ref.shape) == 4 else message_order(index_ref[0])
     if flips:
         index = jnp.bitwise_xor(index, core_ref[0] * WIN)
     index = index.astype(jnp.int16)
@@ -43,32 +57,33 @@
 
 
 def pick(core, table, layer, part, source, others=None, start=0, flips=False):
-    tile = table.shape[3]
-    steps = table.shape[1] if part is None else 1
+    tile = table.shape[3] if len(table.shape) == 4 else table.shape[1] * table.shape[2]
     depth = source.shape[0]
     rows = pl.BlockSpec((tile, HALF), lambda i, word: (i, 0))
 
     def block(i, word):
-        return (layer, i if part is None else part(word[0]), 0, 0)
+        return (layer, 0, 0) if part is None else (layer, part(word[0]), 0, 0)
+
+    index_spec = pl.BlockSpec((1,) * (2 if part else 1) + table.shape[2 if part else 1 :], block)
 
     more = [] if others is None else [others]
     return pl.pallas_call(
         functools.partial(pick_kernel, flips, start),
         grid_spec=pltpu.PrefetchScalarGridSpec(
             num_scalar_prefetch=1,
-            grid=(steps,),
+            grid=(1,),
             in_specs=[
-                pl.BlockSpec((1, 1, 1, tile), block),
+                index_spec,
                 pl.BlockSpec(source.shape, lambda i, word: (0, 0)),
             ]
             + [rows] * len(more),
             out_specs=rows,
         ),
-        out_shape=jax.ShapeDtypeStruct((steps * tile, HALF), jnp.bfloat16),
+        out_shape=jax.ShapeDtypeStruct((tile, HALF), jnp.bfloat16),
         compiler_params=pltpu.CompilerParams(vmem_limit_bytes=VMEM),
         cost_estimate=pl.CostEstimate(
-            flops=4 * steps * tile * depth * HALF,
-            bytes_accessed=(steps * tile + depth) * 256,
+            flops=4 * tile * depth * HALF,
+            bytes_accessed=(tile + depth) * 256,
             transcendentals=0,
         ),
     )(core, table, source, *more)
@@ -220,7 +235,7 @@
     core = lax.axis_index("ch").astype(jnp.int32)
     word = core.reshape(1)
     owned = (qkv_weight.transpose(0, 2, 1, 3), out_weight, up_weight, down_weight)
-    send_table = send_rows.reshape(BLOCKS, 1, 1, -1)
+    send_table = send_rows.transpose(0, 2, 1)
     recv_table = recv_slots.reshape(BLOCKS, 2, 1, WIN)
     picked = pick(word, send_table, 0, None, stream)
     for layer in range(BLOCKS):

time: 122 us -> 123 us (level)
  transfers between devices with their start and end apart: 8 -> 8, of which waited for: 1 -> 1; matrix products, arithmetic and copies ran while one was open for 0% -> 1% of each run, Pallas kernels for 4% -> 4%
where the time goes in v6:
time: 123 us; the launch traced here: 122 us
  blocking collectives  83.3 us (68%)
  Pallas kernels  27.4 us (22%)
  starting transfers between devices  6.62 us (5%)
  local copies, waits for them, and re-layouts  3.43 us (3%)
  waiting for transfers between devices  1.29 us (1%)
    all_to_all x2, blocking collectives, shards(): lax.all_to_all(picked.reshape(-1, 32, HALF), 'pts', split_axis=0, concat_...  83.3 us
    pallas_call x2, Pallas kernels, window_block(): pl.pallas_call(functools.partial(block_kernel, layer), in_specs=[pl.Block...  16.6 us
    pallas_call x7, Pallas kernels, pick(): pl.pallas_call(functools.partial(pick_kernel, flips, start), grid_spec=pl...  10.8 us
    ppermute x8, starting transfers between devices, swap(): return lax.ppermute(value, 'ch', SWAP)  6.62 us
  transfers between devices with their start and end apart: 8, of which 1 were waited for; matrix products, arithmetic and copies ran while one was open for 1% of the time, Pallas kernels for 4%

profile of v6, /device:TPU:1, one launch (start us, length us, event | category | flops | bytes accessed | tf_op | source)
XLA Modules:
  0.0 122.3 jit_solution(14468086998885293338)
XLA Ops:
  0.0 0.0 copy-start
  0.0 1.0 copy-done
  1.0 0.0 copy-start.5
  1.0 0.8 copy-done.5
  1.8 2.5 %shard_map.91 = bf16[4096,128]{1,0:T(8,128)(2,1)S(1)} custom-call(s32[1]{0:T(128)} %bitcast.core_ref, s32[2,32,128]{2,1,0:T(8,128)S(1)} %bitcast.16, bf16[2048,128]{1,0:T(8,128)(2,1)S(1)} %copy-done), custom_call_target="tpu_custom_call" | custom-call | flops 4294967296 | bytes 1572864 | tf_op jit(solution)/shard_map/pallas_call | solution.py:70
  4.3 0.0 copy-start.1
  4.3 0.0 copy-start.2
  4.3 0.0 copy-start.3
  4.3 46.5 %all_to_all.10 = bf16[128,32,128]{2,1,0:T(8,128)(2,1)S(1)} all-to-all(bf16[128,32,128]{2,1,0:T(8,128)(2,1)S(1)} %bitcast.12), channel_id=1, replica_groups=mesh['pts'=128,'ch'=2] {'pts'}, dimensions={0} | all-to-all | bytes 2097152 | tf_op jit(solution)/shard_map/all_to_all | solution.py:242
  50.9 0.0 copy-done.1
  50.9 2.6 %collective-permute-start.3 = (bf16[2,256,512]{2,1,0:T(8,128)(2,1)S(1)}, bf16[2,256,512]{2,1,0:T(8,128)(2,1)S(1)}, u32[]{:S(2)}, u32[]{:S(2)}) collective-permute-start(bf16[2,256,512]{2,1,0:T(8,128)(2,1)S(1)} %copy-done.1), channel_id=1, source_target_pairs={{0,1},{1,0},{2,3},{3,2},{4,5},{5,4},{6,7},{7,6},{8,9},{9,8},{10,11... | collective-permute-start | bytes 1572872 | tf_op jit(solution)/shard_map/ppermute | solution.py:22
  53.5 0.0 copy-done.2
  53.5 0.1 collective-permute-start.4
  53.6 0.7 reshape.19.index_ref
  54.3 0.0 copy-done.3
  54.4 0.0 copy-start.4
  54.4 0.5 collective-permute-start.1
  54.9 1.4 %shard_map.93 = bf16[1024,128]{1,0:T(8,128)(2,1)S(1)} custom-call(s32[1]{0:T(128)} %bitcast.core_ref, s32[2,2,1,1024]{3,2,1,0:T(1,128)S(1)} %reshape.19.index_ref, bf16[4096,128]{1,0:T(8,128)(2,1)S(1)} %bitcast.7), custom_call_target="tpu_custom_call" | custom-call | flops 2147483648 | bytes 1310720 | tf_op jit(solution)/shard_map/pallas_call | solution.py:70
  56.2 0.0 copy-start.7
  56.2 0.0 copy-start.8
  56.3 0.2 collective-permute-start
  56.4 0.0 copy-done.4
  56.4 0.4 collective-permute-start.2
  56.9 1.4 %shard_map.92.mine_ref = bf16[1024,128]{1,0:T(8,128)(2,1)S(1)} custom-call(s32[1]{0:T(128)} %bitcast.core_ref, s32[2,2,1,1024]{3,2,1,0:T(1,128)S(1)} %reshape.19.index_ref, bf16[4096,128]{1,0:T(8,128)(2,1)S(1)} %bitcast.8), custom_call_target="tpu_custom_call" | custom-call | flops 2147483648 | bytes 1310720 | tf_op jit(solution)/shard_map/pallas_call | solution.py:70
  58.2 0.0 copy-start.6
  58.2 0.0 collective-permute-done.2.out_b
  58.2 0.0 collective-permute-done.got_ref
  58.3 0.0 collective-permute-done.1.qkv_b
  58.3 0.0 collective-permute-done.3.up_b
  58.3 0.0 collective-permute-done.4.down_b
  58.3 0.0 copy-done.7
  58.3 0.0 copy-done.8
  58.3 8.3 %shard_map.94 = (bf16[1024,128]{1,0:T(8,128)(2,1)S(1)}, bf16[1024,128]{1,0:T(8,128)(2,1)S(1)}) custom-call(s32[1]{0:T(128)} %bitcast.core_ref, bf16[1024,128]{1,0:T(8,128)(2,1)S(1)} %shard_map.92.mine_ref, bf16[1024,128]{1,0:T(8,128)(2,1)S(1)} %collective-permute-done.got_ref, bf16[2,3,256,128]{3,2,1,0:T(8,128)(2,1)S(1)} %bitcast.14, ...), custom_call_target="tpu_custom_call" | custom-call | flops 6000000000 | bytes 3000000 | tf_op jit(solution)/shard_map/pallas_call | solution.py:204
  66.6 0.6 collective-permute-start.5
  67.2 0.0 copy-done.6
  67.2 1.4 %shard_map.95.refs_0_ = bf16[4096,128]{1,0:T(8,128)(2,1)S(1)} custom-call(s32[1]{0:T(128)} %bitcast.core_ref, s32[2,32,128]{2,1,0:T(8,128)S(1)} %bitcast.17, bf16[1024,128]{1,0:T(8,128)(2,1)S(1)} %get-tuple-element.20.source_ref), custom_call_target="tpu_custom_call" | custom-call | flops 2147483648 | bytes 1310720 | tf_op jit(solution)/shard_map/pallas_call | solution.py:70
  68.6 0.0 collective-permute-done.5.source_ref
  68.7 1.4 %shard_map.96 = bf16[4096,128]{1,0:T(8,128)(2,1)S(1)} custom-call(s32[1]{0:T(128)} %bitcast.core_ref, s32[2,32,128]{2,1,0:T(8,128)S(1)} %bitcast.18, bf16[1024,128]{1,0:T(8,128)(2,1)S(1)} %collective-permute-done.5.source_ref, bf16[4096,128]{1,0:T(8,128)(2,1)S(1)} %shard_map.95.refs_0_), custom_call_target="tpu_custom_call" | custom-call | flops 2147483648 | bytes 1310720 | tf_op jit(solution)/shard_map/pallas_call | solution.py:70
  70.1 36.8 %all_to_all.11 = bf16[128,32,128]{2,1,0:T(8,128)(2,1)S(1)} all-to-all(bf16[128,32,128]{2,1,0:T(8,128)(2,1)S(1)} %bitcast.11), channel_id=1, replica_groups=mesh['pts'=128,'ch'=2] {'pts'}, dimensions={0} | all-to-all | bytes 2097152 | tf_op jit(solution)/shard_map/all_to_all | solution.py:242
  106.9 1.4 %shard_map.98 = bf16[1024,128]{1,0:T(8,128)(2,1)S(1)} custom-call(s32[1]{0:T(128)} %bitcast.core_ref, s32[2,2,1,1024]{3,2,1,0:T(1,128)S(1)} %reshape.19.index_ref, bf16[4096,128]{1,0:T(8,128)(2,1)S(1)} %bitcast.9), custom_call_target="tpu_custom_call" | custom-call | flops 2147483648 | bytes 1310720 | tf_op jit(solution)/shard_map/pallas_call | solution.py:70
  108.2 2.0 %collective-permute-start.6 = (bf16[1024,128]{1,0:T(8,128)(2,1)S(1)}, bf16[1024,128]{1,0:T(8,128)(2,1)S(1)}, u32[]{:S(2)}, u32[]{:S(2)}) collective-permute-start(bf16[1024,128]{1,0:T(8,128)(2,1)S(1)} %shard_map.98), channel_id=1, source_target_pairs={{0,1},{1,0},{2,3},{3,2},{4,5},{5,4},{6,7},{7,6},{8,9},{9,8},{10,11... | collective-permute-start | bytes 786440 | tf_op jit(solution)/shard_map/ppermute | solution.py:22
  110.2 1.4 %shard_map.97.mine_ref = bf16[1024,128]{1,0:T(8,128)(2,1)S(1)} custom-call(s32[1]{0:T(128)} %bitcast.core_ref, s32[2,2,1,1024]{3,2,1,0:T(1,128)S(1)} %reshape.19.index_ref, bf16[4096,128]{1,0:T(8,128)(2,1)S(1)} %bitcast.10), custom_call_target="tpu_custom_call" | custom-call | flops 2147483648 | bytes 1310720 | tf_op jit(solution)/shard_map/pallas_call | solution.py:70
  111.6 0.0 collective-permute-done.6.got_ref
  111.6 8.3 %shard_map.99 = (bf16[1024,128]{1,0:T(8,128)(2,1)S(1)}, bf16[1024,128]{1,0:T(8,128)(2,1)S(1)}) custom-call(s32[1]{0:T(128)} %bitcast.core_ref, bf16[1024,128]{1,0:T(8,128)(2,1)S(1)} %shard_map.97.mine_ref, bf16[1024,128]{1,0:T(8,128)(2,1)S(1)} %collective-permute-done.6.got_ref, bf16[2,3,256,128]{3,2,1,0:T(8,128)(2,1)S(1)} %bitcast.15, ...), custom_call_target="tpu_custom_call" | custom-call | flops 6000000000 | bytes 3000000 | tf_op jit(solution)/shard_map/pallas_call | solution.py:204
  119.9 0.2 collective-permute-start.7
  120.1 0.1 broadcast_in_dim.3
  120.2 0.0 copy-start.9
  120.3 1.3 %collective-permute-done.7 = bf16[1024,128]{1,0:T(8,128)(2,1)S(1)} collective-permute-done((bf16[1024,128]{1,0:T(8,128)(2,1)S(1)}, bf16[1024,128]{1,0:T(8,128)(2,1)S(1)}, u32[]{:S(2)}, u32[]{:S(2)}) %collective-permute-start.7) | collective-permute-done | bytes 262176 | tf_op jit(solution)/shard_map/ppermute | solution.py:22
  121.5 0.0 copy-done.9
  121.5 0.7 constant_dynamic-update-slice_fusion
  (1 shorter events, 0.0 us)
Async XLA Ops:
  0.0 1.0 copy-start
  1.0 0.8 copy-start.5
  4.3 46.6 %copy-start.1 = (bf16[2,256,512]{2,1,0:T(8,128)(2,1)S(1)}, bf16[2,256,512]{2,1,0:T(8,128)(2,1)}, u32[]{:S(2)}) copy-start(bf16[2,256,512]{2,1,0:T(8,128)(2,1)} %up_a.1) | copy-start | bytes 1572868
  4.3 49.2 %copy-start.2 = (bf16[2,512,256]{2,1,0:T(8,128)(2,1)S(1)}, bf16[2,512,256]{2,1,0:T(8,128)(2,1)}, u32[]{:S(2)}) copy-start(bf16[2,512,256]{2,1,0:T(8,128)(2,1)} %down_a.1) | copy-start | bytes 1572868
  4.3 50.0 %copy-start.3 = (bf16[2,256,3,128]{3,1,2,0:T(8,128)(2,1)S(1)}, bf16[2,256,3,128]{3,1,2,0:T(8,128)(2,1)}, u32[]{:S(2)}) copy-start(bf16[2,256,3,128]{3,1,2,0:T(8,128)(2,1)} %param.12) | copy-start | bytes 1179652
  50.9 7.4 %collective-permute-start.3 = (bf16[2,256,512]{2,1,0:T(8,128)(2,1)S(1)}, bf16[2,256,512]{2,1,0:T(8,128)(2,1)S(1)}, u32[]{:S(2)}, u32[]{:S(2)}) collective-permute-start(bf16[2,256,512]{2,1,0:T(8,128)(2,1)S(1)} %copy-done.1), channel_id=1, source_target_pairs={{0,1},{1,0},{2,3},{3,2},{4,5},{5,4},{6,7},{7,6},{8,9},{9,8},{10,11... | collective-permute-start | bytes 1572872 | tf_op jit(solution)/shard_map/ppermute | solution.py:22
  53.5 4.8 %collective-permute-start.4 = (bf16[2,512,256]{2,1,0:T(8,128)(2,1)S(1)}, bf16[2,512,256]{2,1,0:T(8,128)(2,1)S(1)}, u32[]{:S(2)}, u32[]{:S(2)}) collective-permute-start(bf16[2,512,256]{2,1,0:T(8,128)(2,1)S(1)} %copy-done.2), channel_id=1, source_target_pairs={{0,1},{1,0},{2,3},{3,2},{4,5},{5,4},{6,7},{7,6},{8,9},{9,8},{10,11... | collective-permute-start | bytes 1572872 | tf_op jit(solution)/shard_map/ppermute | solution.py:22
  54.4 2.1 %copy-start.4 = (bf16[2,128,256]{2,1,0:T(8,128)(2,1)S(1)}, bf16[2,128,256]{2,1,0:T(8,128)(2,1)}, u32[]{:S(2)}) copy-start(bf16[2,128,256]{2,1,0:T(8,128)(2,1)} %out_a.1) | copy-start | bytes 393220
  54.4 3.9 %collective-permute-start.1 = (bf16[2,3,256,128]{3,2,1,0:T(8,128)(2,1)S(1)}, bf16[2,3,256,128]{3,2,1,0:T(8,128)(2,1)S(1)}, u32[]{:S(2)}, u32[]{:S(2)}) collective-permute-start(bf16[2,3,256,128]{3,2,1,0:T(8,128)(2,1)S(1)} %bitcast.13), channel_id=1, source_target_pairs={{0,1},{1,0},{2,3},{3,2},{4,5},{5,4},{6,7},{7,6},{8,9},{9,8},{10,11... | collective-permute-start | bytes 1179656 | tf_op jit(solution)/shard_map/ppermute | solution.py:22
  56.2 2.1 %copy-start.7 = (f32[2,256]{1,0:T(2,128)S(1)}, f32[2,256]{1,0:T(2,128)}, u32[]{:S(2)}) copy-start(f32[2,256]{1,0:T(2,128)} %gain_a.3) | copy-start | bytes 6148
  56.2 2.1 %copy-start.8 = (f32[2,256]{1,0:T(2,128)S(1)}, f32[2,256]{1,0:T(2,128)}, u32[]{:S(2)}) copy-start(f32[2,256]{1,0:T(2,128)} %gain_m.3) | copy-start | bytes 6148
  56.3 2.0 %collective-permute-start = (bf16[1024,128]{1,0:T(8,128)(2,1)S(1)}, bf16[1024,128]{1,0:T(8,128)(2,1)S(1)}, u32[]{:S(2)}, u32[]{:S(2)}) collective-permute-start(bf16[1024,128]{1,0:T(8,128)(2,1)S(1)} %shard_map.93), channel_id=1, source_target_pairs={{0,1},{1,0},{2,3},{3,2},{4,5},{5,4},{6,7},{7,6},{8,9},{9,8},{10,11... | collective-permute-start | bytes 786440 | tf_op jit(solution)/shard_map/ppermute | solution.py:22
  56.4 1.8 %collective-permute-start.2 = (bf16[2,128,256]{2,1,0:T(8,128)(2,1)S(1)}, bf16[2,128,256]{2,1,0:T(8,128)(2,1)S(1)}, u32[]{:S(2)}, u32[]{:S(2)}) collective-permute-start(bf16[2,128,256]{2,1,0:T(8,128)(2,1)S(1)} %copy-done.4), channel_id=1, source_target_pairs={{0,1},{1,0},{2,3},{3,2},{4,5},{5,4},{6,7},{7,6},{8,9},{9,8},{10,11... | collective-permute-start | bytes 393224 | tf_op jit(solution)/shard_map/ppermute | solution.py:22
  58.2 9.0 %copy-start.6 = (s32[2,128,32]{1,2,0:T(8,128)S(1)}, s32[2,128,32]{1,2,0:T(8,128)}, u32[]{:S(2)}) copy-start(s32[2,128,32]{1,2,0:T(8,128)} %param.10) | copy-start | bytes 98308
  66.6 2.0 %collective-permute-start.5 = (bf16[1024,128]{1,0:T(8,128)(2,1)S(1)}, bf16[1024,128]{1,0:T(8,128)(2,1)S(1)}, u32[]{:S(2)}, u32[]{:S(2)}) collective-permute-start(bf16[1024,128]{1,0:T(8,128)(2,1)S(1)} %get-tuple-element.19), channel_id=1, source_target_pairs={{0,1},{1,0},{2,3},{3,2},{4,5},{5,4},{6,7},{7,6},{8,9},{9,8},{10,11... | collective-permute-start | bytes 786440 | tf_op jit(solution)/shard_map/ppermute | solution.py:22
  108.2 3.4 %collective-permute-start.6 = (bf16[1024,128]{1,0:T(8,128)(2,1)S(1)}, bf16[1024,128]{1,0:T(8,128)(2,1)S(1)}, u32[]{:S(2)}, u32[]{:S(2)}) collective-permute-start(bf16[1024,128]{1,0:T(8,128)(2,1)S(1)} %shard_map.98), channel_id=1, source_target_pairs={{0,1},{1,0},{2,3},{3,2},{4,5},{5,4},{6,7},{7,6},{8,9},{9,8},{10,11... | collective-permute-start | bytes 786440 | tf_op jit(solution)/shard_map/ppermute | solution.py:22
  119.9 1.6 %collective-permute-start.7 = (bf16[1024,128]{1,0:T(8,128)(2,1)S(1)}, bf16[1024,128]{1,0:T(8,128)(2,1)S(1)}, u32[]{:S(2)}, u32[]{:S(2)}) collective-permute-start(bf16[1024,128]{1,0:T(8,128)(2,1)S(1)} %get-tuple-element.22), channel_id=1, source_target_pairs={{0,1},{1,0},{2,3},{3,2},{4,5},{5,4},{6,7},{7,6},{8,9},{9,8},{10,11... | collective-permute-start | bytes 786440 | tf_op jit(solution)/shard_map/ppermute | solution.py:22
  120.2 1.3 %copy-start.9 = (bf16[2048,128]{1,0:T(8,128)(2,1)}, bf16[2048,128]{1,0:T(8,128)(2,1)S(1)}, u32[]{:S(2)}) copy-start(bf16[2048,128]{1,0:T(8,128)(2,1)S(1)} %constant_dynamic-update-slice_fusion.1) | copy-start | bytes 1572868

commit v7 on v5

--- a/solution.py
+++ b/solution.py
@@ -72,6 +72,53 @@
             transcendentals=0,
         ),
     )(core, table, source, *more)
+
+
+def first_pick_kernel(index_ref, stream_ref, out_ref, held, arrived):
+    copies = [
+        pltpu.make_async_copy(stream_ref.at[pl.ds(k * WIN, WIN)], held.at[k], arrived.at[k])
+        for k in range(2)
+    ]
+    for copy in copies:
+        copy.start()
+    index = index_ref[0, 0].astype(jnp.int16)
+    shape = (WIN, index.shape[1])
+    total = None
+    for k, copy in enumerate(copies):
+        row = lax.broadcasted_iota(jnp.int16, shape, 0) + jnp.int16(k * WIN)
+        hot = jnp.where(
+            jnp.broadcast_to(index, shape) == row,
+            jnp.ones(shape, jnp.bfloat16),
+            jnp.zeros(shape, jnp.bfloat16),
+        )
+        copy.wait()
+        part = lax.dot_general(
+            held[k], hot, (((0,), (0,)), ((), ())), preferred_element_type=jnp.float32
+        )
+        total = part if total is None else total + part
+    out_ref[...] = total.T.astype(jnp.bfloat16)
+
+
+def first_pick(table, stream):
+    tile = table.shape[3]
+    return pl.pallas_call(
+        first_pick_kernel,
+        grid=(1,),
+        in_specs=[
+            pl.BlockSpec((1, 1, 1, tile), lambda i: (0, 0, 0, 0)),
+            pl.BlockSpec(memory_space=pltpu.HBM),
+        ],
+        out_specs=pl.BlockSpec((tile, HALF), lambda i: (0, 0)),
+        out_shape=jax.ShapeDtypeStruct((tile, HALF), jnp.bfloat16),
+        scratch_shapes=[
+            pltpu.VMEM((2, WIN, HALF), jnp.bfloat16),
+            pltpu.SemaphoreType.DMA((2,)),
+        ],
+        compiler_params=pltpu.CompilerParams(vmem_limit_bytes=60 * 1024 * 1024),
+        cost_estimate=pl.CostEstimate(
+            flops=8 * tile * WIN * HALF, bytes_accessed=tile * 384, transcendentals=0
+        ),
+    )(table, stream)
 
 
 def layer_norm(values, gain):
@@ -222,7 +269,7 @@
     owned = (qkv_weight.transpose(0, 2, 1, 3), out_weight, up_weight, down_weight)
     send_table = send_rows.reshape(BLOCKS, 1, 1, -1)
     recv_table = recv_slots.reshape(BLOCKS, 2, 1, WIN)
-    picked = pick(word, send_table, 0, None, stream)
+    picked = first_pick(send_table, stream)
     for layer in range(BLOCKS):
         moved = lax.all_to_all(
             picked.reshape(-1, 32, HALF), "pts", split_axis=0, concat_axis=0, tiled=True

time: 122 us -> 125 us (1.025)
  Pallas kernels: 27.2 us -> 30.2 us
    pallas_call x0 -> x1, Pallas kernels: none -> 5.45 us  [first_pick(): pl.pallas_call(first_pick_kernel, grid=(1,), in_specs=[pl.BlockSpec((1, 1...]
    pallas_call x7 -> x6, Pallas kernels: 10.6 us -> 8.16 us  [pick(): pl.pallas_call(functools.partial(pick_kernel, flips, start), grid_spec=pl...]
  transfers between devices with their start and end apart: 8 -> 8, of which waited for: 1 -> 1; matrix products, arithmetic and copies ran while one was open for 0% -> 1% of each run, Pallas kernels for 4% -> 4%
where the time goes in v7:
time: 125 us
  blocking collectives  83.7 us (67%)
  Pallas kernels  30.2 us (24%)
  starting transfers between devices  6.12 us (5%)
  local copies, waits for them, and re-layouts  3.21 us (3%)
  waiting for transfers between devices  1.31 us (1%)
    all_to_all x2, blocking collectives, shards(): lax.all_to_all(picked.reshape(-1, 32, HALF), 'pts', split_axis=0, concat_...  83.7 us
    pallas_call x2, Pallas kernels, window_block(): pl.pallas_call(functools.partial(block_kernel, layer), in_specs=[pl.Block...  16.6 us
    pallas_call x6, Pallas kernels, pick(): pl.pallas_call(functools.partial(pick_kernel, flips, start), grid_spec=pl...  8.16 us
    ppermute x8, starting transfers between devices, swap(): return lax.ppermute(value, 'ch', SWAP)  6.12 us
    pallas_call x1, Pallas kernels, first_pick(): pl.pallas_call(first_pick_kernel, grid=(1,), in_specs=[pl.BlockSpec((1, 1...  5.45 us
  transfers between devices with their start and end apart: 8, of which 1 were waited for; matrix products, arithmetic and copies ran while one was open for 1% of the time, Pallas kernels for 4%

profile of v7, /device:TPU:1, one launch (start us, length us, event | category | flops | bytes accessed | tf_op | source)
XLA Modules:
  0.0 124.8 jit_solution(10173103597226566783)
XLA Ops:
  0.0 0.9 copy.11
  0.9 0.7 reshape.28.index_ref
  1.6 5.5 %shard_map.91 = bf16[4096,128]{1,0:T(8,128)(2,1)} custom-call(s32[2,1,1,4096]{3,2,1,0:T(1,128)} %reshape.28.index_ref, bf16[2048,128]{1,0:T(8,128)(2,1)} %stream_ref.1), custom_call_target="tpu_custom_call" | custom-call | flops 4294967296 | bytes 1572864 | tf_op jit(solution)/shard_map/pallas_call | solution.py:104
  7.1 0.0 copy-start.1
  7.1 0.0 copy-start.2
  7.1 0.0 copy-start.3
  7.1 46.7 %all_to_all.10 = bf16[128,32,128]{2,1,0:T(8,128)(2,1)S(1)} all-to-all(bf16[128,32,128]{2,1,0:T(8,128)(2,1)} %bitcast.14), channel_id=1, replica_groups=mesh['pts'=128,'ch'=2] {'pts'}, dimensions={0} | all-to-all | bytes 2097152 | tf_op jit(solution)/shard_map/all_to_all | solution.py:274
  53.8 0.0 copy-done.1
  53.8 2.6 %collective-permute-start.3 = (bf16[2,256,512]{2,1,0:T(8,128)(2,1)S(1)}, bf16[2,256,512]{2,1,0:T(8,128)(2,1)S(1)}, u32[]{:S(2)}, u32[]{:S(2)}) collective-permute-start(bf16[2,256,512]{2,1,0:T(8,128)(2,1)S(1)} %copy-done.1), channel_id=1, source_target_pairs={{0,1},{1,0},{2,3},{3,2},{4,5},{5,4},{6,7},{7,6},{8,9},{9,8},{10,11... | collective-permute-start | bytes 1572872 | tf_op jit(solution)/shard_map/ppermute | solution.py:22
  56.5 0.0 copy-done.2
  56.5 0.1 collective-permute-start.4
  56.5 0.7 reshape.22.index_ref
  57.3 0.0 copy-done.3
  57.3 0.5 collective-permute-start.1
  57.8 0.0 copy-start.4
  57.8 1.4 %shard_map.93 = bf16[1024,128]{1,0:T(8,128)(2,1)S(1)} custom-call(s32[1]{0:T(128)} %bitcast.core_ref, s32[2,2,1,1024]{3,2,1,0:T(1,128)S(1)} %reshape.22.index_ref, bf16[4096,128]{1,0:T(8,128)(2,1)S(1)} %bitcast.6), custom_call_target="tpu_custom_call" | custom-call | flops 2147483648 | bytes 1310720 | tf_op jit(solution)/shard_map/pallas_call | solution.py:55
  59.2 0.0 copy-start.5
  59.2 0.0 copy-start.6
  59.2 0.2 collective-permute-start
  59.4 0.0 copy-done.4
  59.4 0.4 collective-permute-start.2
  59.8 1.4 %shard_map.92.mine_ref = bf16[1024,128]{1,0:T(8,128)(2,1)S(1)} custom-call(s32[1]{0:T(128)} %bitcast.core_ref, s32[2,2,1,1024]{3,2,1,0:T(1,128)S(1)} %reshape.22.index_ref, bf16[4096,128]{1,0:T(8,128)(2,1)S(1)} %bitcast.7), custom_call_target="tpu_custom_call" | custom-call | flops 2147483648 | bytes 1310720 | tf_op jit(solution)/shard_map/pallas_call | solution.py:55
  61.2 0.0 copy-start
  61.2 0.0 collective-permute-done.2.out_b
  61.2 0.0 collective-permute-done.got_ref
  61.2 0.0 collective-permute-done.1.qkv_b
  61.2 0.0 collective-permute-done.3.up_b
  61.2 0.0 collective-permute-done.4.down_b
  61.2 0.0 copy-done.5
  61.2 0.0 copy-done.6
  61.2 8.3 %shard_map.94 = (bf16[1024,128]{1,0:T(8,128)(2,1)S(1)}, bf16[1024,128]{1,0:T(8,128)(2,1)S(1)}) custom-call(s32[1]{0:T(128)} %bitcast.core_ref, bf16[1024,128]{1,0:T(8,128)(2,1)S(1)} %shard_map.92.mine_ref, bf16[1024,128]{1,0:T(8,128)(2,1)S(1)} %collective-permute-done.got_ref, bf16[2,3,256,128]{3,2,1,0:T(8,128)(2,1)S(1)} %bitcast.12, ...), custom_call_target="tpu_custom_call" | custom-call | flops 6000000000 | bytes 3000000 | tf_op jit(solution)/shard_map/pallas_call | solution.py:236
  69.5 0.4 collective-permute-start.5
  69.9 0.0 copy-done
  69.9 1.4 %shard_map.95.refs_0_ = bf16[4096,128]{1,0:T(8,128)(2,1)S(1)} custom-call(s32[1]{0:T(128)} %bitcast.core_ref, s32[2,1,1,4096]{3,2,1,0:T(1,128)S(1)} %copy-done, bf16[1024,128]{1,0:T(8,128)(2,1)S(1)} %get-tuple-element.20.source_ref), custom_call_target="tpu_custom_call" | custom-call | flops 2147483648 | bytes 1310720 | tf_op jit(solution)/shard_map/pallas_call | solution.py:55
  71.3 0.0 collective-permute-done.5.source_ref
  71.3 1.4 %shard_map.96 = bf16[4096,128]{1,0:T(8,128)(2,1)S(1)} custom-call(s32[1]{0:T(128)} %bitcast.core_ref, s32[2,1,1,4096]{3,2,1,0:T(1,128)S(1)} %copy-done, bf16[1024,128]{1,0:T(8,128)(2,1)S(1)} %collective-permute-done.5.source_ref, bf16[4096,128]{1,0:T(8,128)(2,1)S(1)} %shard_map.95.refs_0_), custom_call_target="tpu_custom_call" | custom-call | flops 2147483648 | bytes 1310720 | tf_op jit(solution)/shard_map/pallas_call | solution.py:55
  72.7 37.0 %all_to_all.11 = bf16[128,32,128]{2,1,0:T(8,128)(2,1)S(1)} all-to-all(bf16[128,32,128]{2,1,0:T(8,128)(2,1)S(1)} %bitcast.10), channel_id=1, replica_groups=mesh['pts'=128,'ch'=2] {'pts'}, dimensions={0} | all-to-all | bytes 2097152 | tf_op jit(solution)/shard_map/all_to_all | solution.py:274
  109.7 1.4 %shard_map.98 = bf16[1024,128]{1,0:T(8,128)(2,1)S(1)} custom-call(s32[1]{0:T(128)} %bitcast.core_ref, s32[2,2,1,1024]{3,2,1,0:T(1,128)S(1)} %reshape.22.index_ref, bf16[4096,128]{1,0:T(8,128)(2,1)S(1)} %bitcast.8), custom_call_target="tpu_custom_call" | custom-call | flops 2147483648 | bytes 1310720 | tf_op jit(solution)/shard_map/pallas_call | solution.py:55
  111.1 1.7 %collective-permute-start.6 = (bf16[1024,128]{1,0:T(8,128)(2,1)S(1)}, bf16[1024,128]{1,0:T(8,128)(2,1)S(1)}, u32[]{:S(2)}, u32[]{:S(2)}) collective-permute-start(bf16[1024,128]{1,0:T(8,128)(2,1)S(1)} %shard_map.98), channel_id=1, source_target_pairs={{0,1},{1,0},{2,3},{3,2},{4,5},{5,4},{6,7},{7,6},{8,9},{9,8},{10,11... | collective-permute-start | bytes 786440 | tf_op jit(solution)/shard_map/ppermute | solution.py:22
  112.8 1.4 %shard_map.97.mine_ref = bf16[1024,128]{1,0:T(8,128)(2,1)S(1)} custom-call(s32[1]{0:T(128)} %bitcast.core_ref, s32[2,2,1,1024]{3,2,1,0:T(1,128)S(1)} %reshape.22.index_ref, bf16[4096,128]{1,0:T(8,128)(2,1)S(1)} %bitcast.9), custom_call_target="tpu_custom_call" | custom-call | flops 2147483648 | bytes 1310720 | tf_op jit(solution)/shard_map/pallas_call | solution.py:55
  114.1 0.0 collective-permute-done.6.got_ref
  114.2 8.3 %shard_map.99 = (bf16[1024,128]{1,0:T(8,128)(2,1)S(1)}, bf16[1024,128]{1,0:T(8,128)(2,1)S(1)}) custom-call(s32[1]{0:T(128)} %bitcast.core_ref, bf16[1024,128]{1,0:T(8,128)(2,1)S(1)} %shard_map.97.mine_ref, bf16[1024,128]{1,0:T(8,128)(2,1)S(1)} %collective-permute-done.6.got_ref, bf16[2,3,256,128]{3,2,1,0:T(8,128)(2,1)S(1)} %bitcast.13, ...), custom_call_target="tpu_custom_call" | custom-call | flops 6000000000 | bytes 3000000 | tf_op jit(solution)/shard_map/pallas_call | solution.py:236
  122.5 0.2 collective-permute-start.7
  122.7 0.1 broadcast_in_dim.3
  122.8 0.0 copy-start.7
  122.8 1.3 %collective-permute-done.7 = bf16[1024,128]{1,0:T(8,128)(2,1)S(1)} collective-permute-done((bf16[1024,128]{1,0:T(8,128)(2,1)S(1)}, bf16[1024,128]{1,0:T(8,128)(2,1)S(1)}, u32[]{:S(2)}, u32[]{:S(2)}) %collective-permute-start.7) | collective-permute-done | bytes 262176 | tf_op jit(solution)/shard_map/ppermute | solution.py:22
  124.1 0.0 copy-done.7
  124.1 0.7 constant_dynamic-update-slice_fusion
  (1 shorter events, 0.0 us)
Async XLA Ops:
  7.1 46.8 %copy-start.1 = (bf16[2,256,512]{2,1,0:T(8,128)(2,1)S(1)}, bf16[2,256,512]{2,1,0:T(8,128)(2,1)}, u32[]{:S(2)}) copy-start(bf16[2,256,512]{2,1,0:T(8,128)(2,1)} %up_a.1) | copy-start | bytes 1572868
  7.1 49.4 %copy-start.2 = (bf16[2,512,256]{2,1,0:T(8,128)(2,1)S(1)}, bf16[2,512,256]{2,1,0:T(8,128)(2,1)}, u32[]{:S(2)}) copy-start(bf16[2,512,256]{2,1,0:T(8,128)(2,1)} %down_a.1) | copy-start | bytes 1572868
  7.1 50.2 %copy-start.3 = (bf16[2,256,3,128]{3,1,2,0:T(8,128)(2,1)S(1)}, bf16[2,256,3,128]{3,1,2,0:T(8,128)(2,1)}, u32[]{:S(2)}) copy-start(bf16[2,256,3,128]{3,1,2,0:T(8,128)(2,1)} %param.12) | copy-start | bytes 1179652
  53.8 7.4 %collective-permute-start.3 = (bf16[2,256,512]{2,1,0:T(8,128)(2,1)S(1)}, bf16[2,256,512]{2,1,0:T(8,128)(2,1)S(1)}, u32[]{:S(2)}, u32[]{:S(2)}) collective-permute-start(bf16[2,256,512]{2,1,0:T(8,128)(2,1)S(1)} %copy-done.1), channel_id=1, source_target_pairs={{0,1},{1,0},{2,3},{3,2},{4,5},{5,4},{6,7},{7,6},{8,9},{9,8},{10,11... | collective-permute-start | bytes 1572872 | tf_op jit(solution)/shard_map/ppermute | solution.py:22
  56.5 4.8 %collective-permute-start.4 = (bf16[2,512,256]{2,1,0:T(8,128)(2,1)S(1)}, bf16[2,512,256]{2,1,0:T(8,128)(2,1)S(1)}, u32[]{:S(2)}, u32[]{:S(2)}) collective-permute-start(bf16[2,512,256]{2,1,0:T(8,128)(2,1)S(1)} %copy-done.2), channel_id=1, source_target_pairs={{0,1},{1,0},{2,3},{3,2},{4,5},{5,4},{6,7},{7,6},{8,9},{9,8},{10,11... | collective-permute-start | bytes 1572872 | tf_op jit(solution)/shard_map/ppermute | solution.py:22
  57.3 3.9 %collective-permute-start.1 = (bf16[2,3,256,128]{3,2,1,0:T(8,128)(2,1)S(1)}, bf16[2,3,256,128]{3,2,1,0:T(8,128)(2,1)S(1)}, u32[]{:S(2)}, u32[]{:S(2)}) collective-permute-start(bf16[2,3,256,128]{3,2,1,0:T(8,128)(2,1)S(1)} %bitcast.11), channel_id=1, source_target_pairs={{0,1},{1,0},{2,3},{3,2},{4,5},{5,4},{6,7},{7,6},{8,9},{9,8},{10,11... | collective-permute-start | bytes 1179656 | tf_op jit(solution)/shard_map/ppermute | solution.py:22
  57.8 1.6 %copy-start.4 = (bf16[2,128,256]{2,1,0:T(8,128)(2,1)S(1)}, bf16[2,128,256]{2,1,0:T(8,128)(2,1)}, u32[]{:S(2)}) copy-start(bf16[2,128,256]{2,1,0:T(8,128)(2,1)} %out_a.1) | copy-start | bytes 393220
  59.2 2.1 %copy-start.5 = (f32[2,256]{1,0:T(2,128)S(1)}, f32[2,256]{1,0:T(2,128)}, u32[]{:S(2)}) copy-start(f32[2,256]{1,0:T(2,128)} %gain_a.3) | copy-start | bytes 6148
  59.2 2.1 %copy-start.6 = (f32[2,256]{1,0:T(2,128)S(1)}, f32[2,256]{1,0:T(2,128)}, u32[]{:S(2)}) copy-start(f32[2,256]{1,0:T(2,128)} %gain_m.3) | copy-start | bytes 6148
  59.2 2.0 %collective-permute-start = (bf16[1024,128]{1,0:T(8,128)(2,1)S(1)}, bf16[1024,128]{1,0:T(8,128)(2,1)S(1)}, u32[]{:S(2)}, u32[]{:S(2)}) collective-permute-start(bf16[1024,128]{1,0:T(8,128)(2,1)S(1)} %shard_map.93), channel_id=1, source_target_pairs={{0,1},{1,0},{2,3},{3,2},{4,5},{5,4},{6,7},{7,6},{8,9},{9,8},{10,11... | collective-permute-start | bytes 786440 | tf_op jit(solution)/shard_map/ppermute | solution.py:22
  59.4 1.8 %collective-permute-start.2 = (bf16[2,128,256]{2,1,0:T(8,128)(2,1)S(1)}, bf16[2,128,256]{2,1,0:T(8,128)(2,1)S(1)}, u32[]{:S(2)}, u32[]{:S(2)}) collective-permute-start(bf16[2,128,256]{2,1,0:T(8,128)(2,1)S(1)} %copy-done.4), channel_id=1, source_target_pairs={{0,1},{1,0},{2,3},{3,2},{4,5},{5,4},{6,7},{7,6},{8,9},{9,8},{10,11... | collective-permute-start | bytes 393224 | tf_op jit(solution)/shard_map/ppermute | solution.py:22
  61.2 8.8 %copy-start = (s32[2,1,1,4096]{3,2,1,0:T(1,128)S(1)}, s32[2,1,1,4096]{3,2,1,0:T(1,128)}, u32[]{:S(2)}) copy-start(s32[2,1,1,4096]{3,2,1,0:T(1,128)} %reshape.28.index_ref) | copy-start | bytes 98308
  69.5 1.8 %collective-permute-start.5 = (bf16[1024,128]{1,0:T(8,128)(2,1)S(1)}, bf16[1024,128]{1,0:T(8,128)(2,1)S(1)}, u32[]{:S(2)}, u32[]{:S(2)}) collective-permute-start(bf16[1024,128]{1,0:T(8,128)(2,1)S(1)} %get-tuple-element.19), channel_id=1, source_target_pairs={{0,1},{1,0},{2,3},{3,2},{4,5},{5,4},{6,7},{7,6},{8,9},{9,8},{10,11... | collective-permute-start | bytes 786440 | tf_op jit(solution)/shard_map/ppermute | solution.py:22
  111.1 3.1 %collective-permute-start.6 = (bf16[1024,128]{1,0:T(8,128)(2,1)S(1)}, bf16[1024,128]{1,0:T(8,128)(2,1)S(1)}, u32[]{:S(2)}, u32[]{:S(2)}) collective-permute-start(bf16[1024,128]{1,0:T(8,128)(2,1)S(1)} %shard_map.98), channel_id=1, source_target_pairs={{0,1},{1,0},{2,3},{3,2},{4,5},{5,4},{6,7},{7,6},{8,9},{9,8},{10,11... | collective-permute-start | bytes 786440 | tf_op jit(solution)/shard_map/ppermute | solution.py:22
  122.5 1.6 %collective-permute-start.7 = (bf16[1024,128]{1,0:T(8,128)(2,1)S(1)}, bf16[1024,128]{1,0:T(8,128)(2,1)S(1)}, u32[]{:S(2)}, u32[]{:S(2)}) collective-permute-start(bf16[1024,128]{1,0:T(8,128)(2,1)S(1)} %get-tuple-element.22), channel_id=1, source_target_pairs={{0,1},{1,0},{2,3},{3,2},{4,5},{5,4},{6,7},{7,6},{8,9},{9,8},{10,11... | collective-permute-start | bytes 786440 | tf_op jit(solution)/shard_map/ppermute | solution.py:22
  122.8 1.3 %copy-start.7 = (bf16[2048,128]{1,0:T(8,128)(2,1)}, bf16[2048,128]{1,0:T(8,128)(2,1)S(1)}, u32[]{:S(2)}) copy-start(bf16[2048,128]{1,0:T(8,128)(2,1)S(1)} %constant_dynamic-update-slice_fusion.1) | copy-start | bytes 1572868
